TPU v7x, 128 devices: a whole 4x4x4 slice. The times are simulated.
128 devices in a mesh: row: 8 (over y, z_hi), col: 16 (over x, z_lo, core).
Axes of the slice: x: 4, y: 4, z: 4 (z_hi: 2, z_lo: 2; z = z_hi * 2 + z_lo), core: 2. Of those that a mesh axis runs over, the one named last changes fastest.
Arguments:
- front_matrix: float32 [16384, 16384], P('row', 'col'), may hold values from -6 to 206
- updates: float32 [16384, 16384], P('row', 'col'), may hold values from -6 to 6
- child_map: int32 [4, 64], replicated, may hold values from 0 to 127, as said below
Outputs:
- factored: float32 [16384, 16384], P('row', 'col')
Inputs may be any that keep to these rules, and one draw needn't show every extreme that they name: `child_map`: entries of each row are distinct. For every child and every g below 8, the entries g * 8 to (g+1) * 8 - 1 are increasing, leave the remainder g modulo 8, and their quotients by 16 are distinct. Counting the blocks of one device's share of updates by the device that owns their parent block in the contiguous 8 x 16 layout of the front, no device sends more than 2 blocks to one device, and some device sends exactly 2 in every draw.
All inputs are finite; a program needn't handle non-finite values.
Results may differ from a plain program's by a relative error of at most 0.00005.
Values sent between devices are 32-bit elements; how exact they have to be, the bound alone decides.
No kernel may reach another device: no remote copies, remote signals or barrier semaphores. Data moves between devices by JAX's collectives and lax.ppermute only.
A program may use at most 192 MiB of HBM per device.

v0:
```python
import jax
import jax.numpy as jnp
from jax import lax
from jax.sharding import PartitionSpec as P

BS = 128
CAP = 2


def broadcast(block, axis, owner):
    block = jnp.where(lax.axis_index(axis) == owner, block, jnp.zeros_like(block))
    return lax.psum(block, axis)


def body(front_matrix, updates, child_map):
    rows_dev, cols_dev = front_matrix.shape
    row_blocks = rows_dev // BS
    col_blocks = cols_dev // BS
    block_count = row_blocks * col_blocks
    grid_rows = lax.axis_size("row")
    grid_cols = lax.axis_size("col")
    row_index = lax.axis_index("row")
    col_index = lax.axis_index("col")
    child_id = row_index // (grid_rows // 2) + 2 * (col_index // (grid_cols // 2))
    sub_row = row_index % (grid_rows // 2)
    sub_col = col_index % (grid_cols // 2)
    child_entries = lax.dynamic_index_in_dim(child_map, child_id, 0, keepdims=False)
    row_map = lax.dynamic_slice_in_dim(child_entries, sub_row * row_blocks, row_blocks)
    col_map = lax.dynamic_slice_in_dim(child_entries, sub_col * col_blocks, col_blocks)
    target = (
        (row_map // row_blocks)[:, None] * grid_cols + (col_map // col_blocks)[None, :]
    ).reshape(-1)
    local_slot = (
        (row_map % row_blocks)[:, None] * col_blocks + (col_map % col_blocks)[None, :]
    ).reshape(-1)
    blocks = (
        updates.reshape(row_blocks, BS, col_blocks, BS)
        .transpose(0, 2, 1, 3)
        .reshape(block_count, BS, BS)
    )
    positions = jnp.arange(block_count)
    before = (target[:, None] == target[None, :]) & (positions[None, :] < positions[:, None])
    block_rank = jnp.sum(before, axis=1, dtype=jnp.int32)
    send_spot = target * CAP + block_rank
    slot_count = grid_rows * grid_cols * CAP
    outgoing = jnp.zeros((slot_count, BS, BS), jnp.float32).at[send_spot].set(blocks)
    labels = jnp.full((slot_count,), block_count, jnp.int32).at[send_spot].set(local_slot)
    incoming, slot_marks = (
        lax.all_to_all(outgoing, ("row", "col"), split_axis=0, concat_axis=0, tiled=True),
        lax.all_to_all(labels, ("row", "col"), split_axis=0, concat_axis=0, tiled=True),
    )
    summed = jnp.zeros((block_count + 1, BS, BS), jnp.float32).at[slot_marks].add(incoming)
    extended = front_matrix + summed[:block_count].reshape(
        row_blocks, col_blocks, BS, BS
    ).transpose(0, 2, 1, 3).reshape(rows_dev, cols_dev)
    raw_panel = broadcast(extended[:, :BS], "col", 0)
    diag_top = broadcast(raw_panel[:BS], "row", 0)
    factor_head = jnp.linalg.cholesky(diag_top)
    panel_slab = lax.linalg.triangular_solve(
        factor_head, raw_panel, left_side=False, lower=True, transpose_a=True
    )
    first_row = row_index == 0
    panel_slab = panel_slab.at[:BS].set(jnp.where(first_row, factor_head, panel_slab[:BS]))
    whole_panel = lax.all_gather(panel_slab, "row", axis=0, tiled=True)
    column_panel = lax.dynamic_slice_in_dim(whole_panel, col_index * cols_dev, cols_dev, 0)
    correction = jnp.dot(
        panel_slab,
        column_panel.T,
        precision=lax.Precision.HIGHEST,
        preferred_element_type=jnp.float32,
    )
    global_rows = row_index * rows_dev + jnp.arange(rows_dev)
    global_cols = col_index * cols_dev + jnp.arange(cols_dev)
    trailing = (global_rows >= BS)[:, None] & (global_cols >= BS)[None, :]
    result = jnp.where(trailing, extended - correction, extended)
    first_cols = jnp.where(col_index == 0, panel_slab, result[:, :BS])
    return result.at[:, :BS].set(first_cols)


def solution(mesh):
    return jax.shard_map(
        body,
        mesh=mesh,
        in_specs=(P("row", "col"), P("row", "col"), P()),
        out_specs=P("row", "col"),
        check_vma=False,
    )
```

profile of v0, /device:TPU:1, one launch (start us, length us, event | category | flops | bytes accessed | tf_op | source)
XLA Modules:
  0.0 763.6 jit_solution(5692032000672147956)
XLA Ops:
  10.2 1.0 scatter_custom_fusion
  11.9 11.5 %all-to-all-start = ((s32[128,2,1]{1,2,0:T(1,128)}), s32[128,2,1]{1,2,0:T(1,128)S(1)}, u32[]{:S(2)}, u32[]{:S(2)}) async-start(s32[128,2,1]{1,2,0:T(1,128)} %bitcast.5), calls=%async_computation | async-start | bytes 131072 | tf_op jit(solution)/shard_map/all_to_all | solution.py:50
  23.4 5.5 copy.18
  29.7 4.9 copy.15
  34.6 7.8 %broadcast_in_dim.13 = f32[256,128,128]{2,1,0:T(8,128)} broadcast(f32[]{:T(128)} %constant.223.clone.1), dimensions={} | broadcast | bytes 16777220 | tf_op jit(solution)/shard_map/broadcast_in_dim | solution.py:46
  42.4 23.5 %scatter_fusion = f32[256,128,128]{2,1,0:T(8,128)} fusion(f32[256,128,128]{2,1,0:T(8,128)} %broadcast_in_dim.13, s32[128]{0:T(128)S(1)} %fusion.10, f32[128,128,128]{2,1,0:T(8,128)} %bitcast.54), kind=kCustom, calls=%fused_computation.1 | custom fusion | bytes 25166336 | tf_op jit(solution)/shard_map/scatter | solution.py:46
  65.9 10.1 %all-to-all-start.1 = ((f32[256,128,128]{2,1,0:T(8,128)}), f32[256,128,128]{2,1,0:T(8,128)}, u32[]{:S(2)}, u32[]{:S(2)}) async-start(f32[256,128,128]{2,1,0:T(8,128)} %scatter_fusion), calls=%async_computation.1 | async-start | bytes 33554432 | tf_op jit(solution)/shard_map/all_to_all | solution.py:49
  77.5 227.9 %all-to-all-done.1 = f32[256,128,128]{2,1,0:T(8,128)} async-done(((f32[256,128,128]{2,1,0:T(8,128)}), f32[256,128,128]{2,1,0:T(8,128)}, u32[]{:S(2)}, u32[]{:S(2)}) %all-to-all-start.1) | async-done | bytes 16777248 | tf_op jit(solution)/shard_map/all_to_all | solution.py:49
  305.5 4.3 broadcast_in_dim.11
  309.8 51.9 %scatter_fusion.1 = f32[129,128,128]{2,1,0:T(8,128)} fusion(f32[129,128,128]{2,1,0:T(8,128)} %broadcast_in_dim.11, s32[256]{0:T(256)S(1)} %bitcast.58, f32[256,128,128]{2,1,0:T(8,128)} %all-to-all-done.1), kind=kCustom, calls=%fused_computation.2 | custom fusion | flops 4194304 | bytes 50332672 | tf_op jit(solution)/shard_map/scatter-add | solution.py:52
  361.7 4.0 slice.64
  365.7 9.9 %copy.16 = f32[16,128,8,128]{3,2,1,0:T(8,128)} copy(f32[16,128,8,128]{3,1,2,0:T(8,128)S(1)} %bitcast.55) | data formatting | bytes 16777216 | tf_op jit(solution)/shard_map/transpose | solution.py:55
  375.6 12.1 %bitcast_add_fusion = f32[2048,1024]{1,0:T(8,128)} fusion(f32[2048,1024]{1,0:T(8,128)} %param.7, f32[256,8,8,128]{3,2,1,0:T(8,128)} %bitcast.53), kind=kLoop, calls=%fused_computation.4 | loop fusion | flops 2097152 | bytes 25165824 | tf_op jit(solution)/shard_map/add | solution.py:53
  387.7 2.3 slice_select_fusion
  390.1 130.8 %all-reduce.3.cloned.1.call-done = f32[2048,128]{1,0:T(8,128)} async-done(((f32[2048,128]{1,0:T(8,128)}), f32[2048,128]{1,0:T(8,128)}) %all-reduce.3.cloned.1.call-update) | async-done | bytes 1048592 | tf_op jit(solution)/shard_map/psum | solution.py:12
  520.8 1.5 slice_select_fusion.2
  522.6 79.5 %all-reduce.5.cloned.1.call-done = f32[128,128]{1,0:T(8,128)} async-done(((f32[128,128]{1,0:T(8,128)}), f32[128,128]{1,0:T(8,128)}) %all-reduce.5.cloned.1.call-update) | async-done | bytes 65552 | tf_op jit(solution)/shard_map/psum | solution.py:12
  603.9 11.7 %cholesky.15 = f32[128,128]{1,0:T(8,128)S(1)} custom-call(f32[128,128]{1,0:T(8,128)S(1)} %fusion.5), custom_call_target="Cholesky" | custom-call | tf_op jit(solution)/shard_map/jit(cholesky)/cholesky | solution.py:58
  616.9 9.8 %custom-call.6 = f32[1,128,128]{1,2,0:T(8,128)S(1)} custom-call(f32[1,128,128]{2,1,0:T(8,128)S(1)} %select_bitcast_fusion), custom_call_target="InvertDiagBlocksLowerTriangular" | custom-call | tf_op jit(solution)/shard_map/triangular_solve | solution.py:59
  626.8 2.2 fusion.3
  629.6 1.0 copy-done
  631.3 110.9 %all-gather.2.cloned.1.call-done = f32[16384,128]{1,0:T(8,128)} async-done(((f32[2048,128]{1,0:T(8,128)}), f32[16384,128]{1,0:T(8,128)}) %all-gather.2.cloned.1.call-update) | async-done | bytes 8388624 | tf_op jit(solution)/shard_map/all_gather | solution.py:64
  742.2 12.0 %subtract_select_fusion = f32[2048,1024]{1,0:T(8,128)} fusion(f32[2048,1024]{1,0:T(8,128)} %bitcast_add_fusion, f32[2048,128]{1,0:T(8,128)} %copy-done, pred[1024]{0:T(1024)(128)(4,1)S(1)} %add_compare_fusion.1, pred[2048]{0:T(1024)(128)(4,1)S(1)} %add_compare_fusion, f32[16384,128]{1,0:T(8,128)} %all-gather.2.cloned.1.call-done, s32[]{:T(128)S(6)} %select_n.144), kind=kOutput, calls=%fused_computation.3 | convolution fusion | flops 3227516928 | bytes 18353156 | tf_op jit(solution)/shard_map/dot_general | solution.py:66
  754.3 2.9 fusion
  (36 shorter events, 11.5 us)
Async XLA Ops:
  11.9 54.0 %all-to-all-start = ((s32[128,2,1]{1,2,0:T(1,128)}), s32[128,2,1]{1,2,0:T(1,128)S(1)}, u32[]{:S(2)}, u32[]{:S(2)}) async-start(s32[128,2,1]{1,2,0:T(1,128)} %bitcast.5), calls=%async_computation | async-start | bytes 131072 | tf_op jit(solution)/shard_map/all_to_all | solution.py:50
  65.9 239.6 %all-to-all-start.1 = ((f32[256,128,128]{2,1,0:T(8,128)}), f32[256,128,128]{2,1,0:T(8,128)}, u32[]{:S(2)}, u32[]{:S(2)}) async-start(f32[256,128,128]{2,1,0:T(8,128)} %scatter_fusion), calls=%async_computation.1 | async-start | bytes 33554432 | tf_op jit(solution)/shard_map/all_to_all | solution.py:49
  76.0 444.8 %all-reduce.3.cloned.1.call-start = ((), (), s32[]{:S(2)}) async-start(), calls=%async_computation.2 | async-start | bytes 2097152 | tf_op jit(solution)/shard_map/psum | solution.py:12
  390.0 212.1 %all-reduce.5.cloned.1.call-start = ((), (), s32[]{:S(2)}) async-start(), calls=%async_computation.3 | async-start | bytes 131072 | tf_op jit(solution)/shard_map/psum | solution.py:12
  522.3 219.9 %all-gather.2.cloned.1.call-start = ((), (), s32[]{:S(2)}) async-start(), calls=%async_computation.4 | async-start | bytes 9437184 | tf_op jit(solution)/shard_map/all_gather | solution.py:64
  629.6 1.0 copy-start
  631.3 123.0 %copy-start.1 = (f32[2048,128]{1,0:T(8,128)S(1)}, f32[2048,128]{1,0:T(8,128)}, u32[]{:S(2)}) copy-start(f32[2048,128]{1,0:T(8,128)} %copy-done) | copy-start | bytes 3145732
Sparse Core Ops, SparseCore 0:
  390.1 130.6 all-reduce.2
  523.4 78.6 all-reduce.4
  630.8 111.4 all-gather.1
where the time goes:
time: 765 us; the launch traced here: 764 us
  waiting for transfers between devices  549 us (72%)
  other arithmetic  99.9 us (13%)
  local copies, waits for them, and re-layouts  65.2 us (9%)
  starting transfers between devices  21.9 us (3%)
  matrix products  14.2 us (2%)
  between operations  13.3 us (2%)
    all_to_all x1, waiting for transfers between devices, body(): lax.all_to_all(outgoing, ('row', 'col'), split_axis=0, concat_axis=0, til...  228 us
    psum x2, waiting for transfers between devices, broadcast(): return lax.psum(block, axis)  210 us
    all_gather x1, waiting for transfers between devices, body(): whole_panel = lax.all_gather(panel_slab, 'row', axis=0, tiled=True)  111 us
    scatter-add x1, other arithmetic, body(): jnp.zeros((block_count + 1, BS, BS), jnp.float32).at[slot_marks]  51.9 us
    scatter x1, local copies, waits for them, and re-layouts, body(): jnp.zeros((slot_count, BS, BS), jnp.float32).at[send_spot].set(blocks)  23.5 us
  transfers between devices with their start and end apart: 5, of which 4 were waited for; matrix products, arithmetic and copies ran while one was open for 6% of the time, Pallas kernels for 0%

commit v1 on v0

v1 whole, which is shorter than its diff:
```python
import functools

import jax
import jax.numpy as jnp
from jax import lax
from jax.experimental import pallas as pl
from jax.experimental.pallas import tpu as pltpu
from jax.sharding import Mesh
from jax.sharding import PartitionSpec as P

CHIP = ("y", "zh", "x", "zl")
ALL = CHIP + ("core",)
CHUNKS = 2


def dev(row, col, core):
    return (row * 8 + col) * 2 + core


def child_sums(flags, blocks, own_out, sib_out):
    sr, g = pl.program_id(0), pl.program_id(1)
    groups = pl.num_programs(1)
    for scp in range(4):
        for half in range(2):
            own = jnp.zeros(own_out.shape[-2:], jnp.float32)
            sib = jnp.zeros(own_out.shape[-2:], jnp.float32)
            for h in range(2):
                for v in range(2):
                    child = h + 2 * v
                    at = ((((child * 4 + sr) * groups + g) * 4 + scp) * 2 + half) * 2
                    block = blocks[h, 0, v, scp, 0]
                    own += flags[at] * block
                    sib += flags[at + 1] * block
            own_out[half, 0, 0, scp] = own
            sib_out[half, 0, 0, scp] = sib


def add_sums(core, base, own, sib, out):
    bs = own.shape[-1]
    first = core[0] == 0
    for scp in range(4):
        mine, other = own[0, 0, 0, scp], sib[0, 0, 0, scp]
        left, right = pl.ds(2 * scp * bs, bs), pl.ds((2 * scp + 1) * bs, bs)
        out[0, :, left] = base[0, :, left] + jnp.where(first, mine, other)
        out[0, :, right] = base[0, :, right] + jnp.where(first, other, mine)


def run_child_sums(flags, recv, groups, rows, bs):
    recv = recv.reshape(2, 4, 2, 4, groups, rows, bs)
    part = jax.ShapeDtypeStruct((2, 4, groups, 4, rows, bs), jnp.float32)
    spec = pl.BlockSpec((2, 1, 1, 4, rows, bs), lambda sr, g, *_: (0, sr, g, 0, 0, 0))
    return pl.pallas_call(
        child_sums,
        out_shape=(part, part),
        grid_spec=pltpu.PrefetchScalarGridSpec(
            num_scalar_prefetch=1,
            grid=(4, groups),
            in_specs=[pl.BlockSpec((2, 1, 2, 4, 1, rows, bs), lambda sr, g, *_: (0, sr, 0, 0, g, 0, 0))],
            out_specs=(spec, spec),
        ),
        compiler_params=pltpu.CompilerParams(vmem_limit_bytes=32 << 20),
        cost_estimate=pl.CostEstimate(flops=8 * recv.size, bytes_accessed=8 * recv.size, transcendentals=0),
        name="child_sums",
    )(flags, recv)


def run_add_sums(core, base, own, sib, first_group, groups, row_at, rows, bs):
    cols = base.shape[-1]
    place = pl.BlockSpec((1, rows, cols), lambda half, sr, g, *_: (8 * half + 2 * sr + first_group + g, row_at, 0))
    part = pl.BlockSpec((1, 1, 1, 4, rows, bs), lambda half, sr, g, *_: (half, sr, g, 0, 0, 0))
    return pl.pallas_call(
        add_sums,
        out_shape=jax.ShapeDtypeStruct(base.shape, jnp.float32),
        grid_spec=pltpu.PrefetchScalarGridSpec(
            num_scalar_prefetch=1,
            grid=(2, 4, groups),
            in_specs=[place, part, part],
            out_specs=place,
        ),
        input_output_aliases={1: 0},
        compiler_params=pltpu.CompilerParams(vmem_limit_bytes=32 << 20),
        cost_estimate=pl.CostEstimate(flops=2 * own.size, bytes_accessed=24 * own.size, transcendentals=0),
        name="add_sums",
    )(core, base, own, sib)


def body(front, updates, child_map):
    rows_dev, cols_dev = front.shape
    bs = rows_dev // 16
    y, zh, x, zl, t = (lax.axis_index(a) for a in ALL)
    ji, jc = 2 * y + zh, 2 * x + zl
    col = 2 * jc + t
    bits = (child_map.reshape(4, 8, 8) // 8) % 2
    take = functools.partial(lax.dynamic_index_in_dim, keepdims=False)

    child = y // 2 + 2 * (x // 2)
    sr_me = 2 * (y % 2) + zh
    is_corner = (ji == 0) & (col == 0)
    head_bit = take(bits[:, 0, 0], child, 0)
    live = (head_bit == 0).astype(jnp.float32)
    ucol = updates[:, :bs].reshape(2, 8, bs, bs) * live
    fcol = front[:, :bs]
    corner = ucol[0, 0] + jnp.where(is_corner, fcol[:bs], 0.0)
    sources = [(r, v) for r in range(8) for v in range(2)]
    landed = []
    for k in range(8):
        to = (k + 2 * child) % 8
        load = jnp.concatenate([take(ucol, to, 1), corner[None]])
        pairs = []
        for r, v in sources:
            c = r // 4 + 2 * v
            pairs.append((dev(r, 4 * v, 0), dev((k + 2 * c) % 8, 2 * (r % 4), 0)))
        landed.append(lax.ppermute(load, ALL, pairs))
    fq = fcol.reshape(2, 4, 2, bs, bs)
    front_part = jnp.where(x == 0, fq[:, 0], 0.0)
    for q in range(1, 4):
        pairs = [(dev(r, 0, 0), dev(r, 2 * q, 0)) for r in range(8)]
        front_part = front_part + lax.ppermute(fq[:, q], ALL, pairs)
    landed = jnp.stack(landed)
    e00 = jnp.zeros((bs, bs), jnp.float32)
    owned = front_part
    row_bits = lax.dynamic_slice_in_dim(take(bits, ji, 2), 2 * x, 2, 1)
    for c in range(4):
        piece = take(landed, (ji - 2 * c) % 8, 0)
        mask = (row_bits[c][None, :] == jnp.arange(2)[:, None]).astype(jnp.float32)
        owned = owned + mask[:, :, None, None] * piece[None, :2]
        e00 = e00 + piece[2]
    load = jnp.concatenate([owned.reshape(4, bs, bs), e00[None]])
    got = lax.ppermute(load, ALL, [(dev(r, 2 * q, 0), dev(r, 2 * q, 1)) for r in range(8) for q in range(4)])
    load = jnp.where(t == 0, load, got)
    mine = jnp.where(t == 0, load[0:2], load[2:4])
    load = jnp.concatenate([mine, load[4:]])
    along = []
    for dx in range(4):
        total = jnp.where(zl == 0, load, 0.0) if dx == 0 else None
        for dz in range(2):
            if dx == 0 and dz == 0:
                continue
            pairs = [
                (dev(r, 2 * q, core), dev(r, 2 * ((q + dx) % 4) + dz, core))
                for r in range(8) for q in range(4) for core in range(2)
            ]
            got = lax.ppermute(load, ALL, pairs)
            total = got if total is None else total + got
        along.append(total)
    along = jnp.stack(along)
    pieces = [take(along, (x - q) % 4, 0) for q in range(4)]
    head_raw = pieces[0][2]
    half_slab = jnp.concatenate([p[:2] for p in pieces])
    other_half = lax.ppermute(half_slab, "core", [(0, 1), (1, 0)])
    slab = jnp.where(t == 0, jnp.stack([half_slab, other_half]), jnp.stack([other_half, half_slab]))
    slab = slab.reshape(rows_dev, bs)
    down = []
    for k in range(8):
        pairs = [
            (dev(r, 2 * q, core), dev((k + 2 * q) % 8, r, core))
            for r in range(8) for q in range(4) for core in range(2)
        ]
        down.append(lax.ppermute(mine, ALL, pairs))
    down = jnp.stack(down)
    col_slab = jnp.concatenate([take(down, (ji - 2 * q) % 8, 0) for q in range(4)]).reshape(cols_dev, bs)

    head = jnp.linalg.cholesky(head_raw)
    solved = lax.linalg.triangular_solve(
        head, jnp.concatenate([slab, col_slab]), left_side=False, lower=True, transpose_a=True
    )
    panel, col_panel = solved[:rows_dev], solved[rows_dev:]
    product = jnp.dot(panel, col_panel.T, precision=lax.Precision.HIGHEST, preferred_element_type=jnp.float32)
    in_rows = (ji * rows_dev + jnp.arange(rows_dev)) >= bs
    in_cols = (col * cols_dev + jnp.arange(cols_dev)) >= bs
    base = jnp.where(in_rows[:, None] & in_cols[None, :], front - product, front)
    panel = panel.at[:bs].set(jnp.where(ji == 0, head, panel[:bs]))
    base = base.at[:, :bs].set(jnp.where(col == 0, panel, base[:, :bs]))
    base = base.reshape(16, bs, cols_dev)

    groups = 2 if CHUNKS == 1 else 1
    parts = max(CHUNKS // 2, 1)
    rows = bs // parts
    core_id = t.reshape(1).astype(jnp.int32)
    col_bits = take(take(bits, jc, 2).reshape(4, 4, 2), t, 2)
    row_bits = take(bits, ji, 2).reshape(4, 4, 2)
    to_own = col_bits == t
    in_panel = (col == 0) & (jnp.arange(4) == 0)
    send = updates.reshape(2, 8, bs, 8, bs)
    for gi in range(0, 2, groups):
        for part in range(parts):
            block = send[gi:gi + groups, :, part * rows:(part + 1) * rows].transpose(1, 3, 0, 2, 4)
            recv = lax.all_to_all(block.reshape(64, groups * rows, bs), CHIP, 0, 0, tiled=True)
            here = (row_bits[:, :, gi:gi + groups, None, None] == jnp.arange(2))
            own = (to_own & ~in_panel)[:, None, None, :, None] & here
            sib = (~to_own)[:, None, None, :, None] & here
            flags = jnp.stack([own, sib], -1).astype(jnp.float32).reshape(-1)
            own_sum, sib_sum = run_child_sums(flags, recv, groups, rows, bs)
            sib_sum = lax.ppermute(sib_sum, "core", [(0, 1), (1, 0)])
            base = run_add_sums(core_id, base, own_sum, sib_sum, gi, groups, part, rows, bs)
    return base.reshape(rows_dev, cols_dev)


def solution(mesh):
    fine = Mesh(mesh.devices.reshape(4, 2, 4, 2, 2), ALL)
    spec = P(("y", "zh"), ("x", "zl", "core"))
    return jax.shard_map(body, mesh=fine, in_specs=(spec, spec, P()), out_specs=spec, check_vma=False)
```

time: 765 us -> 316 us (0.41)
  the two profiles are of different devices: /device:TPU:1 before, /device:TPU:121 now
where the time goes in v1:
time: 316 us; the launch traced here: 314 us
  waiting for transfers between devices  135 us (43%)
  starting transfers between devices  77.5 us (25%)
  other arithmetic  33.2 us (11%)
  local copies, waits for them, and re-layouts  29.3 us (9%)
  Pallas kernels  24.8 us (8%)
  matrix products  12.2 us (4%)
    ppermute x8, waiting for transfers between devices, body(): down.append(lax.ppermute(mine, ALL, pairs))  97.4 us
    all_to_all x2, starting transfers between devices, body(): lax.all_to_all(block.reshape(64, groups * rows, bs), CHIP, 0, 0, tiled=True)  52.8 us
    all_to_all x2, waiting for transfers between devices, body(): lax.all_to_all(block.reshape(64, groups * rows, bs), CHIP, 0, 0, tiled=True)  19.5 us
    ppermute x7, waiting for transfers between devices, body(): got = lax.ppermute(load, ALL, pairs)  18.2 us
    unnamed x38, local copies, waits for them, and re-layouts  17.8 us
    pallas_call x2, Pallas kernels, run_add_sums(): pl.pallas_call(add_sums, out_shape=jax.ShapeDtypeStruct(base.shape, jnp.f...  14.2 us
    another operation x3, other arithmetic, body(): head = jnp.linalg.cholesky(head_raw)  12.4 us
    pallas_call x2, Pallas kernels, run_child_sums(): pl.pallas_call(child_sums, out_shape=(part, part), grid_spec=pltpu.Prefet...  10.5 us
  transfers between devices with their start and end apart: 32, of which 6 were waited for; matrix products, arithmetic and copies ran while one was open for 20% of the time, Pallas kernels for 6%

profile of v1, /device:TPU:121, one launch (start us, length us, event | category | flops | bytes accessed | tf_op | source)
XLA Modules:
  0.0 314.0 jit_solution(7392055589492778244)
XLA Ops:
  10.4 6.7 %slice_bitcast_fusion = (f32[128,8,8,128]{3,1,2,0:T(8,128)S(1)}, f32[128,8,8,128]{3,1,2,0:T(8,128)}) fusion(f32[2048,1024]{1,0:T(8,128)} %param.8), kind=kLoop, calls=%fused_computation.1 | loop fusion | bytes 16777216
  18.1 2.8 copy.155
  20.9 9.7 %all-to-all-start.1 = ((f32[64,128,128]{2,1,0:T(8,128)}), f32[64,128,128]{2,1,0:T(8,128)}, u32[]{:S(2)}, u32[]{:S(2)}) async-start(f32[64,128,128]{2,1,0:T(8,128)} %bitcast.156), calls=%async_computation.1 | async-start | bytes 8388608 | tf_op jit(solution)/shard_map/all_to_all | solution.py:188
  33.1 3.2 %copy.161 = f32[128,8,8,128]{3,2,1,0:T(8,128)S(1)} copy(f32[128,8,8,128]{3,1,2,0:T(8,128)} %get-tuple-element.44) | data formatting | bytes 8388608
  36.4 2.8 copy.152
  44.8 19.5 %all-to-all-done.1 = f32[64,128,128]{2,1,0:T(8,128)} async-done(((f32[64,128,128]{2,1,0:T(8,128)}), f32[64,128,128]{2,1,0:T(8,128)}, u32[]{:S(2)}, u32[]{:S(2)}) %all-to-all-start.1) | async-done | bytes 4194336 | tf_op jit(solution)/shard_map/all_to_all | solution.py:188
  64.3 43.0 %all-to-all-start = ((f32[64,128,128]{2,1,0:T(8,128)}), f32[64,128,128]{2,1,0:T(8,128)}, u32[]{:S(2)}, u32[]{:S(2)}) async-start(f32[64,128,128]{2,1,0:T(8,128)} %bitcast.155), calls=%async_computation | async-start | bytes 8388608 | tf_op jit(solution)/shard_map/all_to_all | solution.py:188
  115.1 88.0 %collective-permute-done.21 = f32[2,128,128]{1,2,0:T(8,128)S(1)} collective-permute-done((f32[2,128,128]{1,2,0:T(8,128)S(1)}, f32[2,128,128]{1,2,0:T(8,128)S(1)}, u32[]{:S(2)}, u32[]{:S(2)}) %collective-permute-start.21) | collective-permute-done | bytes 131104 | tf_op jit(solution)/shard_map/ppermute | solution.py:159
  205.2 9.3 %collective-permute-done.23 = f32[2,128,128]{1,2,0:T(8,128)S(1)} collective-permute-done((f32[2,128,128]{1,2,0:T(8,128)S(1)}, f32[2,128,128]{1,2,0:T(8,128)S(1)}, u32[]{:S(2)}, u32[]{:S(2)}) %collective-permute-start.23) | collective-permute-done | bytes 131104 | tf_op jit(solution)/shard_map/ppermute | solution.py:159
  220.7 3.3 %collective-permute-done.16 = f32[3,128,128]{1,2,0:T(8,128)S(1)} collective-permute-done((f32[3,128,128]{1,2,0:T(8,128)S(1)}, f32[3,128,128]{1,2,0:T(8,128)S(1)}, u32[]{:S(2)}, u32[]{:S(2)}) %collective-permute-start.16) | collective-permute-done | bytes 196640 | tf_op jit(solution)/shard_map/ppermute | solution.py:143
  226.7 9.2 %collective-permute-done.14 = f32[3,128,128]{1,2,0:T(8,128)S(1)} collective-permute-done((f32[3,128,128]{1,2,0:T(8,128)S(1)}, f32[3,128,128]{1,2,0:T(8,128)S(1)}, u32[]{:S(2)}, u32[]{:S(2)}) %collective-permute-start.14) | collective-permute-done | bytes 196640 | tf_op jit(solution)/shard_map/ppermute | solution.py:143
  235.9 5.7 %collective-permute-done.12 = f32[3,128,128]{1,2,0:T(8,128)S(1)} collective-permute-done((f32[3,128,128]{1,2,0:T(8,128)S(1)}, f32[3,128,128]{1,2,0:T(8,128)S(1)}, u32[]{:S(2)}, u32[]{:S(2)}) %collective-permute-start.12) | collective-permute-done | bytes 196640 | tf_op jit(solution)/shard_map/ppermute | solution.py:143
  243.0 11.7 %cholesky.15 = f32[128,128]{1,0:T(8,128)S(1)} custom-call(f32[128,128]{1,0:T(8,128)S(1)} %fusion.16), custom_call_target="Cholesky" | custom-call | tf_op jit(solution)/shard_map/jit(cholesky)/cholesky | solution.py:163
  254.8 5.3 %child_sums.3 = (f32[2,4,1,4,128,128]{5,4,3,2,1,0:T(8,128)S(1)}, f32[2,4,1,4,128,128]{5,4,3,2,1,0:T(8,128)}) custom-call(f32[256]{0:T(256)S(1)} %reshape.386.flags, f32[2,4,2,4,1,128,128]{6,5,4,3,2,1,0:T(8,128)} %bitcast.71.blocks), custom_call_target="tpu_custom_call" | custom-call | flops 8388608 | bytes 8388608 | tf_op jit(solution)/shard_map/child_sums/pallas_call | solution.py:52
  260.1 5.3 %child_sums.2 = (f32[2,4,1,4,128,128]{5,4,3,2,1,0:T(8,128)S(1)}, f32[2,4,1,4,128,128]{5,4,3,2,1,0:T(8,128)}) custom-call(f32[256]{0:T(256)S(1)} %reshape.385.flags, f32[2,4,2,4,1,128,128]{6,5,4,3,2,1,0:T(8,128)} %bitcast.67.blocks), custom_call_target="tpu_custom_call" | custom-call | flops 8388608 | bytes 8388608 | tf_op jit(solution)/shard_map/child_sums/pallas_call | solution.py:52
  265.3 1.4 copy-done
  268.6 9.8 %custom-call.6 = f32[1,128,128]{1,2,0:T(8,128)S(1)} custom-call(f32[1,128,128]{2,1,0:T(8,128)S(1)} %select_bitcast_fusion), custom_call_target="InvertDiagBlocksLowerTriangular" | custom-call | tf_op jit(solution)/shard_map/triangular_solve | solution.py:164
  278.4 2.3 maximum_select_fusion
  280.7 1.6 copy.141
  282.2 2.4 fusion
  285.5 9.7 %subtract_select_fusion = f32[2048,1024]{1,0:T(8,128)S(1)} fusion(f32[2048,1024]{1,0:T(8,128)} %param.7, pred[1024]{0:T(1024)(128)(4,1)S(1)} %add_compare_fusion.1, pred[2048]{0:T(1024)(128)(4,1)S(1)} %add_compare_fusion, f32[3072,128]{1,0:T(8,128)S(1)} %fusion), kind=kOutput, calls=%fused_computation | convolution fusion | flops 3227516928 | bytes 18353152 | tf_op jit(solution)/shard_map/dot_general | solution.py:168
  296.4 3.4 %copy-done.2 = f32[2048,1024]{1,0:T(8,128)} copy-done((f32[2048,1024]{1,0:T(8,128)}, f32[2048,1024]{1,0:T(8,128)S(1)}, u32[]{:S(2)}) %copy-start.2) | copy-done | bytes 8388632
  299.8 7.1 %add_sums.2.base = f32[16,128,1024]{2,1,0:T(8,128)} custom-call(s32[1]{0:T(128)} %bitcast.core, f32[16,128,1024]{2,1,0:T(8,128)} %bitcast.154, f32[2,4,1,4,128,128]{5,4,3,2,1,0:T(8,128)S(1)} %copy-done.1, f32[2,4,1,4,128,128]{5,4,3,2,1,0:T(8,128)} %collective-permute-done.28.sib), custom_call_target="tpu_custom_call", output_to_operand_aliasing={{}: (1, {})} | custom-call | flops 1048576 | bytes 12582912 | tf_op jit(solution)/shard_map/add_sums/pallas_call | solution.py:71
  306.9 7.1 %add_sums.3 = f32[16,128,1024]{2,1,0:T(8,128)} custom-call(s32[1]{0:T(128)} %bitcast.core, f32[16,128,1024]{2,1,0:T(8,128)} %add_sums.2.base, f32[2,4,1,4,128,128]{5,4,3,2,1,0:T(8,128)S(1)} %get-tuple-element.35.own, f32[2,4,1,4,128,128]{5,4,3,2,1,0:T(8,128)} %collective-permute-done.29.sib), custom_call_target="tpu_custom_call", output_to_operand_aliasing={{}: (1, {})} | custom-call | flops 1048576 | bytes 12582912 | tf_op jit(solution)/shard_map/add_sums/pallas_call | solution.py:71
  (166 shorter events, 41.7 us)
Async XLA Ops:
  7.0 36.6 %collective-permute-start.10 = (f32[3,128,128]{1,2,0:T(8,128)S(1)}, f32[3,128,128]{1,2,0:T(8,128)S(1)}, u32[]{:S(2)}, u32[]{:S(2)}) collective-permute-start(f32[3,128,128]{1,2,0:T(8,128)S(1)} %get-tuple-element.71), channel_id=1, source_target_pairs={{0,112},{8,48},{16,116},{24,52},{32,120},{40,56},{48,124},{56,60},... | collective-permute-start | bytes 589832 | tf_op jit(solution)/shard_map/ppermute | solution.py:113
  7.6 32.3 %collective-permute-start.4 = (f32[3,128,128]{1,2,0:T(8,128)}, f32[3,128,128]{1,2,0:T(8,128)S(1)}, u32[]{:S(2)}, u32[]{:S(2)}) collective-permute-start(f32[3,128,128]{1,2,0:T(8,128)} %get-tuple-element.72), channel_id=1, source_target_pairs={{0,16},{8,80},{16,20},{24,84},{32,24},{40,88},{48,28},{56,92},{64,... | collective-permute-start | bytes 589832 | tf_op jit(solution)/shard_map/ppermute | solution.py:113
  8.3 32.3 %collective-permute-start.5 = (f32[3,128,128]{1,2,0:T(8,128)}, f32[3,128,128]{1,2,0:T(8,128)S(1)}, u32[]{:S(2)}, u32[]{:S(2)}) collective-permute-start(f32[3,128,128]{1,2,0:T(8,128)} %get-tuple-element.73), channel_id=1, source_target_pairs={{0,32},{8,96},{16,36},{24,100},{32,40},{40,104},{48,44},{56,108},{... | collective-permute-start | bytes 589832 | tf_op jit(solution)/shard_map/ppermute | solution.py:113
  9.0 32.4 %collective-permute-start.6 = (f32[3,128,128]{1,2,0:T(8,128)}, f32[3,128,128]{1,2,0:T(8,128)S(1)}, u32[]{:S(2)}, u32[]{:S(2)}) collective-permute-start(f32[3,128,128]{1,2,0:T(8,128)} %get-tuple-element.74), channel_id=1, source_target_pairs={{0,48},{8,112},{16,52},{24,116},{32,56},{40,120},{48,60},{56,124},... | collective-permute-start | bytes 589832 | tf_op jit(solution)/shard_map/ppermute | solution.py:113
  9.7 29.5 %collective-permute-start.3 = (f32[3,128,128]{1,2,0:T(8,128)}, f32[3,128,128]{1,2,0:T(8,128)S(1)}, u32[]{:S(2)}, u32[]{:S(2)}) collective-permute-start(f32[3,128,128]{1,2,0:T(8,128)} %get-tuple-element.78), channel_id=1, source_target_pairs={{0,0},{8,64},{16,4},{24,68},{32,8},{40,72},{48,12},{56,76},{64,32}... | collective-permute-start | bytes 589832 | tf_op jit(solution)/shard_map/ppermute | solution.py:113
  20.9 43.4 %all-to-all-start.1 = ((f32[64,128,128]{2,1,0:T(8,128)}), f32[64,128,128]{2,1,0:T(8,128)}, u32[]{:S(2)}, u32[]{:S(2)}) async-start(f32[64,128,128]{2,1,0:T(8,128)} %bitcast.156), calls=%async_computation.1 | async-start | bytes 8388608 | tf_op jit(solution)/shard_map/all_to_all | solution.py:188
  64.3 195.8 %all-to-all-start = ((f32[64,128,128]{2,1,0:T(8,128)}), f32[64,128,128]{2,1,0:T(8,128)}, u32[]{:S(2)}, u32[]{:S(2)}) async-start(f32[64,128,128]{2,1,0:T(8,128)} %bitcast.155), calls=%async_computation | async-start | bytes 8388608 | tf_op jit(solution)/shard_map/all_to_all | solution.py:188
  107.4 6.4 %collective-permute-start.20 = (f32[2,128,128]{1,2,0:T(8,128)S(1)}, f32[2,128,128]{1,2,0:T(8,128)S(1)}, u32[]{:S(2)}, u32[]{:S(2)}) collective-permute-start(f32[2,128,128]{1,2,0:T(8,128)S(1)} %slice_select_fusion), channel_id=1, source_target_pairs={{0,0},{1,1},{4,32},{5,33},{8,64},{9,65},{12,96},{13,97},{16,2},{17... | collective-permute-start | bytes 393224 | tf_op jit(solution)/shard_map/ppermute | solution.py:159
  109.8 108.7 %collective-permute-start.27 = (f32[2,128,128]{1,2,0:T(8,128)S(1)}, f32[2,128,128]{1,2,0:T(8,128)S(1)}, u32[]{:S(2)}, u32[]{:S(2)}) collective-permute-start(f32[2,128,128]{1,2,0:T(8,128)S(1)} %slice_select_fusion), channel_id=1, source_target_pairs={{0,112},{1,113},{4,16},{5,17},{8,48},{9,49},{12,80},{13,81},{16,11... | collective-permute-start | bytes 393224 | tf_op jit(solution)/shard_map/ppermute | solution.py:159
  111.1 106.1 %collective-permute-start.26 = (f32[2,128,128]{1,2,0:T(8,128)S(1)}, f32[2,128,128]{1,2,0:T(8,128)S(1)}, u32[]{:S(2)}, u32[]{:S(2)}) collective-permute-start(f32[2,128,128]{1,2,0:T(8,128)S(1)} %slice_select_fusion), channel_id=1, source_target_pairs={{0,96},{1,97},{4,0},{5,1},{8,32},{9,33},{12,64},{13,65},{16,98},{1... | collective-permute-start | bytes 393224 | tf_op jit(solution)/shard_map/ppermute | solution.py:159
  111.8 104.7 %collective-permute-start.25 = (f32[2,128,128]{1,2,0:T(8,128)S(1)}, f32[2,128,128]{1,2,0:T(8,128)S(1)}, u32[]{:S(2)}, u32[]{:S(2)}) collective-permute-start(f32[2,128,128]{1,2,0:T(8,128)S(1)} %slice_select_fusion), channel_id=1, source_target_pairs={{0,80},{1,81},{4,112},{5,113},{8,16},{9,17},{12,48},{13,49},{16,82... | collective-permute-start | bytes 393224 | tf_op jit(solution)/shard_map/ppermute | solution.py:159
  113.1 102.1 %collective-permute-start.24 = (f32[2,128,128]{1,2,0:T(8,128)S(1)}, f32[2,128,128]{1,2,0:T(8,128)S(1)}, u32[]{:S(2)}, u32[]{:S(2)}) collective-permute-start(f32[2,128,128]{1,2,0:T(8,128)S(1)} %slice_select_fusion), channel_id=1, source_target_pairs={{0,64},{1,65},{4,96},{5,97},{8,0},{9,1},{12,32},{13,33},{16,66},{1... | collective-permute-start | bytes 393224 | tf_op jit(solution)/shard_map/ppermute | solution.py:159
  113.8 89.3 %collective-permute-start.21 = (f32[2,128,128]{1,2,0:T(8,128)S(1)}, f32[2,128,128]{1,2,0:T(8,128)S(1)}, u32[]{:S(2)}, u32[]{:S(2)}) collective-permute-start(f32[2,128,128]{1,2,0:T(8,128)S(1)} %slice_select_fusion), channel_id=1, source_target_pairs={{0,16},{1,17},{4,48},{5,49},{8,80},{9,81},{12,112},{13,113},{16,18... | collective-permute-start | bytes 393224 | tf_op jit(solution)/shard_map/ppermute | solution.py:159
  203.8 10.7 %collective-permute-start.23 = (f32[2,128,128]{1,2,0:T(8,128)S(1)}, f32[2,128,128]{1,2,0:T(8,128)S(1)}, u32[]{:S(2)}, u32[]{:S(2)}) collective-permute-start(f32[2,128,128]{1,2,0:T(8,128)S(1)} %slice_select_fusion), channel_id=1, source_target_pairs={{0,48},{1,49},{4,80},{5,81},{8,112},{9,113},{12,16},{13,17},{16,50... | collective-permute-start | bytes 393224 | tf_op jit(solution)/shard_map/ppermute | solution.py:159
  214.5 27.1 %collective-permute-start.17 = (f32[3,128,128]{1,2,0:T(8,128)S(1)}, f32[3,128,128]{1,2,0:T(8,128)S(1)}, u32[]{:S(2)}, u32[]{:S(2)}) collective-permute-start(f32[3,128,128]{1,2,0:T(8,128)S(1)} %pad_maximum_fusion.12), channel_id=1, source_target_pairs={{0,12},{1,13},{4,0},{5,1},{8,4},{9,5},{12,8},{13,9},{16,28},{17,29... | collective-permute-start | bytes 589832 | tf_op jit(solution)/shard_map/ppermute | solution.py:143
  215.2 8.9 %collective-permute-start.16 = (f32[3,128,128]{1,2,0:T(8,128)S(1)}, f32[3,128,128]{1,2,0:T(8,128)S(1)}, u32[]{:S(2)}, u32[]{:S(2)}) collective-permute-start(f32[3,128,128]{1,2,0:T(8,128)S(1)} %pad_maximum_fusion.12), channel_id=1, source_target_pairs={{0,10},{1,11},{4,14},{5,15},{8,2},{9,3},{12,6},{13,7},{16,26},{17,... | collective-permute-start | bytes 589832 | tf_op jit(solution)/shard_map/ppermute | solution.py:143
  216.5 8.8 %collective-permute-start.15 = (f32[3,128,128]{1,2,0:T(8,128)S(1)}, f32[3,128,128]{1,2,0:T(8,128)S(1)}, u32[]{:S(2)}, u32[]{:S(2)}) collective-permute-start(f32[3,128,128]{1,2,0:T(8,128)S(1)} %pad_maximum_fusion.12), channel_id=1, source_target_pairs={{0,8},{1,9},{4,12},{5,13},{8,0},{9,1},{12,4},{13,5},{16,24},{17,25... | collective-permute-start | bytes 589832 | tf_op jit(solution)/shard_map/ppermute | solution.py:143
  217.2 18.6 %collective-permute-start.14 = (f32[3,128,128]{1,2,0:T(8,128)S(1)}, f32[3,128,128]{1,2,0:T(8,128)S(1)}, u32[]{:S(2)}, u32[]{:S(2)}) collective-permute-start(f32[3,128,128]{1,2,0:T(8,128)S(1)} %pad_maximum_fusion.12), channel_id=1, source_target_pairs={{0,6},{1,7},{4,10},{5,11},{8,14},{9,15},{12,2},{13,3},{16,22},{17,... | collective-permute-start | bytes 589832 | tf_op jit(solution)/shard_map/ppermute | solution.py:143
  218.6 17.3 %collective-permute-start.13 = (f32[3,128,128]{1,2,0:T(8,128)S(1)}, f32[3,128,128]{1,2,0:T(8,128)S(1)}, u32[]{:S(2)}, u32[]{:S(2)}) collective-permute-start(f32[3,128,128]{1,2,0:T(8,128)S(1)} %pad_maximum_fusion.12), channel_id=1, source_target_pairs={{0,4},{1,5},{4,8},{5,9},{8,12},{9,13},{12,0},{13,1},{16,20},{17,21... | collective-permute-start | bytes 589832 | tf_op jit(solution)/shard_map/ppermute | solution.py:143
  224.0 17.5 %collective-permute-start.12 = (f32[3,128,128]{1,2,0:T(8,128)S(1)}, f32[3,128,128]{1,2,0:T(8,128)S(1)}, u32[]{:S(2)}, u32[]{:S(2)}) collective-permute-start(f32[3,128,128]{1,2,0:T(8,128)S(1)} %pad_maximum_fusion.12), channel_id=1, source_target_pairs={{0,2},{1,3},{4,6},{5,7},{8,10},{9,11},{12,14},{13,15},{16,18},{17,... | collective-permute-start | bytes 589832 | tf_op jit(solution)/shard_map/ppermute | solution.py:143
  225.3 16.3 %collective-permute-start.18 = (f32[3,128,128]{1,2,0:T(8,128)S(1)}, f32[3,128,128]{1,2,0:T(8,128)S(1)}, u32[]{:S(2)}, u32[]{:S(2)}) collective-permute-start(f32[3,128,128]{1,2,0:T(8,128)S(1)} %pad_maximum_fusion.12), channel_id=1, source_target_pairs={{0,14},{1,15},{4,2},{5,3},{8,6},{9,7},{12,10},{13,11},{16,30},{17,... | collective-permute-start | bytes 589832 | tf_op jit(solution)/shard_map/ppermute | solution.py:143
  242.0 36.4 %collective-permute-start.19 = (f32[8,128,128]{1,2,0:T(8,128)S(1)}, f32[8,128,128]{1,2,0:T(8,128)}, u32[]{:S(2)}, u32[]{:S(2)}) collective-permute-start(f32[8,128,128]{1,2,0:T(8,128)S(1)} %get-tuple-element.70), channel_id=1, source_target_pairs={{0,1},{1,0},{2,3},{3,2},{4,5},{5,4},{6,7},{7,6},{8,9},{9,8},{10,11... | collective-permute-start | bytes 1572872 | tf_op jit(solution)/shard_map/ppermute | solution.py:150
  260.0 46.9 %collective-permute-start.29 = (f32[2,4,1,4,128,128]{5,4,3,2,1,0:T(8,128)}, f32[2,4,1,4,128,128]{5,4,3,2,1,0:T(8,128)}, u32[]{:S(2)}, u32[]{:S(2)}) collective-permute-start(f32[2,4,1,4,128,128]{5,4,3,2,1,0:T(8,128)} %get-tuple-element.36), channel_id=1, source_target_pairs={{0,1},{1,0},{2,3},{3,2},{4,5},{5,4},{6,7},{7,6},{8,9},{9,8},{10,11... | collective-permute-start | bytes 6291464 | tf_op jit(solution)/shard_map/ppermute | solution.py:194
  266.7 29.7 %collective-permute-start.28 = (f32[2,4,1,4,128,128]{5,4,3,2,1,0:T(8,128)}, f32[2,4,1,4,128,128]{5,4,3,2,1,0:T(8,128)}, u32[]{:S(2)}, u32[]{:S(2)}) collective-permute-start(f32[2,4,1,4,128,128]{5,4,3,2,1,0:T(8,128)} %get-tuple-element.34), channel_id=1, source_target_pairs={{0,1},{1,0},{2,3},{3,2},{4,5},{5,4},{6,7},{7,6},{8,9},{9,8},{10,11... | collective-permute-start | bytes 6291464 | tf_op jit(solution)/shard_map/ppermute | solution.py:194
  (17 other events, 37.5 us)

commit v2 on v0

v2 whole, which is shorter than its diff:
```python
import jax
import jax.numpy as jnp
from jax import lax
from jax.experimental import pallas as pl
from jax.experimental.pallas import tpu as pltpu
from jax.sharding import Mesh
from jax.sharding import PartitionSpec as P

CHIP = ("y", "zh", "x", "zl")
ALL = CHIP + ("core",)
CORE_SWAP = [(0, 1), (1, 0)]
VMEM = pl.BlockSpec(memory_space=pltpu.VMEM)
SMEM = pl.BlockSpec(memory_space=pltpu.SMEM)
HBM = pl.BlockSpec(memory_space=pltpu.HBM)
F32 = jnp.float32


def call(kernel, out_shape, in_specs, out_specs, name, moved, scratch=(), aliases=None, limit=16):
    many = isinstance(out_shape, tuple)
    outs = zip(out_shape, out_specs) if many else ((out_shape, out_specs),)
    outs = tuple(pltpu.HBM(array.shape, array.dtype) if spec is HBM else array for array, spec in outs)
    run = pl.pallas_call(
        kernel,
        out_shape=outs if many else outs[0],
        in_specs=in_specs,
        out_specs=out_specs,
        scratch_shapes=scratch,
        input_output_aliases=aliases or {},
        compiler_params=pltpu.CompilerParams(vmem_limit_bytes=limit << 20),
        cost_estimate=pl.CostEstimate(flops=0, bytes_accessed=moved, transcendentals=0),
        name=name,
    )

    def placed(*args):
        return run(*(
            pltpu.with_memory_space_constraint(arg, pltpu.HBM) if spec is HBM else arg
            for arg, spec in zip(args, in_specs)
        ))

    return placed


def shape(*dims):
    return jax.ShapeDtypeStruct(dims, F32)


TOKEN = shape(8, 128)


def run_lift(updates, front, bs):
    rows = updates.shape[0]
    half = bs // 2

    def lift(updates, front, low, high, token, ucol, fcol, sems):
        copies = [
            pltpu.make_async_copy(whole.at[:, pl.ds(0, bs)], part, sems.at[i])
            for i, (whole, part) in enumerate(((updates, ucol), (front, fcol)))
        ]
        for copy in copies:
            copy.start()
        token[...] = jnp.zeros_like(token)
        for at, (copy, part) in enumerate(zip(copies, (ucol, fcol))):
            copy.wait()

            def one(chip, carry):
                low[chip, 16 * at:16 * at + 16] = part[pl.ds(chip, 16, stride=bs), :]
                high[chip, 16 * at:16 * at + 16] = part[pl.ds(half + chip, 16, stride=bs), :]
                return carry

            lax.fori_loop(0, half, one, 0, unroll=4)

    share = shape(half, 32, bs)
    return call(
        lift, (share, share, TOKEN), [HBM, HBM], (VMEM,) * 3, "lift", 16 * rows * bs,
        [pltpu.VMEM((rows, bs), F32), pltpu.VMEM((rows, bs), F32), pltpu.SemaphoreType.DMA((2,))],
    )(updates, front)


def run_pack(blocks, wait, gi, at, rows, extra):
    bs = blocks.shape[1]

    def pack(blocks, wait, out, held, read_sems, write_sems):
        def read(j):
            return pltpu.make_async_copy(blocks.at[8 * gi + j, pl.ds(at, rows)], held.at[j], read_sems.at[j])

        def write(j, jc):
            lanes = pl.ds(jc * bs, bs)
            return pltpu.make_async_copy(
                held.at[j, :, lanes], out.at[8 * j + jc, pl.ds(0, rows)], write_sems.at[8 * j + jc]
            )

        for j in range(8):
            read(j).start()
        for j in range(8):
            read(j).wait()
            for jc in range(8):
                write(j, jc).start()
        for j in range(8):
            for jc in range(8):
                write(j, jc).wait()

    return call(
        pack, shape(64, rows + extra, bs), [HBM, VMEM], HBM, "pack", 512 * rows * bs,
        [pltpu.VMEM((8, rows, 8 * bs), F32), pltpu.SemaphoreType.DMA((8,)), pltpu.SemaphoreType.DMA((64,))],
    )(blocks, wait)


def run_put_rows(load, low, other, core, rows):
    def put_rows(core, load, low, other, out, token, sem):
        token[...] = jnp.zeros_like(token)
        for c, part in ((0, low), (1, other)):
            @pl.when(core[0] == c)
            def _():
                copy = pltpu.make_async_copy(part, out.at[:, pl.ds(rows, 32)], sem)
                copy.start()
                copy.wait()

    return call(
        put_rows, (shape(*load.shape), TOKEN), [SMEM, HBM, VMEM, VMEM], (HBM, VMEM), "put_rows", 8 * other.size,
        [pltpu.SemaphoreType.DMA], aliases={1: 0},
    )(core, load, low, other)


def run_sum_rows(marks, recv, load, first, last):
    bs = recv.shape[-1]

    def sum_rows(marks, recv, load, out, token, kids, total, rows, sem):
        token[...] = jnp.zeros_like(token)
        for up in range(2):
            for sr in range(4):
                acc = jnp.zeros((16, bs), F32)
                for h in range(2):
                    for v in range(2):
                        acc += marks[up, sr, 2 * v + h] * recv[(4 * h + sr) * 8 + 4 * v, first:first + 16]
                kids[pl.ds((up * 4 + sr) * 16, 16)] = acc
        for j in range(8):
            total[j] = kids[pl.ds(j, 16, stride=8), :] + recv[8 * j, first + 16:first + 32]
        corner = total[0, 0:8]
        for j in range(8):
            for jc in range(8):
                at = 8 * j + jc
                rows[at, 0:16] = total[j]
                rows[at, 16:32] = total[jc]
                rows[at, 32:40] = corner
        copy = pltpu.make_async_copy(rows, out.at[:, pl.ds(last, 40)], sem)
        copy.start()
        copy.wait()

    return call(
        sum_rows, (shape(*load.shape), TOKEN), [VMEM, VMEM, HBM], (HBM, VMEM), "sum_rows", 64 * 40 * bs * 8,
        [pltpu.VMEM((128, bs), F32), pltpu.VMEM((8, 16, bs), F32), pltpu.VMEM((64, 40, bs), F32), pltpu.SemaphoreType.DMA],
        aliases={2: 0},
    )(marks, recv, load)


def add_blocks(flags, recv, sr, scp, here, sides):
    sums = {}
    for h in range(2):
        for v in range(2):
            block = recv[(4 * h + sr) * 8 + 4 * v + scp, here]
            for up in range(2):
                for side in sides:
                    term = flags[((((h + 2 * v) * 4 + sr) * 4 + scp) * 2 + up) * 2 + side] * block
                    sums[up, side] = sums[up, side] + term if (up, side) in sums else term
    return sums


def child_sums(flags, recv, own, sib):
    rows, step = own.shape[3], 32

    def one(i, carry):
        sr, at = i // (rows // step), pl.multiple_of(i % (rows // step) * step, step)
        for scp in range(4):
            sums = add_blocks(flags, recv, sr, scp, pl.ds(at, step), (0, 1))
            for up in range(2):
                own[up, sr, scp, pl.ds(at, step)] = sums[up, 0]
                sib[up, sr, scp, pl.ds(at, step)] = sums[up, 1]
        return carry

    lax.fori_loop(0, 4 * (rows // step), one, 0)


def run_child_sums(flags, recv, wait, rows, bs):
    def kernel(flags, recv, wait, own, sib, token):
        token[...] = jnp.zeros_like(token)
        child_sums(flags, recv, own, sib)

    part = shape(2, 4, 4, rows, bs)
    return call(
        kernel, (part, part, TOKEN), [SMEM, VMEM, VMEM], (VMEM,) * 3, "child_sums", 64 * rows * bs * 8,
    )(flags, recv, wait)


def run_assemble(core, flags, mine, other, first):
    chips, width, bs = mine.shape
    half = bs // 2

    def assemble(core, flags, flat, mine, other, out, corner, own, sib):
        t = core[0]
        for who, (part, span, at) in enumerate(((flat, width, first), (other, 40, 0))):
            rows_at = pl.multiple_of(half * (t if who == 0 else 1 - t), half)
            for s in range(25):
                start = at + s if s < 16 else at + s + 8 * t if s < 24 else at + 32
                rows = part[pl.ds(start, half, stride=span), :]
                if s < 24:
                    out[s, pl.ds(rows_at, half)] = rows
                else:
                    corner[pl.ds(rows_at, half)] = rows
        child_sums(flags, mine, own, sib)

    part = shape(2, 4, 4, first, bs)
    return call(
        assemble, (shape(24, bs, bs), shape(bs, bs), part, part), [SMEM, SMEM, VMEM, VMEM, VMEM], (VMEM,) * 4, "assemble",
        200 * bs * bs,
    )(core, flags, mine.reshape(chips * width, bs), mine, other.reshape(chips * 40, bs))


def split(a):
    high = a.astype(jnp.bfloat16)
    left = a - high.astype(F32)
    mid = left.astype(jnp.bfloat16)
    return high, mid, (left - mid.astype(F32)).astype(jnp.bfloat16)


def spread(left, mine, other):
    return jnp.where(left, mine, other), jnp.where(left, other, mine)


def pair(scp, bs):
    return slice(2 * scp * bs, (2 * scp + 1) * bs), slice((2 * scp + 1) * bs, (2 * scp + 2) * bs)


def run_base(edge, front, solved, head, early, bs):
    rows, cols = front.shape
    blocks, tile, step = rows // bs, 256, 32
    cut = early[0].shape[3]

    def base(edge, front, solved, head, own0, sib0, own1, sib1, out, rest, token, held, right, sems, back):
        top, col_zero, left = edge[0] == 1, edge[1] == 1, edge[2] == 0
        token[...] = jnp.zeros_like(token)

        def room(i):
            return held.at[i // 2] if i % 2 == 0 else rest.at[i // 2]

        for i in range(blocks):
            pltpu.make_async_copy(front.at[i], room(i), sems.at[i]).start()

        for at in range(0, cols, bs):
            high, mid, low = split(solved[rows + at:rows + at + bs])
            right[at:at + bs] = jnp.concatenate([high, high, mid, high, mid, low], axis=1)

        def less(i, to, sem, n):
            pltpu.make_async_copy(front.at[i], to.at[n], sem).wait()
            own = solved[pl.ds(pl.multiple_of(i * bs, bs), bs)]
            high, mid, low = split(own)
            parts = jnp.concatenate([high, mid, high, low, mid, high], axis=1)
            keep = jnp.where(top & (i == 0), 0.0, 1.0)
            for at in range(0, cols, tile):
                lanes = slice(at, at + tile)
                product = lax.dot_general(
                    parts, right[at:at + tile], (((1,), (1,)), ((), ())), preferred_element_type=F32
                )
                to[n, :, lanes] -= keep * product

            @pl.when(col_zero)
            def _():
                to[n, :, 0:bs] = own

            @pl.when(top & col_zero & (i == 0))
            def _():
                to[n, :, 0:bs] = head[...]

        def write(n):
            return pltpu.make_async_copy(held.at[n], out.at[n, pl.ds(0, bs)], back.at[n])

        def one(n, carry):
            less(2 * n, held, sems.at[2 * n], n)
            up, sr = n // 4, n % 4
            for at in range(0, bs, step):
                here = slice(at, at + step)
                own, sib, inner = (own0, sib0, at) if at < cut else (own1, sib1, at - cut)
                for scp in range(4):
                    two = spread(left, own[up, sr, scp, inner:inner + step], sib[up, sr, scp, inner:inner + step])
                    for lanes, add in zip(pair(scp, bs), two):
                        held[n, here, lanes] += add
            write(n).start()
            less(2 * n + 1, rest, sems.at[2 * n + 1], n)
            return carry

        lax.fori_loop(0, blocks // 2, one, 0)
        lax.fori_loop(0, blocks // 2, lambda n, c: (write(n).wait(), c)[1], 0)

    return call(
        base, (shape(blocks // 2, 2 * bs, cols), shape(blocks // 2, bs, cols), TOKEN), [SMEM, HBM] + [VMEM] * 6,
        (HBM, VMEM, VMEM), "base", rows * cols * 8,
        [pltpu.VMEM((blocks // 2, bs, cols), F32), pltpu.VMEM((cols, 6 * bs), jnp.bfloat16)]
        + [pltpu.SemaphoreType.DMA((n,)) for n in (blocks, blocks // 2)],
        limit=20,
    )(edge, front.reshape(blocks, bs, cols), solved, head, *early)


def run_late_sums(flags, recv, wait):
    chips, bs, _ = recv.shape
    step = 32

    def late_sums(flags, recv, wait, sib):
        def one(i, carry):
            sr, here = i // (bs // step), pl.ds(pl.multiple_of(i % (bs // step) * step, step), step)
            for scp in range(4):
                sums = add_blocks(flags, recv, sr, scp, here, (1,))
                for up in range(2):
                    sib[up, sr, scp, here] = sums[up, 1]
            return carry

        lax.fori_loop(0, 4 * (bs // step), one, 0)

    return call(
        late_sums, shape(2, 4, 4, bs, bs), [SMEM, VMEM, VMEM], VMEM, "late_sums", 96 * bs * bs * 4,
    )(flags, recv, wait)


def run_add_own(core, flags, rest, recv):
    bs, step = recv.shape[1], 32

    def add_own(core, flags, rest, recv, out):
        def one(i, carry):
            sr, here = i // (bs // step), pl.ds(pl.multiple_of(i % (bs // step) * step, step), step)
            for scp in range(4):
                sums = add_blocks(flags, recv, sr, scp, here, (0,))
                for up in range(2):
                    n = 4 * up + sr
                    for lanes, add in zip(pair(scp, bs), spread(core[0] == 0, sums[up, 0], 0.0)):
                        out[n, here, lanes] = rest[n, here, lanes] + add
            return carry

        lax.fori_loop(0, 4 * (bs // step), one, 0)

    return call(
        add_own, shape(*rest.shape), [SMEM, SMEM, VMEM, VMEM], VMEM, "add_own", rest.size * 12, aliases={2: 0},
    )(core, flags, rest, recv)


def run_add_late(core, out, rest, sib):
    blocks, bs, cols = rest.shape
    step = 32

    def add_late(core, before, rest, sib, out, done, sems):
        def write(i):
            return pltpu.make_async_copy(done.at[i], out.at[i, pl.ds(bs, bs)], sems.at[i])

        def one(i, carry):
            up, sr = i // 4, i % 4
            for at in range(0, bs, step):
                here = slice(at, at + step)
                for scp in range(4):
                    for lanes, add in zip(pair(scp, bs), spread(core[0] == 0, 0.0, sib[up, sr, scp, here])):
                        done[i, here, lanes] = rest[i, here, lanes] + add
            write(i).start()
            return carry

        lax.fori_loop(0, blocks, one, 0)
        lax.fori_loop(0, blocks, lambda i, c: (write(i).wait(), c)[1], 0)

    return call(
        add_late, shape(*out.shape), [SMEM, HBM, VMEM, VMEM], HBM, "add_late", out.size * 6,
        [pltpu.VMEM((blocks, bs, cols), F32), pltpu.SemaphoreType.DMA((blocks,))], aliases={1: 0},
    )(core, out, rest, sib)


def body(front, updates, child_map):
    rows_dev, cols_dev = front.shape
    bs = rows_dev // 16
    half = bs // 2
    y, zh, x, zl, t = (lax.axis_index(a) for a in ALL)
    ji, jc = 2 * y + zh, 2 * x + zl
    col = 2 * jc + t
    core = t.reshape(1).astype(jnp.int32)
    blocks = updates.reshape(16, bs, cols_dev)

    def swap(a):
        return lax.ppermute(a, "core", CORE_SWAP)

    def send(load):
        return lax.all_to_all(load, CHIP, 0, 0, tiled=True)

    bits = (child_map.reshape(4, 8, 8) // 8) % 2
    col_bits = lax.dynamic_index_in_dim(bits, jc, 2, keepdims=False).reshape(4, 4, 2)
    col_bits = lax.dynamic_index_in_dim(col_bits, t, 2, keepdims=False)
    row_bits = lax.dynamic_index_in_dim(bits, ji, 2, keepdims=False).reshape(4, 4, 2)
    in_panel = (col == 0) & (jnp.arange(4) == 0)
    side = jnp.stack([(col_bits == t) & ~in_panel, col_bits != t], -1)
    up = row_bits[..., None] == jnp.arange(2)
    flags = [
        (up[:, :, gi, None, :, None] & side[:, None, :, None, :]).astype(F32).reshape(-1) for gi in range(2)
    ]
    live = bits[:, 0, 0] == 0
    marks = (bits.reshape(4, 4, 16).transpose(1, 0, 2) == jnp.arange(2)[:, None, None, None]) & live[:, None]
    marks = jnp.broadcast_to(marks.astype(F32)[..., None], (2, 4, 4, 16, bs))

    low, high, lifted = run_lift(updates, front, bs)
    other = lax.ppermute(high, ALL, [((r * 8 + q) * 2, (r * 8 + q) * 2 + 1) for r in range(8) for q in (0, 4)])
    load0, sent0 = run_put_rows(run_pack(blocks, lifted, 0, 0, half, 32), low, other, core, half)
    recv0 = send(load0)

    load1, sent1 = run_sum_rows(marks, recv0, run_pack(blocks, sent0, 0, half, half, 40), half, half)
    recv1 = send(load1)
    own0, sib0, summed0 = run_child_sums(flags[0], recv0, sent1, half, bs)
    sib0 = swap(sib0)

    recv2 = send(run_pack(blocks, summed0, 1, 0, bs, 0))
    recv2 = pltpu.with_memory_space_constraint(recv2, pltpu.VMEM)

    slabs, corner, own1, sib1 = run_assemble(core, flags[0], recv1, swap(recv1[:, half:]), half)
    sib1 = swap(sib1)
    head = jnp.linalg.cholesky(corner)
    solved = lax.linalg.triangular_solve(
        head, slabs.reshape(24 * bs, bs), left_side=False, lower=True, transpose_a=True
    )
    edge = jnp.stack([ji == 0, col == 0, t == 1]).astype(jnp.int32)
    out, rest, based = run_base(edge, front, solved, head, (own0, sib0, own1, sib1), bs)

    sib2 = swap(run_late_sums(flags[1], recv2, based))
    rest = run_add_own(core, flags[1], rest, recv2)
    return run_add_late(core, out, rest, sib2).reshape(rows_dev, cols_dev)


def solution(mesh):
    fine = Mesh(mesh.devices.reshape(4, 2, 4, 2, 2), ALL)
    spec = P(("y", "zh"), ("x", "zl", "core"))
    return jax.shard_map(body, mesh=fine, in_specs=(spec, spec, P()), out_specs=spec, check_vma=False)
```

time: 765 us -> 181 us (0.24)
  waiting for transfers between devices: 549 us -> 72.7 us
  other arithmetic: 99.9 us -> 23.5 us
  local copies, waits for them, and re-layouts: 65.2 us -> 11.3 us
  Pallas kernels: 0 us -> 41.9 us
  between operations: 13.3 us -> 0.48 us
  matrix products: 14.2 us -> 2.79 us
    psum x2 -> x0, waiting for transfers between devices: 210 us -> none  [broadcast(): return lax.psum(block, axis)]
    all_to_all x2 -> x3, waiting for transfers between devices: 228 us -> 69.3 us  [send(): return lax.all_to_all(load, CHIP, 0, 0, tiled=True)]
    all_gather x1 -> x0, waiting for transfers between devices: 111 us -> none  [body(): whole_panel = lax.all_gather(panel_slab, 'row', axis=0, tiled=True)]
    scatter-add x1 -> x0, other arithmetic: 51.9 us -> none  [body(): jnp.zeros((block_count + 1, BS, BS), jnp.float32).at[slot_marks]]
    pallas_call x0 -> x12, Pallas kernels: none -> 41.9 us  [placed(): run(*(pltpu.with_memory_space_constraint(arg, pltpu.HBM) if spec is HBM e...]
    scatter x2 -> x0, local copies, waits for them, and re-layouts: 24.5 us -> none  [the longest x1 23.5 us: body(): jnp.zeros((slot_count, BS, BS), jnp.float32).at[send_spot].set(blocks)]
    transpose x3 -> x1, local copies, waits for them, and re-layouts: 15.6 us -> 0.01 us  [body(): bits.reshape(4, 4, 16).transpose(1, 0, 2)]
    add x5 -> x0, other arithmetic: 13.8 us -> none  [the longest x1 12.1 us: body(): front_matrix + summed[:block_count].reshape(row_blocks, col_blocks, BS, B...]
  transfers between devices with their start and end apart: 5 -> 8, of which waited for: 4 -> 4; matrix products, arithmetic and copies ran while one was open for 6% -> 16% of each run, Pallas kernels for 0% -> 18%
where the time goes in v2:
time: 181 us
  waiting for transfers between devices  72.7 us (40%)
  Pallas kernels  41.9 us (23%)
  starting transfers between devices  28 us (15%)
  other arithmetic  23.5 us (13%)
  local copies, waits for them, and re-layouts  11.3 us (6%)
  matrix products  2.79 us (2%)
    all_to_all x3, waiting for transfers between devices, send(): return lax.all_to_all(load, CHIP, 0, 0, tiled=True)  69.3 us
    pallas_call x12, Pallas kernels, placed(): run(*(pltpu.with_memory_space_constraint(arg, pltpu.HBM) if spec is HBM e...  41.9 us
    all_to_all x3, starting transfers between devices, send(): return lax.all_to_all(load, CHIP, 0, 0, tiled=True)  23.5 us
    another operation x3, other arithmetic, body(): head = jnp.linalg.cholesky(corner)  12.4 us
    another operation x2, other arithmetic, body(): lax.linalg.triangular_solve(head, slabs.reshape(24 * bs, bs), left_side=F...  10.5 us
    unnamed x22, local copies, waits for them, and re-layouts  8.66 us
  transfers between devices with their start and end apart: 8, of which 4 were waited for; matrix products, arithmetic and copies ran while one was open for 16% of the time, Pallas kernels for 18%

profile of v2, /device:TPU:1, one launch (start us, length us, event | category | flops | bytes accessed | tf_op | source)
XLA Modules:
  0.0 180.6 jit_solution(7628913281298242849)
XLA Ops:
  0.0 2.6 %lift.1 = (f32[64,32,128]{2,1,0:T(8,128)S(1)}, f32[64,32,128]{2,1,0:T(8,128)S(1)}, f32[8,128]{1,0:T(8,128)S(1)}) custom-call(f32[2048,1024]{1,0:T(8,128)} %updates.1, f32[2048,1024]{1,0:T(8,128)} %front.1), custom_call_target="tpu_custom_call" | custom-call | bytes 4194304 | tf_op jit(solution)/shard_map/lift/pallas_call | solution.py:35
  2.6 1.3 collective-permute-start
  3.9 3.0 %pack.3.load = f32[64,96,128]{2,1,0:T(8,128)} custom-call(f32[16,128,1024]{2,1,0:T(8,128)} %bitcast.30, f32[8,128]{1,0:T(8,128)S(1)} %get-tuple-element.22.wait), custom_call_target="tpu_custom_call" | custom-call | bytes 4194304 | tf_op jit(solution)/shard_map/pack/pallas_call | solution.py:35
  8.5 11.5 %all-to-all-start = ((f32[64,96,128]{2,1,0:T(8,128)}), f32[64,96,128]{2,1,0:T(8,128)S(1)}, u32[]{:S(2)}, u32[]{:S(2)}) async-start(f32[64,96,128]{2,1,0:T(8,128)} %get-tuple-element.25), calls=%async_computation | async-start | bytes 6291456 | tf_op jit(solution)/shard_map/all_to_all | solution.py:384
  20.5 2.9 %pack.4.load = f32[64,104,128]{2,1,0:T(8,128)} custom-call(f32[16,128,1024]{2,1,0:T(8,128)} %bitcast.31, f32[8,128]{1,0:T(8,128)S(1)} %get-tuple-element.26.wait), custom_call_target="tpu_custom_call" | custom-call | bytes 4194304 | tf_op jit(solution)/shard_map/pack/pallas_call | solution.py:35
  23.4 37.0 %all-to-all-done.recv = f32[64,96,128]{2,1,0:T(8,128)S(1)} async-done(((f32[64,96,128]{2,1,0:T(8,128)}), f32[64,96,128]{2,1,0:T(8,128)S(1)}, u32[]{:S(2)}, u32[]{:S(2)}) %all-to-all-start) | async-done | bytes 3145760 | tf_op jit(solution)/shard_map/all_to_all | solution.py:384
  60.5 1.4 sum_rows.1
  62.5 5.7 %all-to-all-start.1 = ((f32[64,104,128]{2,1,0:T(8,128)}), f32[64,104,128]{2,1,0:T(8,128)S(1)}, u32[]{:S(2)}, u32[]{:S(2)}) async-start(f32[64,104,128]{2,1,0:T(8,128)} %get-tuple-element.27), calls=%async_computation.1 | async-start | bytes 6815744 | tf_op jit(solution)/shard_map/all_to_all | solution.py:384
  69.4 1.9 %copy-done.1 = f32[64,96,128]{2,1,0:T(8,128)S(1)} copy-done((f32[64,96,128]{2,1,0:T(8,128)S(1)}, f32[64,96,128]{2,1,0:T(8,128)}, u32[]{:S(2)}) %copy-start.1) | copy-done | bytes 3145752
  71.3 1.2 child_sums.1
  74.5 4.1 %pack.5 = f32[64,128,128]{2,1,0:T(8,128)} custom-call(f32[16,128,1024]{2,1,0:T(8,128)} %bitcast.32, f32[8,128]{1,0:T(8,128)S(1)} %get-tuple-element.37.wait), custom_call_target="tpu_custom_call" | custom-call | bytes 8388608 | tf_op jit(solution)/shard_map/pack/pallas_call | solution.py:35
  78.6 32.4 %all-to-all-done.1.mine = f32[64,104,128]{2,1,0:T(8,128)S(1)} async-done(((f32[64,104,128]{2,1,0:T(8,128)}), f32[64,104,128]{2,1,0:T(8,128)S(1)}, u32[]{:S(2)}, u32[]{:S(2)}) %all-to-all-start.1) | async-done | bytes 3407904 | tf_op jit(solution)/shard_map/all_to_all | solution.py:384
  111.0 6.3 %all-to-all-start.2 = ((f32[64,128,128]{2,1,0:T(8,128)}), f32[64,128,128]{2,1,0:T(8,128)}, u32[]{:S(2)}, u32[]{:S(2)}) async-start(f32[64,128,128]{2,1,0:T(8,128)} %pack.5), calls=%async_computation.2 | async-start | bytes 8388608 | tf_op jit(solution)/shard_map/all_to_all | solution.py:384
  118.4 2.1 %collective-permute-start.1 = (f32[64,40,128]{2,1,0:T(8,128)}, f32[64,40,128]{2,1,0:T(8,128)}, u32[]{:S(2)}, u32[]{:S(2)}) collective-permute-start(f32[64,40,128]{2,1,0:T(8,128)} %slice.28), channel_id=1, source_target_pairs={{0,1},{1,0},{2,3},{3,2},{4,5},{5,4},{6,7},{7,6},{8,9},{9,8},{10,11... | collective-permute-start | bytes 3932168 | tf_op jit(solution)/shard_map/ppermute | solution.py:381
  120.8 2.8 %collective-permute-done.1 = f32[64,40,128]{2,1,0:T(8,128)} collective-permute-done((f32[64,40,128]{2,1,0:T(8,128)}, f32[64,40,128]{2,1,0:T(8,128)}, u32[]{:S(2)}, u32[]{:S(2)}) %collective-permute-start.1) | collective-permute-done | bytes 1310752 | tf_op jit(solution)/shard_map/ppermute | solution.py:381
  123.5 3.2 %assemble.1 = (f32[24,128,128]{2,1,0:T(8,128)S(1)}, f32[128,128]{1,0:T(8,128)S(1)}, f32[2,4,4,64,128]{4,3,2,1,0:T(8,128)S(1)}, f32[2,4,4,64,128]{4,3,2,1,0:T(8,128)}) custom-call(s32[1]{0:T(128)} %bitcast.core, f32[256]{0:T(256)S(1)} %reshape.95.flags, f32[6656,128]{1,0:T(8,128)S(1)} %bitcast.28, f32[64,104,128]{2,1,0:T(8,128)S(1)} %all-to-all-done.1.mine, ...), custom_call_target="tpu_custom_call" | custom-call | bytes 3276800 | tf_op jit(solution)/shard_map/assemble/pallas_call | solution.py:35
  129.5 11.7 %cholesky.16 = f32[128,128]{1,0:T(8,128)S(1)} custom-call(f32[128,128]{1,0:T(8,128)S(1)} %fusion.2), custom_call_target="Cholesky" | custom-call | tf_op jit(solution)/shard_map/jit(cholesky)/cholesky | solution.py:415
  142.6 9.8 %custom-call.6 = f32[1,128,128]{1,2,0:T(8,128)S(1)} custom-call(f32[1,128,128]{2,1,0:T(8,128)S(1)} %get-tuple-element.39), custom_call_target="InvertDiagBlocksLowerTriangular" | custom-call | tf_op jit(solution)/shard_map/triangular_solve | solution.py:416
  152.4 2.8 %fusion.solved = f32[3072,128]{1,0:T(8,128)S(1)} fusion(f32[3072,128]{1,0:T(8,128)} %bitcast.29, f32[1,128,128]{1,2,0:T(8,128)S(1)} %custom-call.6), kind=kOutput, calls=%fused_computation.2 | convolution fusion | flops 603979776 | bytes 3211264 | tf_op jit(solution)/shard_map/triangular_solve | solution.py:416
  155.2 13.5 %base.1 = (f32[8,256,1024]{2,1,0:T(8,128)}, f32[8,128,1024]{2,1,0:T(8,128)S(1)}, f32[8,128]{1,0:T(8,128)S(1)}) custom-call(s32[3]{0:T(128)S(1)} %add_convert_fusion.edge, f32[16,128,1024]{2,1,0:T(8,128)} %bitcast.33, f32[3072,128]{1,0:T(8,128)S(1)} %fusion.solved, f32[128,128]{1,0:T(8,128)S(1)} %get-tuple-element.40.head, ...), custom_call_target="tpu_custom_call" | custom-call | bytes 16777216 | tf_op jit(solution)/shard_map/base/pallas_call | solution.py:35
  168.8 2.0 %copy-done.2 = f32[8,128,1024]{2,1,0:T(8,128)} copy-done((f32[8,128,1024]{2,1,0:T(8,128)}, f32[8,128,1024]{2,1,0:T(8,128)S(1)}, u32[]{:S(2)}) %copy-start.2) | copy-done | bytes 4194328
  170.8 3.1 %late_sums.1 = f32[2,4,4,128,128]{4,3,2,1,0:T(8,128)S(1)} custom-call(f32[256]{0:T(256)S(1)} %reshape.96.flags, f32[64,128,128]{2,1,0:T(8,128)} %all-to-all-done.2.recv, f32[8,128]{1,0:T(8,128)S(1)} %get-tuple-element.38.wait), custom_call_target="tpu_custom_call" | custom-call | bytes 6291456 | tf_op jit(solution)/shard_map/late_sums/pallas_call | solution.py:35
  174.6 3.7 %add_own.1.rest = f32[8,128,1024]{2,1,0:T(8,128)S(1)} custom-call(s32[1]{0:T(128)} %bitcast.core, f32[256]{0:T(256)S(1)} %reshape.96.flags, f32[8,128,1024]{2,1,0:T(8,128)S(1)} %copy-done.3, f32[64,128,128]{2,1,0:T(8,128)} %all-to-all-done.2.recv), custom_call_target="tpu_custom_call", output_to_operand_aliasing={{}: (2, {})} | custom-call | bytes 12582912 | tf_op jit(solution)/shard_map/add_own/pallas_call | solution.py:35
  178.4 2.1 %add_late.1 = f32[8,256,1024]{2,1,0:T(8,128)} custom-call(s32[1]{0:T(128)} %bitcast.core, f32[8,256,1024]{2,1,0:T(8,128)} %get-tuple-element.35.before, f32[8,128,1024]{2,1,0:T(8,128)S(1)} %add_own.1.rest, f32[2,4,4,128,128]{4,3,2,1,0:T(8,128)S(1)} %collective-permute-done.4.sib), custom_call_target="tpu_custom_call", output_to_operand_aliasing={{}: (1, {})} | custom-call | bytes 12582912 | tf_op jit(solution)/shard_map/add_late/pallas_call | solution.py:35
  (59 shorter events, 12.1 us)
Async XLA Ops:
  2.6 4.9 %collective-permute-start = (f32[64,32,128]{2,1,0:T(8,128)S(1)}, f32[64,32,128]{2,1,0:T(8,128)S(1)}, u32[]{:S(2)}, u32[]{:S(2)}) collective-permute-start(f32[64,32,128]{2,1,0:T(8,128)S(1)} %get-tuple-element.24), channel_id=1, source_target_pairs={{0,1},{8,9},{16,17},{24,25},{32,33},{40,41},{48,49},{56,57},{64,65... | collective-permute-start | bytes 3145736 | tf_op jit(solution)/shard_map/ppermute | solution.py:401
  8.5 11.5 %copy-start.10 = (s32[4,64]{1,0:T(4,128)S(1)}, s32[4,64]{1,0:T(4,128)}, u32[]{:S(2)}) copy-start(s32[4,64]{1,0:T(4,128)} %param.5) | copy-start | bytes 3076
  8.5 51.9 %all-to-all-start = ((f32[64,96,128]{2,1,0:T(8,128)}), f32[64,96,128]{2,1,0:T(8,128)S(1)}, u32[]{:S(2)}, u32[]{:S(2)}) async-start(f32[64,96,128]{2,1,0:T(8,128)} %get-tuple-element.25), calls=%async_computation | async-start | bytes 6291456 | tf_op jit(solution)/shard_map/all_to_all | solution.py:384
  60.4 2.1 %copy-start = (f32[64,96,128]{2,1,0:T(8,128)}, f32[64,96,128]{2,1,0:T(8,128)S(1)}, u32[]{:S(2)}) copy-start(f32[64,96,128]{2,1,0:T(8,128)S(1)} %all-to-all-done.recv) | copy-start | bytes 9437188
  62.5 48.5 %all-to-all-start.1 = ((f32[64,104,128]{2,1,0:T(8,128)}), f32[64,104,128]{2,1,0:T(8,128)S(1)}, u32[]{:S(2)}, u32[]{:S(2)}) async-start(f32[64,104,128]{2,1,0:T(8,128)} %get-tuple-element.27), calls=%async_computation.1 | async-start | bytes 6815744 | tf_op jit(solution)/shard_map/all_to_all | solution.py:384
  69.4 1.9 %copy-start.1 = (f32[64,96,128]{2,1,0:T(8,128)S(1)}, f32[64,96,128]{2,1,0:T(8,128)}, u32[]{:S(2)}) copy-start(f32[64,96,128]{2,1,0:T(8,128)} %copy-done) | copy-start | bytes 9437188
  72.5 1.0 copy-start.5
  73.5 1.0 copy-start.9
  111.0 59.8 %all-to-all-start.2 = ((f32[64,128,128]{2,1,0:T(8,128)}), f32[64,128,128]{2,1,0:T(8,128)}, u32[]{:S(2)}, u32[]{:S(2)}) async-start(f32[64,128,128]{2,1,0:T(8,128)} %pack.5), calls=%async_computation.2 | async-start | bytes 8388608 | tf_op jit(solution)/shard_map/all_to_all | solution.py:384
  118.4 5.1 %collective-permute-start.1 = (f32[64,40,128]{2,1,0:T(8,128)}, f32[64,40,128]{2,1,0:T(8,128)}, u32[]{:S(2)}, u32[]{:S(2)}) collective-permute-start(f32[64,40,128]{2,1,0:T(8,128)} %slice.28), channel_id=1, source_target_pairs={{0,1},{1,0},{2,3},{3,2},{4,5},{5,4},{6,7},{7,6},{8,9},{9,8},{10,11... | collective-permute-start | bytes 3932168 | tf_op jit(solution)/shard_map/ppermute | solution.py:381
  120.7 34.5 %collective-permute-start.2 = (f32[2,4,4,64,128]{4,3,2,1,0:T(8,128)}, f32[2,4,4,64,128]{4,3,2,1,0:T(8,128)}, u32[]{:S(2)}, u32[]{:S(2)}) collective-permute-start(f32[2,4,4,64,128]{4,3,2,1,0:T(8,128)} %copy-done.9), channel_id=1, source_target_pairs={{0,1},{1,0},{2,3},{3,2},{4,5},{5,4},{6,7},{7,6},{8,9},{9,8},{10,11... | collective-permute-start | bytes 3145736 | tf_op jit(solution)/shard_map/ppermute | solution.py:381
  126.8 1.1 copy-start.4
  127.9 1.0 copy-start.7
  128.9 26.3 %copy-start.6 = (f32[2,4,4,64,128]{4,3,2,1,0:T(8,128)S(1)}, f32[2,4,4,64,128]{4,3,2,1,0:T(8,128)}, u32[]{:S(2)}) copy-start(f32[2,4,4,64,128]{4,3,2,1,0:T(8,128)} %copy-done.5) | copy-start | bytes 3145732
  128.9 26.3 %copy-start.8 = (f32[2,4,4,64,128]{4,3,2,1,0:T(8,128)S(1)}, f32[2,4,4,64,128]{4,3,2,1,0:T(8,128)}, u32[]{:S(2)}) copy-start(f32[2,4,4,64,128]{4,3,2,1,0:T(8,128)} %copy-done.7) | copy-start | bytes 3145732
  129.0 26.3 %collective-permute-start.3 = (f32[2,4,4,64,128]{4,3,2,1,0:T(8,128)}, f32[2,4,4,64,128]{4,3,2,1,0:T(8,128)S(1)}, u32[]{:S(2)}, u32[]{:S(2)}) collective-permute-start(f32[2,4,4,64,128]{4,3,2,1,0:T(8,128)} %get-tuple-element.34), channel_id=1, source_target_pairs={{0,1},{1,0},{2,3},{3,2},{4,5},{5,4},{6,7},{7,6},{8,9},{9,8},{10,11... | collective-permute-start | bytes 3145736 | tf_op jit(solution)/shard_map/ppermute | solution.py:381
  168.8 2.0 %copy-start.2 = (f32[8,128,1024]{2,1,0:T(8,128)}, f32[8,128,1024]{2,1,0:T(8,128)S(1)}, u32[]{:S(2)}) copy-start(f32[8,128,1024]{2,1,0:T(8,128)S(1)} %get-tuple-element.36.rest) | copy-start | bytes 12582916
  170.8 3.8 %copy-start.3 = (f32[8,128,1024]{2,1,0:T(8,128)S(1)}, f32[8,128,1024]{2,1,0:T(8,128)}, u32[]{:S(2)}) copy-start(f32[8,128,1024]{2,1,0:T(8,128)} %copy-done.2) | copy-start | bytes 12582916
  173.9 4.4 %collective-permute-start.4 = (f32[2,4,4,128,128]{4,3,2,1,0:T(8,128)S(1)}, f32[2,4,4,128,128]{4,3,2,1,0:T(8,128)S(1)}, u32[]{:S(2)}, u32[]{:S(2)}) collective-permute-start(f32[2,4,4,128,128]{4,3,2,1,0:T(8,128)S(1)} %late_sums.1), channel_id=1, source_target_pairs={{0,1},{1,0},{2,3},{3,2},{4,5},{5,4},{6,7},{7,6},{8,9},{9,8},{10,11... | collective-permute-start | bytes 6291464 | tf_op jit(solution)/shard_map/ppermute | solution.py:381

commit v3 on v2

v3 whole, which is shorter than its diff:
```python
import jax
import jax.numpy as jnp
from jax import lax
from jax.experimental import pallas as pl
from jax.experimental.pallas import tpu as pltpu
from jax.sharding import Mesh
from jax.sharding import PartitionSpec as P

CHIP = ("y", "zh", "x", "zl")
ALL = CHIP + ("core",)
CORE_SWAP = [(0, 1), (1, 0)]
VMEM = pl.BlockSpec(memory_space=pltpu.VMEM)
SMEM = pl.BlockSpec(memory_space=pltpu.SMEM)
HBM = pl.BlockSpec(memory_space=pltpu.HBM)
F32 = jnp.float32


def call(kernel, out_shape, in_specs, out_specs, name, moved, scratch=(), aliases=None, limit=16):
    many = isinstance(out_shape, tuple)
    outs = zip(out_shape, out_specs) if many else ((out_shape, out_specs),)
    outs = tuple(pltpu.HBM(array.shape, array.dtype) if spec is HBM else array for array, spec in outs)
    run = pl.pallas_call(
        kernel,
        out_shape=outs if many else outs[0],
        in_specs=in_specs,
        out_specs=out_specs,
        scratch_shapes=scratch,
        input_output_aliases=aliases or {},
        compiler_params=pltpu.CompilerParams(vmem_limit_bytes=limit << 20),
        cost_estimate=pl.CostEstimate(flops=0, bytes_accessed=moved, transcendentals=0),
        name=name,
    )

    def placed(*args):
        return run(*(
            pltpu.with_memory_space_constraint(arg, pltpu.HBM) if spec is HBM else arg
            for arg, spec in zip(args, in_specs)
        ))

    return placed


def shape(*dims):
    return jax.ShapeDtypeStruct(dims, F32)


TOKEN = shape(8, 128)


def run_lift(updates, front, bs):
    rows = updates.shape[0]
    half = bs // 2

    def lift(updates, front, low, high, token, ucol, fcol, sems):
        copies = [
            pltpu.make_async_copy(whole.at[:, pl.ds(0, bs)], part, sems.at[i])
            for i, (whole, part) in enumerate(((updates, ucol), (front, fcol)))
        ]
        for copy in copies:
            copy.start()
        token[...] = jnp.zeros_like(token)
        for at, (copy, part) in enumerate(zip(copies, (ucol, fcol))):
            copy.wait()

            def one(chip, carry):
                low[chip, 16 * at:16 * at + 16] = part[pl.ds(chip, 16, stride=bs), :]
                high[chip, 16 * at:16 * at + 16] = part[pl.ds(half + chip, 16, stride=bs), :]
                return carry

            lax.fori_loop(0, half, one, 0, unroll=8)

    share = shape(half, 32, bs)
    return call(
        lift, (share, share, TOKEN), [HBM, HBM], (VMEM,) * 3, "lift", 16 * rows * bs,
        [pltpu.VMEM((rows, bs), F32), pltpu.VMEM((rows, bs), F32), pltpu.SemaphoreType.DMA((2,))],
    )(updates, front)


def run_pack(blocks, wait, gi, at, rows, extra, ends=False):
    bs = blocks.shape[1]

    def pack(blocks, wait, out, *rest):
        held, read_sems, write_sems, end_sem = rest[-4:]

        def read(j):
            return pltpu.make_async_copy(blocks.at[8 * gi + j, pl.ds(at, rows)], held.at[j], read_sems.at[j])

        def write(j, jc):
            lanes = pl.ds(jc * bs, bs)
            return pltpu.make_async_copy(
                held.at[j, :, lanes], out.at[8 * j + jc, pl.ds(0, rows)], write_sems.at[8 * j + jc]
            )

        for j in range(8):
            read(j).start()
        if ends:
            last = pltpu.make_async_copy(blocks.at[pl.ds(0, 8), pl.ds(bs - 8, 8)], rest[0], end_sem)
            last.start()
        for j in range(8):
            read(j).wait()
            for jc in range(8):
                write(j, jc).start()
        if ends:
            last.wait()
        for j in range(8):
            for jc in range(8):
                write(j, jc).wait()

    load = shape(64, rows + extra, bs)
    return call(
        pack, (load, shape(8, 8, 8 * bs)) if ends else load, [HBM, VMEM], (HBM, VMEM) if ends else HBM, "pack",
        512 * rows * bs,
        [
            pltpu.VMEM((8, rows, 8 * bs), F32), pltpu.SemaphoreType.DMA((8,)), pltpu.SemaphoreType.DMA((64,)),
            pltpu.SemaphoreType.DMA,
        ],
    )(blocks, wait)


def run_put_rows(child_map, ends, load, low, other, rows):
    bs = low.shape[-1]

    def put_rows(child_map, ends, load, low, other, out, token, region, sem):
        y, zh, x, zl, t = (lax.axis_index(a) for a in ALL)
        me, col_pair = 2 * y + zh, 2 * x + zl
        token[...] = jnp.zeros_like(token)
        for c, part in ((0, low), (1, other)):
            @pl.when(t == c)
            def _():
                region[...] = part[...]

        @pl.when((col_pair == 0) & (child_map[me // 4, 0] // 8 % 2 == 0))
        def _():
            for gi in range(2):
                group = 2 * (me % 4) + gi
                up = child_map[me // 4, 8 * group + me] // 8 % 2
                to, of = pl.ds(16 + 8 * up + group, 1), pl.ds(8 * gi + me, 1)
                for at in range(64):
                    region[at, to, :] += region[at, of, :]

        slot = pl.ds(jnp.where(col_pair == 4, slot_of(0, 4), slot_of(me, 0)), 1)
        for j in range(8):
            for jc in range(8):
                region[8 * j + jc, slot, :] = ends[j, 7:8, jc * bs:(jc + 1) * bs]
        copy = pltpu.make_async_copy(region, out.at[:, pl.ds(rows, 32)], sem)
        copy.start()
        copy.wait()

    return call(
        put_rows, (shape(*load.shape), TOKEN), [SMEM, VMEM, HBM, VMEM, VMEM], (HBM, VMEM), "put_rows", 8 * other.size,
        [pltpu.VMEM(low.shape, F32), pltpu.SemaphoreType.DMA], aliases={2: 0},
    )(child_map, ends, load, low, other)


def run_sum_rows(marks, recv, ends, load, first):
    bs = recv.shape[-1]
    last = load.shape[1] - 40

    def sum_rows(marks, recv, ends, load, out, token, kids, total, rows, sems):
        token[...] = jnp.zeros_like(token)
        for up in range(2):
            for sr in range(4):
                acc = jnp.zeros((16, bs), F32)
                for h in range(2):
                    for v in range(2):
                        acc += marks[up, sr, 2 * v + h] * recv[(4 * h + sr) * 8 + 4 * v, first:first + 16]
                kids[pl.ds((up * 4 + sr) * 16, 16)] = acc
        for j in range(8):
            total[j] = kids[pl.ds(j, 16, stride=8), :] + recv[8 * j, first + 16:first + 32]
        copies = []
        for j in range(8):
            for jc in range(8):
                at = 8 * j + jc
                rows[at, 0:8] = ends[j, :, jc * bs:(jc + 1) * bs]
                rows[at, 7:8] = total[0, 0:1]
                rows[at, 8:24] = total[j]
                rows[at, 24:40] = total[jc]
            some = pl.ds(8 * j, 8)
            copies.append(pltpu.make_async_copy(rows.at[some], out.at[some, pl.ds(last, 40)], sems.at[j]))
            copies[-1].start()
        for copy in copies:
            copy.wait()

    return call(
        sum_rows, (shape(*load.shape), TOKEN), [VMEM, VMEM, VMEM, HBM], (HBM, VMEM), "sum_rows", 64 * 40 * bs * 8,
        [
            pltpu.VMEM((128, bs), F32), pltpu.VMEM((8, 16, bs), F32), pltpu.VMEM((64, 40, bs), F32),
            pltpu.SemaphoreType.DMA((8,)),
        ],
        aliases={3: 0},
    )(marks, recv, ends, load)


def add_blocks(flags, recv, sr, scp, here, sides, behind=None):
    sums = {}
    for h in range(2):
        for v in range(2):
            source, col_pair = 4 * h + sr, 4 * v + scp
            rows = here if behind is None else pl.ds(behind + slot_of(source, col_pair), 1)
            block = recv[source * 8 + col_pair, rows]
            for up in range(2):
                for side in sides:
                    term = flags[((((h + 2 * v) * 4 + sr) * 4 + scp) * 2 + up) * 2 + side] * block
                    sums[up, side] = sums[up, side] + term if (up, side) in sums else term
    return sums


def slot_of(row, col_pair):
    return 16 if col_pair == 4 else 8 + row


def child_sums(flags, recv, outs, held, sems, rows):
    step = 32
    more = held[0].shape[3] > rows

    def write(side, sr):
        return pltpu.make_async_copy(held[side].at[:, sr], outs[side].at[:, sr], sems.at[side, sr])

    for sr in range(4):
        def one(i, carry):
            at = pl.multiple_of(i * step, step)
            for scp in range(4):
                sums = add_blocks(flags, recv, sr, scp, pl.ds(at, step), (0, 1))
                for up in range(2):
                    for side in range(2):
                        held[side][up, sr, scp, pl.ds(at, step)] = sums[up, side]
            return carry

        lax.fori_loop(0, rows // step, one, 0)
        for scp in range(4) if more else ():
            sums = add_blocks(flags, recv, sr, scp, None, (0, 1), rows)
            for up in range(2):
                for side in range(2):
                    held[side][up, sr, scp, rows:rows + 1] = sums[up, side]
        for side in range(2):
            write(side, sr).start()

    def finish():
        for sr in range(4):
            for side in range(2):
                write(side, sr).wait()

    return finish


def sums_scratch(rows, bs):
    return [pltpu.VMEM((2, 4, 4, rows, bs), F32)] * 2 + [pltpu.SemaphoreType.DMA((2, 4))]


def run_child_sums(flags, recv, wait, rows, bs):
    def kernel(flags, recv, wait, own, sib, token, *held):
        token[...] = jnp.zeros_like(token)
        child_sums(flags, recv, (own, sib), held[:2], held[2], rows)()

    part = shape(2, 4, 4, rows + 8, bs)
    return call(
        kernel, (part, part, TOKEN), [SMEM, VMEM, VMEM], (HBM, HBM, VMEM), "child_sums", 64 * rows * bs * 8,
        sums_scratch(rows + 8, bs),
    )(flags, recv, wait)


def run_assemble(core, flags, mine, other, first):
    chips, width, bs = mine.shape
    half = bs // 2

    def assemble(core, flags, flat, mine, other, slabs, corner, own, sib, out, sem, *held):
        t = core[0]
        finish = child_sums(flags, mine, (own, sib), held[:2], held[2], first)
        for who, (part, span, at) in enumerate(((flat, width, first), (other, 40, 8))):
            rows_at = pl.multiple_of(half * (t if who == 0 else 1 - t), half)
            for s in range(25):
                start = at + s if s < 16 else at + s + 8 * t if s < 24 else at - 1
                rows = part[pl.ds(start, half, stride=span), :]
                if s < 24:
                    out[s, pl.ds(rows_at, half)] = rows
                else:
                    corner[pl.ds(rows_at, half)] = rows
        copy = pltpu.make_async_copy(out, slabs, sem)
        copy.start()
        finish()
        copy.wait()

    part = shape(2, 4, 4, first, bs)
    return call(
        assemble, (shape(24, bs, bs), shape(bs, bs), part, part), [SMEM, SMEM, VMEM, VMEM, VMEM], (HBM, VMEM, HBM, HBM),
        "assemble", 200 * bs * bs,
        [pltpu.VMEM((24, bs, bs), F32), pltpu.SemaphoreType.DMA] + sums_scratch(first, bs),
    )(core, flags, mine.reshape(chips * width, bs), mine, other.reshape(chips * 40, bs))


def split(a):
    high = a.astype(jnp.bfloat16)
    left = a - high.astype(F32)
    mid = left.astype(jnp.bfloat16)
    return high, mid, (left - mid.astype(F32)).astype(jnp.bfloat16)


def spread(left, mine, other):
    return jnp.where(left, mine, other), jnp.where(left, other, mine)


def pair(scp, bs):
    return slice(2 * scp * bs, (2 * scp + 1) * bs), slice((2 * scp + 1) * bs, (2 * scp + 2) * bs)


def run_base(edge, front, solved, head, early, bs):
    rows, cols = front.shape
    blocks, tile, step = rows // bs, 256, 32
    cut = early[0].shape[3] - 8

    group = 4

    def base(edge, front, solved, head, own0, sib0, own1, sib1, out, rest, token, held, right, o0, s0, o1, s1, sems, more, back):
        top, col_zero, left = edge[0] == 1, edge[1] == 1, edge[2] == 0
        token[...] = jnp.zeros_like(token)

        def read(i):
            return pltpu.make_async_copy(front.at[i], held.at[i], sems.at[i])

        def write(i, to):
            return pltpu.make_async_copy(held.at[i], to.at[i // 2, pl.ds(0, bs)], back.at[i])

        sums = [
            pltpu.make_async_copy(src, dst, more.at[n])
            for n, (src, dst) in enumerate(((own0, o0), (sib0, s0), (own1, o1), (sib1, s1)))
        ]
        for i in range(blocks):
            read(i).start()
            if i == group - 1:
                for copy in sums:
                    copy.start()

        for at in range(0, cols, bs):
            high, mid, low = split(solved[rows + at:rows + at + bs])
            right[at:at + bs] = jnp.concatenate([high, high, mid, high, mid, low], axis=1)

        def some(q, carry):
            own = solved[pl.ds(pl.multiple_of(q * group * bs, group * bs), group * bs)]
            high, mid, low = split(own)
            parts = jnp.concatenate([high, mid, high, low, mid, high], axis=1)
            for n in range(group):
                read(q * group + n).wait()
            for at in range(0, cols, tile):
                lanes = slice(at, at + tile)
                product = lax.dot_general(
                    parts, right[at:at + tile], (((1,), (1,)), ((), ())), preferred_element_type=F32
                )
                for n in range(group):
                    keep = jnp.where(top & (q == 0), 0.0, 1.0) if n == 0 else 1.0
                    held[q * group + n, :, lanes] -= keep * product[n * bs:(n + 1) * bs]

            @pl.when(col_zero)
            def _():
                for n in range(group):
                    held[q * group + n, :, 0:bs] = own[n * bs:(n + 1) * bs]

            @pl.when(top & col_zero & (q == 0))
            def _():
                held[0, :, 0:bs] = head[...]

            @pl.when(q == 0)
            def _():
                for copy in sums:
                    copy.wait()
                for late, soon in ((o1, o0), (s1, s0)):
                    late[:, :, :, bs - cut - 1:bs - cut] = soon[:, :, :, cut:cut + 1]

            for n in range(0, group, 2):
                i = q * group + n
                up, sr = i // 8, i // 2 % 4
                for at in range(0, bs, step):
                    here = slice(at, at + step)
                    own, sib, inner = (o0, s0, at) if at < cut else (o1, s1, at - cut)
                    for scp in range(4):
                        two = spread(left, own[up, sr, scp, inner:inner + step], sib[up, sr, scp, inner:inner + step])
                        for lanes, add in zip(pair(scp, bs), two):
                            held[i, here, lanes] += add
                write(i, out).start()
                write(i + 1, rest).start()
            return carry

        lax.fori_loop(0, blocks // group, some, 0)

        def finish(n, carry):
            write(2 * n, out).wait()
            write(2 * n + 1, rest).wait()
            return carry

        lax.fori_loop(0, blocks // 2, finish, 0)

    parts = [pltpu.VMEM(a.shape, F32) for a in early]
    return call(
        base, (shape(blocks // 2, 2 * bs, cols), shape(blocks // 2, bs, cols), TOKEN), [SMEM, HBM, VMEM, VMEM] + [HBM] * 4,
        (HBM, HBM, VMEM), "base", rows * cols * 8,
        [pltpu.VMEM((blocks, bs, cols), F32), pltpu.VMEM((cols, 6 * bs), jnp.bfloat16)] + parts
        + [pltpu.SemaphoreType.DMA((n,)) for n in (blocks, 4, blocks)],
        limit=28,
    )(edge, front.reshape(blocks, bs, cols), solved, head, *early)


def run_late_sums(flags, recv, wait):
    chips, bs, _ = recv.shape
    step = 32

    def late_sums(flags, recv, wait, sib, held, sems):
        def read(sr, h):
            some = pl.ds((4 * h + sr) * 8, 8)
            return pltpu.make_async_copy(recv.at[some], held.at[some], sems.at[2 * sr + h])

        for sr in range(4):
            for h in range(2):
                read(sr, h).start()
        for sr in range(4):
            for h in range(2):
                read(sr, h).wait()

            def one(i, carry):
                here = pl.ds(pl.multiple_of(i * step, step), step)
                for scp in range(4):
                    sums = add_blocks(flags, held, sr, scp, here, (1,))
                    for up in range(2):
                        sib[up, sr, scp, here] = sums[up, 1]
                return carry

            lax.fori_loop(0, bs // step, one, 0)

    return call(
        late_sums, shape(2, 4, 4, bs, bs), [SMEM, HBM, VMEM], VMEM, "late_sums", 96 * bs * bs * 4,
        [pltpu.VMEM((chips, bs, bs), F32), pltpu.SemaphoreType.DMA((8,))],
    )(flags, recv, wait)


def run_add_own(core, flags, rest, recv):
    blocks, bs, cols = rest.shape
    step = 32

    def add_own(core, flags, rest, recv, out, held, sems, more):
        def read(sr, h):
            some = pl.ds((4 * h + sr) * 8, 8)
            return pltpu.make_async_copy(recv.at[some], held.at[some], sems.at[2 * sr + h])

        def base(i):
            return pltpu.make_async_copy(rest.at[i], out.at[i], more.at[i])

        for sr in range(4):
            for n in range(2):
                read(sr, n).start()
                base(4 * n + sr).start()
        for sr in range(4):
            for n in range(2):
                read(sr, n).wait()
                base(4 * n + sr).wait()

            def one(i, carry):
                here = pl.ds(pl.multiple_of(i * step, step), step)
                for scp in range(4):
                    sums = add_blocks(flags, held, sr, scp, here, (0,))
                    for up in range(2):
                        two = spread(core[0] == 0, sums[up, 0], 0.0)
                        for lanes, add in zip(pair(scp, bs), two):
                            out[4 * up + sr, here, lanes] += add
                return carry

            lax.fori_loop(0, bs // step, one, 0)

    return call(
        add_own, shape(blocks, bs, cols), [SMEM, SMEM, HBM, HBM], VMEM, "add_own", blocks * bs * cols * 12,
        [pltpu.VMEM(recv.shape, F32), pltpu.SemaphoreType.DMA((8,)), pltpu.SemaphoreType.DMA((8,))],
    )(core, flags, rest, recv)


def run_add_late(core, out, rest, sib):
    blocks, bs, cols = rest.shape
    step = 32

    def add_late(core, before, rest, sib, out, done, sems):
        def write(i):
            return pltpu.make_async_copy(done.at[i], out.at[i, pl.ds(bs, bs)], sems.at[i])

        def one(i, carry):
            up, sr = i // 4, i % 4
            for at in range(0, bs, step):
                here = slice(at, at + step)
                for scp in range(4):
                    for lanes, add in zip(pair(scp, bs), spread(core[0] == 0, 0.0, sib[up, sr, scp, here])):
                        done[i, here, lanes] = rest[i, here, lanes] + add
            write(i).start()
            return carry

        lax.fori_loop(0, blocks, one, 0)
        lax.fori_loop(0, blocks, lambda i, c: (write(i).wait(), c)[1], 0)

    return call(
        add_late, shape(*out.shape), [SMEM, HBM, VMEM, VMEM], HBM, "add_late", out.size * 6,
        [pltpu.VMEM((blocks, bs, cols), F32), pltpu.SemaphoreType.DMA((blocks,))], aliases={1: 0},
    )(core, out, rest, sib)


def body(front, updates, child_map):
    rows_dev, cols_dev = front.shape
    bs = rows_dev // 16
    half = bs // 2
    y, zh, x, zl, t = (lax.axis_index(a) for a in ALL)
    ji, jc = 2 * y + zh, 2 * x + zl
    col = 2 * jc + t
    core = t.reshape(1).astype(jnp.int32)
    blocks = updates.reshape(16, bs, cols_dev)

    def swap(a):
        return lax.ppermute(a, "core", CORE_SWAP)

    def send(load):
        return lax.all_to_all(load, CHIP, 0, 0, tiled=True)

    bits = (child_map.reshape(4, 8, 8) // 8) % 2
    col_bits = lax.dynamic_index_in_dim(bits, jc, 2, keepdims=False).reshape(4, 4, 2)
    col_bits = lax.dynamic_index_in_dim(col_bits, t, 2, keepdims=False)
    row_bits = lax.dynamic_index_in_dim(bits, ji, 2, keepdims=False).reshape(4, 4, 2)
    in_panel = (col == 0) & (jnp.arange(4) == 0)
    side = jnp.stack([(col_bits == t) & ~in_panel, col_bits != t], -1)
    up = row_bits[..., None] == jnp.arange(2)
    flags = [
        (up[:, :, gi, None, :, None] & side[:, None, :, None, :]).astype(F32).reshape(-1) for gi in range(2)
    ]
    live = bits[:, 0, 0] == 0
    marks = (bits.reshape(4, 4, 16).transpose(1, 0, 2) == jnp.arange(2)[:, None, None, None]) & live[:, None]
    sr_at, h_at, j_at = jnp.arange(4)[:, None, None], jnp.arange(4)[None, :, None], jnp.arange(16)[None, None] % 8
    marks &= ~((h_at < 2) & (4 * h_at + sr_at == j_at))
    marks = jnp.broadcast_to(marks.astype(F32)[..., None], (2, 4, 4, 16, bs))

    low, high, lifted = run_lift(updates, front, bs)
    other = lax.ppermute(high, ALL, [((r * 8 + q) * 2, (r * 8 + q) * 2 + 1) for r in range(8) for q in (0, 4)])
    load0, ends = run_pack(blocks, lifted, 0, 0, half, 32, True)
    load0, sent0 = run_put_rows(child_map, ends, load0, low, other, half)
    recv0 = send(load0)

    load1, sent1 = run_sum_rows(marks, recv0, ends, run_pack(blocks, sent0, 0, half, half, 32), half)
    recv1 = send(load1)
    own0, sib0, summed0 = run_child_sums(flags[0], recv0, sent1, half, bs)
    sib0 = swap(sib0)

    recv2 = send(run_pack(blocks, summed0, 1, 0, bs, 0))

    slabs, corner, own1, sib1 = run_assemble(core, flags[0], recv1, swap(recv1[:, half - 8:]), half)
    sib1 = swap(sib1)
    head = jnp.linalg.cholesky(corner)
    solved = lax.linalg.triangular_solve(
        head, slabs.reshape(24 * bs, bs), left_side=False, lower=True, transpose_a=True
    )
    edge = jnp.stack([ji == 0, col == 0, t == 1]).astype(jnp.int32)
    out, rest, based = run_base(edge, front, solved, head, (own0, sib0, own1, sib1), bs)

    sib2 = swap(run_late_sums(flags[1], recv2, based))
    rest = run_add_own(core, flags[1], rest, recv2)
    return run_add_late(core, out, rest, sib2).reshape(rows_dev, cols_dev)


def solution(mesh):
    fine = Mesh(mesh.devices.reshape(4, 2, 4, 2, 2), ALL)
    spec = P(("y", "zh"), ("x", "zl", "core"))
    return jax.shard_map(body, mesh=fine, in_specs=(spec, spec, P()), out_specs=spec, check_vma=False)
```

time: 181 us -> 179 us (0.989)
  local copies, waits for them, and re-layouts: 11.3 us -> 6.1 us
  starting transfers between devices: 28 us -> 31.3 us
    unnamed x22 -> x8, local copies, waits for them, and re-layouts: 8.66 us -> 3.45 us
    ppermute x4, starting transfers between devices: 3.25 us -> 6.57 us  [swap(): return lax.ppermute(a, 'core', CORE_SWAP)]
  transfers between devices with their start and end apart: 8 -> 8, of which waited for: 4 -> 5; matrix products, arithmetic and copies ran while one was open for 16% -> 16% of each run, Pallas kernels for 18% -> 17%
where the time goes in v3:
time: 179 us
  waiting for transfers between devices  72.7 us (41%)
  Pallas kernels  41.7 us (23%)
  starting transfers between devices  31.3 us (17%)
  other arithmetic  23.7 us (13%)
  local copies, waits for them, and re-layouts  6.1 us (3%)
  matrix products  2.83 us (2%)
    all_to_all x3, waiting for transfers between devices, send(): return lax.all_to_all(load, CHIP, 0, 0, tiled=True)  69.2 us
    pallas_call x12, Pallas kernels, placed(): run(*(pltpu.with_memory_space_constraint(arg, pltpu.HBM) if spec is HBM e...  41.7 us
    all_to_all x3, starting transfers between devices, send(): return lax.all_to_all(load, CHIP, 0, 0, tiled=True)  23.4 us
    another operation x3, other arithmetic, body(): head = jnp.linalg.cholesky(corner)  12.5 us
    another operation x2, other arithmetic, body(): lax.linalg.triangular_solve(head, slabs.reshape(24 * bs, bs), left_side=F...  10.5 us
    ppermute x4, starting transfers between devices, swap(): return lax.ppermute(a, 'core', CORE_SWAP)  6.57 us
  transfers between devices with their start and end apart: 8, of which 5 were waited for; matrix products, arithmetic and copies ran while one was open for 16% of the time, Pallas kernels for 17%

profile of v3, /device:TPU:1, one launch (start us, length us, event | category | flops | bytes accessed | tf_op | source)
XLA Modules:
  0.0 178.8 jit_solution(6566852296244418847)
XLA Ops:
  0.0 2.5 %lift.1 = (f32[64,32,128]{2,1,0:T(8,128)S(1)}, f32[64,32,128]{2,1,0:T(8,128)S(1)}, f32[8,128]{1,0:T(8,128)S(1)}) custom-call(f32[2048,1024]{1,0:T(8,128)} %updates.1, f32[2048,1024]{1,0:T(8,128)} %front.1), custom_call_target="tpu_custom_call" | custom-call | bytes 4194304 | tf_op jit(solution)/shard_map/lift/pallas_call | solution.py:35
  3.8 2.9 %pack.3 = (f32[64,96,128]{2,1,0:T(8,128)}, f32[8,8,1024]{2,1,0:T(8,128)S(1)}) custom-call(f32[16,128,1024]{2,1,0:T(8,128)} %bitcast.29, f32[8,128]{1,0:T(8,128)S(1)} %get-tuple-element.24.wait), custom_call_target="tpu_custom_call" | custom-call | bytes 4194304 | tf_op jit(solution)/shard_map/pack/pallas_call | solution.py:35
  7.4 2.0 %put_rows.1 = (f32[64,96,128]{2,1,0:T(8,128)}, f32[8,128]{1,0:T(8,128)S(1)}) custom-call(s32[4,64]{1,0:T(4,128)S(1)} %copy-done.2, f32[8,8,1024]{2,1,0:T(8,128)S(1)} %get-tuple-element.25.ends, f32[64,96,128]{2,1,0:T(8,128)} %get-tuple-element.26.load, f32[64,32,128]{2,1,0:T(8,128)S(1)} %get-tuple-element.27.low, ...), custom_call_target="tpu_custom_call", output_to_operand_aliasing={{0}: (2, {})} | custom-call | bytes 2097152 | tf_op jit(solution)/shard_map/put_rows/pallas_call | solution.py:35
  9.4 11.2 %all-to-all-start = ((f32[64,96,128]{2,1,0:T(8,128)}), f32[64,96,128]{2,1,0:T(8,128)S(1)}, u32[]{:S(2)}, u32[]{:S(2)}) async-start(f32[64,96,128]{2,1,0:T(8,128)} %get-tuple-element.29), calls=%async_computation | async-start | bytes 6291456 | tf_op jit(solution)/shard_map/all_to_all | solution.py:513
  21.2 3.0 %pack.4.load = f32[64,96,128]{2,1,0:T(8,128)} custom-call(f32[16,128,1024]{2,1,0:T(8,128)} %bitcast.30, f32[8,128]{1,0:T(8,128)S(1)} %get-tuple-element.30.wait), custom_call_target="tpu_custom_call" | custom-call | bytes 4194304 | tf_op jit(solution)/shard_map/pack/pallas_call | solution.py:35
  24.2 36.8 %all-to-all-done.recv = f32[64,96,128]{2,1,0:T(8,128)S(1)} async-done(((f32[64,96,128]{2,1,0:T(8,128)}), f32[64,96,128]{2,1,0:T(8,128)S(1)}, u32[]{:S(2)}, u32[]{:S(2)}) %all-to-all-start) | async-done | bytes 3145760 | tf_op jit(solution)/shard_map/all_to_all | solution.py:513
  63.1 6.0 %all-to-all-start.1 = ((f32[64,96,128]{2,1,0:T(8,128)}), f32[64,96,128]{2,1,0:T(8,128)S(1)}, u32[]{:S(2)}, u32[]{:S(2)}) async-start(f32[64,96,128]{2,1,0:T(8,128)} %get-tuple-element.31), calls=%async_computation.1 | async-start | bytes 6291456 | tf_op jit(solution)/shard_map/all_to_all | solution.py:513
  70.3 1.9 %copy-done.1 = f32[64,96,128]{2,1,0:T(8,128)S(1)} copy-done((f32[64,96,128]{2,1,0:T(8,128)S(1)}, f32[64,96,128]{2,1,0:T(8,128)}, u32[]{:S(2)}) %copy-start.1) | copy-done | bytes 3145752
  72.2 2.2 %child_sums.1 = (f32[2,4,4,72,128]{4,3,2,1,0:T(8,128)}, f32[2,4,4,72,128]{4,3,2,1,0:T(8,128)}, f32[8,128]{1,0:T(8,128)S(1)}) custom-call(f32[256]{0:T(256)S(1)} %reshape.147.flags, f32[64,96,128]{2,1,0:T(8,128)S(1)} %copy-done.1, f32[8,128]{1,0:T(8,128)S(1)} %get-tuple-element.34.wait), custom_call_target="tpu_custom_call" | custom-call | bytes 4194304 | tf_op jit(solution)/shard_map/child_sums/pallas_call | solution.py:35
  74.4 4.1 %pack.5 = f32[64,128,128]{2,1,0:T(8,128)} custom-call(f32[16,128,1024]{2,1,0:T(8,128)} %bitcast.31, f32[8,128]{1,0:T(8,128)S(1)} %get-tuple-element.41.wait), custom_call_target="tpu_custom_call" | custom-call | bytes 8388608 | tf_op jit(solution)/shard_map/pack/pallas_call | solution.py:35
  78.5 30.2 %all-to-all-done.1.mine = f32[64,96,128]{2,1,0:T(8,128)S(1)} async-done(((f32[64,96,128]{2,1,0:T(8,128)}), f32[64,96,128]{2,1,0:T(8,128)S(1)}, u32[]{:S(2)}, u32[]{:S(2)}) %all-to-all-start.1) | async-done | bytes 3145760 | tf_op jit(solution)/shard_map/all_to_all | solution.py:513
  108.7 6.3 %all-to-all-start.2 = ((f32[64,128,128]{2,1,0:T(8,128)}), f32[64,128,128]{2,1,0:T(8,128)}, u32[]{:S(2)}, u32[]{:S(2)}) async-start(f32[64,128,128]{2,1,0:T(8,128)} %pack.5), calls=%async_computation.2 | async-start | bytes 8388608 | tf_op jit(solution)/shard_map/all_to_all | solution.py:513
  116.2 2.2 %collective-permute-start.1 = (f32[64,40,128]{2,1,0:T(8,128)}, f32[64,40,128]{2,1,0:T(8,128)}, u32[]{:S(2)}, u32[]{:S(2)}) collective-permute-start(f32[64,40,128]{2,1,0:T(8,128)} %slice.28), channel_id=1, source_target_pairs={{0,1},{1,0},{2,3},{3,2},{4,5},{5,4},{6,7},{7,6},{8,9},{9,8},{10,11... | collective-permute-start | bytes 3932168 | tf_op jit(solution)/shard_map/ppermute | solution.py:510
  118.6 2.9 %collective-permute-done.1 = f32[64,40,128]{2,1,0:T(8,128)} collective-permute-done((f32[64,40,128]{2,1,0:T(8,128)}, f32[64,40,128]{2,1,0:T(8,128)}, u32[]{:S(2)}, u32[]{:S(2)}) %collective-permute-start.1) | collective-permute-done | bytes 1310752 | tf_op jit(solution)/shard_map/ppermute | solution.py:510
  121.4 3.8 %assemble.1 = (f32[24,128,128]{2,1,0:T(8,128)}, f32[128,128]{1,0:T(8,128)S(1)}, f32[2,4,4,64,128]{4,3,2,1,0:T(8,128)}, f32[2,4,4,64,128]{4,3,2,1,0:T(8,128)}) custom-call(s32[1]{0:T(128)} %bitcast.core, f32[256]{0:T(256)S(1)} %reshape.147.flags, f32[6144,128]{1,0:T(8,128)S(1)} %bitcast.28, f32[64,96,128]{2,1,0:T(8,128)S(1)} %all-to-all-done.1.mine, ...), custom_call_target="tpu_custom_call" | custom-call | bytes 3276800 | tf_op jit(solution)/shard_map/assemble/pallas_call | solution.py:35
  126.1 11.7 %cholesky.16 = f32[128,128]{1,0:T(8,128)S(1)} custom-call(f32[128,128]{1,0:T(8,128)S(1)} %fusion.2), custom_call_target="Cholesky" | custom-call | tf_op jit(solution)/shard_map/jit(cholesky)/cholesky | solution.py:546
  139.3 9.8 %custom-call.6 = f32[1,128,128]{1,2,0:T(8,128)S(1)} custom-call(f32[1,128,128]{2,1,0:T(8,128)S(1)} %get-tuple-element.43), custom_call_target="InvertDiagBlocksLowerTriangular" | custom-call | tf_op jit(solution)/shard_map/triangular_solve | solution.py:547
  149.1 2.8 %fusion.solved = f32[3072,128]{1,0:T(8,128)S(1)} fusion(f32[3072,128]{1,0:T(8,128)} %bitcast.33, f32[1,128,128]{1,2,0:T(8,128)S(1)} %custom-call.6), kind=kOutput, calls=%fused_computation.2 | convolution fusion | flops 603979776 | bytes 3211264 | tf_op jit(solution)/shard_map/triangular_solve | solution.py:547
  152.9 10.4 %base.1 = (f32[8,256,1024]{2,1,0:T(8,128)}, f32[8,128,1024]{2,1,0:T(8,128)}, f32[8,128]{1,0:T(8,128)S(1)}) custom-call(s32[3]{0:T(128)S(1)} %add_convert_fusion.edge, f32[16,128,1024]{2,1,0:T(8,128)} %bitcast.32, f32[3072,128]{1,0:T(8,128)S(1)} %fusion.solved, f32[128,128]{1,0:T(8,128)S(1)} %get-tuple-element.44.head, ...), custom_call_target="tpu_custom_call" | custom-call | bytes 16777216 | tf_op jit(solution)/shard_map/base/pallas_call | solution.py:35
  163.3 2.2 %all-to-all-done.2.recv = f32[64,128,128]{2,1,0:T(8,128)} async-done(((f32[64,128,128]{2,1,0:T(8,128)}), f32[64,128,128]{2,1,0:T(8,128)}, u32[]{:S(2)}, u32[]{:S(2)}) %all-to-all-start.2) | async-done | bytes 4194336 | tf_op jit(solution)/shard_map/all_to_all | solution.py:513
  165.5 2.9 %late_sums.1 = f32[2,4,4,128,128]{4,3,2,1,0:T(8,128)S(1)} custom-call(f32[256]{0:T(256)S(1)} %reshape.148.flags, f32[64,128,128]{2,1,0:T(8,128)} %all-to-all-done.2.recv, f32[8,128]{1,0:T(8,128)S(1)} %get-tuple-element.42.wait), custom_call_target="tpu_custom_call" | custom-call | bytes 6291456 | tf_op jit(solution)/shard_map/late_sums/pallas_call | solution.py:35
  168.4 3.7 %collective-permute-start.4 = (f32[2,4,4,128,128]{4,3,2,1,0:T(8,128)S(1)}, f32[2,4,4,128,128]{4,3,2,1,0:T(8,128)S(1)}, u32[]{:S(2)}, u32[]{:S(2)}) collective-permute-start(f32[2,4,4,128,128]{4,3,2,1,0:T(8,128)S(1)} %late_sums.1), channel_id=1, source_target_pairs={{0,1},{1,0},{2,3},{3,2},{4,5},{5,4},{6,7},{7,6},{8,9},{9,8},{10,11... | collective-permute-start | bytes 6291464 | tf_op jit(solution)/shard_map/ppermute | solution.py:510
  172.2 4.3 %add_own.1.rest = f32[8,128,1024]{2,1,0:T(8,128)S(1)} custom-call(s32[1]{0:T(128)} %bitcast.core, f32[256]{0:T(256)S(1)} %reshape.148.flags, f32[8,128,1024]{2,1,0:T(8,128)} %get-tuple-element.40.rest, f32[64,128,128]{2,1,0:T(8,128)} %all-to-all-done.2.recv), custom_call_target="tpu_custom_call" | custom-call | bytes 12582912 | tf_op jit(solution)/shard_map/add_own/pallas_call | solution.py:35
  176.5 2.1 %add_late.1 = f32[8,256,1024]{2,1,0:T(8,128)} custom-call(s32[1]{0:T(128)} %bitcast.core, f32[8,256,1024]{2,1,0:T(8,128)} %get-tuple-element.39.before, f32[8,128,1024]{2,1,0:T(8,128)S(1)} %add_own.1.rest, f32[2,4,4,128,128]{4,3,2,1,0:T(8,128)S(1)} %collective-permute-done.4.sib), custom_call_target="tpu_custom_call", output_to_operand_aliasing={{}: (1, {})} | custom-call | bytes 12582912 | tf_op jit(solution)/shard_map/add_late/pallas_call | solution.py:35
  (50 shorter events, 10.3 us)
Async XLA Ops:
  2.5 4.9 %collective-permute-start = (f32[64,32,128]{2,1,0:T(8,128)S(1)}, f32[64,32,128]{2,1,0:T(8,128)S(1)}, u32[]{:S(2)}, u32[]{:S(2)}) collective-permute-start(f32[64,32,128]{2,1,0:T(8,128)S(1)} %get-tuple-element.28), channel_id=1, source_target_pairs={{0,1},{8,9},{16,17},{24,25},{32,33},{40,41},{48,49},{56,57},{64,65... | collective-permute-start | bytes 3145736 | tf_op jit(solution)/shard_map/ppermute | solution.py:532
  3.8 3.6 %copy-start.2 = (s32[4,64]{1,0:T(4,128)S(1)}, s32[4,64]{1,0:T(4,128)}, u32[]{:S(2)}) copy-start(s32[4,64]{1,0:T(4,128)} %child_map.1) | copy-start | bytes 3076
  9.4 51.6 %all-to-all-start = ((f32[64,96,128]{2,1,0:T(8,128)}), f32[64,96,128]{2,1,0:T(8,128)S(1)}, u32[]{:S(2)}, u32[]{:S(2)}) async-start(f32[64,96,128]{2,1,0:T(8,128)} %get-tuple-element.29), calls=%async_computation | async-start | bytes 6291456 | tf_op jit(solution)/shard_map/all_to_all | solution.py:513
  61.0 2.1 %copy-start = (f32[64,96,128]{2,1,0:T(8,128)}, f32[64,96,128]{2,1,0:T(8,128)S(1)}, u32[]{:S(2)}) copy-start(f32[64,96,128]{2,1,0:T(8,128)S(1)} %all-to-all-done.recv) | copy-start | bytes 9437188
  63.1 45.6 %all-to-all-start.1 = ((f32[64,96,128]{2,1,0:T(8,128)}), f32[64,96,128]{2,1,0:T(8,128)S(1)}, u32[]{:S(2)}, u32[]{:S(2)}) async-start(f32[64,96,128]{2,1,0:T(8,128)} %get-tuple-element.31), calls=%async_computation.1 | async-start | bytes 6291456 | tf_op jit(solution)/shard_map/all_to_all | solution.py:513
  70.3 1.9 %copy-start.1 = (f32[64,96,128]{2,1,0:T(8,128)S(1)}, f32[64,96,128]{2,1,0:T(8,128)}, u32[]{:S(2)}) copy-start(f32[64,96,128]{2,1,0:T(8,128)} %copy-done) | copy-start | bytes 9437188
  108.7 56.8 %all-to-all-start.2 = ((f32[64,128,128]{2,1,0:T(8,128)}), f32[64,128,128]{2,1,0:T(8,128)}, u32[]{:S(2)}, u32[]{:S(2)}) async-start(f32[64,128,128]{2,1,0:T(8,128)} %pack.5), calls=%async_computation.2 | async-start | bytes 8388608 | tf_op jit(solution)/shard_map/all_to_all | solution.py:513
  116.2 5.2 %collective-permute-start.1 = (f32[64,40,128]{2,1,0:T(8,128)}, f32[64,40,128]{2,1,0:T(8,128)}, u32[]{:S(2)}, u32[]{:S(2)}) collective-permute-start(f32[64,40,128]{2,1,0:T(8,128)} %slice.28), channel_id=1, source_target_pairs={{0,1},{1,0},{2,3},{3,2},{4,5},{5,4},{6,7},{7,6},{8,9},{9,8},{10,11... | collective-permute-start | bytes 3932168 | tf_op jit(solution)/shard_map/ppermute | solution.py:510
  118.4 33.5 %collective-permute-start.2 = (f32[2,4,4,72,128]{4,3,2,1,0:T(8,128)}, f32[2,4,4,72,128]{4,3,2,1,0:T(8,128)}, u32[]{:S(2)}, u32[]{:S(2)}) collective-permute-start(f32[2,4,4,72,128]{4,3,2,1,0:T(8,128)} %get-tuple-element.36), channel_id=1, source_target_pairs={{0,1},{1,0},{2,3},{3,2},{4,5},{5,4},{6,7},{7,6},{8,9},{9,8},{10,11... | collective-permute-start | bytes 3538952 | tf_op jit(solution)/shard_map/ppermute | solution.py:510
  125.3 26.7 %collective-permute-start.3 = (f32[2,4,4,64,128]{4,3,2,1,0:T(8,128)}, f32[2,4,4,64,128]{4,3,2,1,0:T(8,128)S(1)}, u32[]{:S(2)}, u32[]{:S(2)}) collective-permute-start(f32[2,4,4,64,128]{4,3,2,1,0:T(8,128)} %get-tuple-element.38), channel_id=1, source_target_pairs={{0,1},{1,0},{2,3},{3,2},{4,5},{5,4},{6,7},{7,6},{8,9},{9,8},{10,11... | collective-permute-start | bytes 3145736 | tf_op jit(solution)/shard_map/ppermute | solution.py:510
  151.9 1.0 copy-start.3
  168.4 8.0 %collective-permute-start.4 = (f32[2,4,4,128,128]{4,3,2,1,0:T(8,128)S(1)}, f32[2,4,4,128,128]{4,3,2,1,0:T(8,128)S(1)}, u32[]{:S(2)}, u32[]{:S(2)}) collective-permute-start(f32[2,4,4,128,128]{4,3,2,1,0:T(8,128)S(1)} %late_sums.1), channel_id=1, source_target_pairs={{0,1},{1,0},{2,3},{3,2},{4,5},{5,4},{6,7},{7,6},{8,9},{9,8},{10,11... | collective-permute-start | bytes 6291464 | tf_op jit(solution)/shard_map/ppermute | solution.py:510

commit v4 on v3

--- a/solution.py
+++ b/solution.py
@@ -51,29 +51,38 @@
     rows = updates.shape[0]
     half = bs // 2
 
+    cuts = 4
+    some = half // cuts
+
     def lift(updates, front, low, high, token, ucol, fcol, sems):
-        copies = [
-            pltpu.make_async_copy(whole.at[:, pl.ds(0, bs)], part, sems.at[i])
-            for i, (whole, part) in enumerate(((updates, ucol), (front, fcol)))
-        ]
-        for copy in copies:
-            copy.start()
+        def read(i, cut, core):
+            whole, part = ((updates, ucol), (front, fcol))[i]
+            here = pl.ds(core * half + cut * some, some)
+            return pltpu.make_async_copy(
+                whole.at[:, here, pl.ds(0, bs)], part.reshape(17, bs, bs).at[pl.ds(0, 16), here], sems.at[i, cut, core]
+            )
+
+        pieces = [(i, cut, core) for cut in range(cuts) for i in range(2) for core in range(2)]
+        for piece in pieces:
+            read(*piece).start()
         token[...] = jnp.zeros_like(token)
-        for at, (copy, part) in enumerate(zip(copies, (ucol, fcol))):
-            copy.wait()
-
-            def one(chip, carry):
-                low[chip, 16 * at:16 * at + 16] = part[pl.ds(chip, 16, stride=bs), :]
-                high[chip, 16 * at:16 * at + 16] = part[pl.ds(half + chip, 16, stride=bs), :]
+        for i, cut, core in pieces:
+            read(i, cut, core).wait()
+            part, out = (ucol, fcol)[i], (low, high)[core]
+
+            def one(n, carry):
+                chip = cut * some + n
+                out[chip, 16 * i:16 * i + 16] = part[pl.ds(core * half + chip, 16, stride=bs), :]
                 return carry
 
-            lax.fori_loop(0, half, one, 0, unroll=8)
+            lax.fori_loop(0, some, one, 0, unroll=8)
 
     share = shape(half, 32, bs)
+    blocks = (16, bs, updates.shape[1])
     return call(
         lift, (share, share, TOKEN), [HBM, HBM], (VMEM,) * 3, "lift", 16 * rows * bs,
-        [pltpu.VMEM((rows, bs), F32), pltpu.VMEM((rows, bs), F32), pltpu.SemaphoreType.DMA((2,))],
-    )(updates, front)
+        [pltpu.VMEM((rows + bs, bs), F32)] * 2 + [pltpu.SemaphoreType.DMA((2, cuts, 2))],
+    )(updates.reshape(blocks), front.reshape(blocks))
 
 
 def run_pack(blocks, wait, gi, at, rows, extra, ends=False):
@@ -120,7 +129,7 @@
 def run_put_rows(child_map, ends, load, low, other, rows):
     bs = low.shape[-1]
 
-    def put_rows(child_map, ends, load, low, other, out, token, region, sem):
+    def put_rows(child_map, ends, load, low, other, out, token, region, sems):
         y, zh, x, zl, t = (lax.axis_index(a) for a in ALL)
         me, col_pair = 2 * y + zh, 2 * x + zl
         token[...] = jnp.zeros_like(token)
@@ -129,26 +138,30 @@
             def _():
                 region[...] = part[...]
 
-        @pl.when((col_pair == 0) & (child_map[me // 4, 0] // 8 % 2 == 0))
-        def _():
-            for gi in range(2):
-                group = 2 * (me % 4) + gi
-                up = child_map[me // 4, 8 * group + me] // 8 % 2
-                to, of = pl.ds(16 + 8 * up + group, 1), pl.ds(8 * gi + me, 1)
-                for at in range(64):
-                    region[at, to, :] += region[at, of, :]
-
+        adds = (col_pair == 0) & (child_map[me // 4, 0] // 8 % 2 == 0)
         slot = pl.ds(jnp.where(col_pair == 4, slot_of(0, 4), slot_of(me, 0)), 1)
+        copies = []
         for j in range(8):
+            @pl.when(adds)
+            def _():
+                for gi in range(2):
+                    group = 2 * (me % 4) + gi
+                    up = child_map[me // 4, 8 * group + me] // 8 % 2
+                    to, of = pl.ds(16 + 8 * up + group, 1), pl.ds(8 * gi + me, 1)
+                    for at in range(8 * j, 8 * j + 8):
+                        region[at, to, :] += region[at, of, :]
+
             for jc in range(8):
                 region[8 * j + jc, slot, :] = ends[j, 7:8, jc * bs:(jc + 1) * bs]
-        copy = pltpu.make_async_copy(region, out.at[:, pl.ds(rows, 32)], sem)
-        copy.start()
-        copy.wait()
+            some = pl.ds(8 * j, 8)
+            copies.append(pltpu.make_async_copy(region.at[some], out.at[some, pl.ds(rows, 32)], sems.at[j]))
+            copies[-1].start()
+        for copy in copies:
+            copy.wait()
 
     return call(
         put_rows, (shape(*load.shape), TOKEN), [SMEM, VMEM, HBM, VMEM, VMEM], (HBM, VMEM), "put_rows", 8 * other.size,
-        [pltpu.VMEM(low.shape, F32), pltpu.SemaphoreType.DMA], aliases={2: 0},
+        [pltpu.VMEM(low.shape, F32), pltpu.SemaphoreType.DMA((8,))], aliases={2: 0},
     )(child_map, ends, load, low, other)
 
 
@@ -184,7 +197,7 @@
     return call(
         sum_rows, (shape(*load.shape), TOKEN), [VMEM, VMEM, VMEM, HBM], (HBM, VMEM), "sum_rows", 64 * 40 * bs * 8,
         [
-            pltpu.VMEM((128, bs), F32), pltpu.VMEM((8, 16, bs), F32), pltpu.VMEM((64, 40, bs), F32),
+            pltpu.VMEM((136, bs), F32), pltpu.VMEM((8, 16, bs), F32), pltpu.VMEM((64, 40, bs), F32),
             pltpu.SemaphoreType.DMA((8,)),
         ],
         aliases={3: 0},
@@ -263,29 +276,41 @@
     chips, width, bs = mine.shape
     half = bs // 2
 
-    def assemble(core, flags, flat, mine, other, slabs, corner, own, sib, out, sem, *held):
+    wide = width - first + 8
+
+    def assemble(core, flags, mine, other, slabs, corner, own, sib, here, there, out, sems, *held):
         t = core[0]
+        copies = [
+            pltpu.make_async_copy(
+                mine.at[:, pl.ds(first - 8, wide)], here.reshape(chips + 1, wide, bs).at[pl.ds(0, chips)], sems.at[0]
+            ),
+            pltpu.make_async_copy(other, there.reshape(chips + 1, wide, bs).at[pl.ds(0, chips)], sems.at[1]),
+        ]
+        for copy in copies:
+            copy.start()
         finish = child_sums(flags, mine, (own, sib), held[:2], held[2], first)
-        for who, (part, span, at) in enumerate(((flat, width, first), (other, 40, 8))):
+        for who, (copy, part) in enumerate(zip(copies, (here, there))):
+            copy.wait()
             rows_at = pl.multiple_of(half * (t if who == 0 else 1 - t), half)
             for s in range(25):
-                start = at + s if s < 16 else at + s + 8 * t if s < 24 else at - 1
-                rows = part[pl.ds(start, half, stride=span), :]
+                start = 8 + s if s < 16 else 8 + s + 8 * t if s < 24 else 7
+                rows = part[pl.ds(start, half, stride=wide), :]
                 if s < 24:
                     out[s, pl.ds(rows_at, half)] = rows
                 else:
                     corner[pl.ds(rows_at, half)] = rows
-        copy = pltpu.make_async_copy(out, slabs, sem)
+        copy = pltpu.make_async_copy(out, slabs, sems.at[2])
         copy.start()
         finish()
         copy.wait()
 
     part = shape(2, 4, 4, first, bs)
     return call(
-        assemble, (shape(24, bs, bs), shape(bs, bs), part, part), [SMEM, SMEM, VMEM, VMEM, VMEM], (HBM, VMEM, HBM, HBM),
+        assemble, (shape(24, bs, bs), shape(bs, bs), part, part), [SMEM, SMEM, VMEM, HBM], (HBM, VMEM, HBM, HBM),
         "assemble", 200 * bs * bs,
-        [pltpu.VMEM((24, bs, bs), F32), pltpu.SemaphoreType.DMA] + sums_scratch(first, bs),
-    )(core, flags, mine.reshape(chips * width, bs), mine, other.reshape(chips * 40, bs))
+        [pltpu.VMEM(((chips + 1) * wide, bs), F32)] * 2 + [pltpu.VMEM((24, bs, bs), F32), pltpu.SemaphoreType.DMA((3,))]
+        + sums_scratch(first, bs),
+    )(core, flags, mine, other)
 
 
 def split(a):

time: 179 us -> 179 us (level)
  transfers between devices with their start and end apart: 8 -> 8, of which waited for: 5 -> 4; matrix products, arithmetic and copies ran while one was open for 16% -> 16% of each run, Pallas kernels for 17% -> 18%
where the time goes in v4:
time: 179 us; the launch traced here: 178 us
  waiting for transfers between devices  72.7 us (41%)
  Pallas kernels  42.8 us (24%)
  starting transfers between devices  30.8 us (17%)
  other arithmetic  23.5 us (13%)
  local copies, waits for them, and re-layouts  5.02 us (3%)
  matrix products  2.81 us (2%)
    all_to_all x3, waiting for transfers between devices, send(): return lax.all_to_all(load, CHIP, 0, 0, tiled=True)  68.7 us
    pallas_call x12, Pallas kernels, placed(): run(*(pltpu.with_memory_space_constraint(arg, pltpu.HBM) if spec is HBM e...  42.8 us
    all_to_all x3, starting transfers between devices, send(): return lax.all_to_all(load, CHIP, 0, 0, tiled=True)  23.9 us
    another operation x3, other arithmetic, body(): head = jnp.linalg.cholesky(corner)  12.4 us
    another operation x2, other arithmetic, body(): lax.linalg.triangular_solve(head, slabs.reshape(24 * bs, bs), left_side=F...  10.4 us
    ppermute x4, starting transfers between devices, swap(): return lax.ppermute(a, 'core', CORE_SWAP)  5.56 us
  transfers between devices with their start and end apart: 8, of which 4 were waited for; matrix products, arithmetic and copies ran while one was open for 16% of the time, Pallas kernels for 18%

profile of v4, /device:TPU:1, one launch (start us, length us, event | category | flops | bytes accessed | tf_op | source)
XLA Modules:
  0.0 178.1 jit_solution(7694362801666673770)
XLA Ops:
  0.0 2.4 %lift.1 = (f32[64,32,128]{2,1,0:T(8,128)S(1)}, f32[64,32,128]{2,1,0:T(8,128)S(1)}, f32[8,128]{1,0:T(8,128)S(1)}) custom-call(f32[16,128,1024]{2,1,0:T(8,128)} %bitcast.26, f32[16,128,1024]{2,1,0:T(8,128)} %bitcast.30), custom_call_target="tpu_custom_call" | custom-call | bytes 4194304 | tf_op jit(solution)/shard_map/lift/pallas_call | solution.py:35
  2.4 1.3 collective-permute-start
  3.7 2.9 %pack.3 = (f32[64,96,128]{2,1,0:T(8,128)}, f32[8,8,1024]{2,1,0:T(8,128)S(1)}) custom-call(f32[16,128,1024]{2,1,0:T(8,128)} %bitcast.27, f32[8,128]{1,0:T(8,128)S(1)} %get-tuple-element.24.wait), custom_call_target="tpu_custom_call" | custom-call | bytes 4194304 | tf_op jit(solution)/shard_map/pack/pallas_call | solution.py:35
  7.3 1.9 %put_rows.1 = (f32[64,96,128]{2,1,0:T(8,128)}, f32[8,128]{1,0:T(8,128)S(1)}) custom-call(s32[4,64]{1,0:T(4,128)S(1)} %copy-done, f32[8,8,1024]{2,1,0:T(8,128)S(1)} %get-tuple-element.25.ends, f32[64,96,128]{2,1,0:T(8,128)} %get-tuple-element.26.load, f32[64,32,128]{2,1,0:T(8,128)S(1)} %get-tuple-element.27.low, ...), custom_call_target="tpu_custom_call", output_to_operand_aliasing={{0}: (2, {})} | custom-call | bytes 2097152 | tf_op jit(solution)/shard_map/put_rows/pallas_call | solution.py:35
  9.2 11.4 %all-to-all-start = ((f32[64,96,128]{2,1,0:T(8,128)}), f32[64,96,128]{2,1,0:T(8,128)S(1)}, u32[]{:S(2)}, u32[]{:S(2)}) async-start(f32[64,96,128]{2,1,0:T(8,128)} %get-tuple-element.29), calls=%async_computation | async-start | bytes 6291456 | tf_op jit(solution)/shard_map/all_to_all | solution.py:538
  21.1 2.9 %pack.4.load = f32[64,96,128]{2,1,0:T(8,128)} custom-call(f32[16,128,1024]{2,1,0:T(8,128)} %bitcast.28, f32[8,128]{1,0:T(8,128)S(1)} %get-tuple-element.30.wait), custom_call_target="tpu_custom_call" | custom-call | bytes 4194304 | tf_op jit(solution)/shard_map/pack/pallas_call | solution.py:35
  24.1 36.9 %all-to-all-done.recv = f32[64,96,128]{2,1,0:T(8,128)S(1)} async-done(((f32[64,96,128]{2,1,0:T(8,128)}), f32[64,96,128]{2,1,0:T(8,128)S(1)}, u32[]{:S(2)}, u32[]{:S(2)}) %all-to-all-start) | async-done | bytes 3145760 | tf_op jit(solution)/shard_map/all_to_all | solution.py:538
  62.3 6.2 %all-to-all-start.1 = ((f32[64,96,128]{2,1,0:T(8,128)}), f32[64,96,128]{2,1,0:T(8,128)}, u32[]{:S(2)}, u32[]{:S(2)}) async-start(f32[64,96,128]{2,1,0:T(8,128)} %get-tuple-element.31), calls=%async_computation.1 | async-start | bytes 6291456 | tf_op jit(solution)/shard_map/all_to_all | solution.py:538
  69.8 2.2 %child_sums.1 = (f32[2,4,4,72,128]{4,3,2,1,0:T(8,128)}, f32[2,4,4,72,128]{4,3,2,1,0:T(8,128)}, f32[8,128]{1,0:T(8,128)S(1)}) custom-call(f32[256]{0:T(256)S(1)} %reshape.141.flags, f32[64,96,128]{2,1,0:T(8,128)S(1)} %all-to-all-done.recv, f32[8,128]{1,0:T(8,128)S(1)} %get-tuple-element.34.wait), custom_call_target="tpu_custom_call" | custom-call | bytes 4194304 | tf_op jit(solution)/shard_map/child_sums/pallas_call | solution.py:35
  72.0 4.1 %pack.5 = f32[64,128,128]{2,1,0:T(8,128)} custom-call(f32[16,128,1024]{2,1,0:T(8,128)} %bitcast.29, f32[8,128]{1,0:T(8,128)S(1)} %get-tuple-element.41.wait), custom_call_target="tpu_custom_call" | custom-call | bytes 8388608 | tf_op jit(solution)/shard_map/pack/pallas_call | solution.py:35
  76.1 31.8 %all-to-all-done.1.mine = f32[64,96,128]{2,1,0:T(8,128)} async-done(((f32[64,96,128]{2,1,0:T(8,128)}), f32[64,96,128]{2,1,0:T(8,128)}, u32[]{:S(2)}, u32[]{:S(2)}) %all-to-all-start.1) | async-done | bytes 3145760 | tf_op jit(solution)/shard_map/all_to_all | solution.py:538
  107.9 6.3 %all-to-all-start.2 = ((f32[64,128,128]{2,1,0:T(8,128)}), f32[64,128,128]{2,1,0:T(8,128)}, u32[]{:S(2)}, u32[]{:S(2)}) async-start(f32[64,128,128]{2,1,0:T(8,128)} %pack.5), calls=%async_computation.2 | async-start | bytes 8388608 | tf_op jit(solution)/shard_map/all_to_all | solution.py:538
  114.3 1.4 slice.28
  115.7 2.3 %collective-permute-start.1 = (f32[64,40,128]{2,1,0:T(8,128)S(1)}, f32[64,40,128]{2,1,0:T(8,128)S(1)}, u32[]{:S(2)}, u32[]{:S(2)}) collective-permute-start(f32[64,40,128]{2,1,0:T(8,128)S(1)} %slice.28), channel_id=1, source_target_pairs={{0,1},{1,0},{2,3},{3,2},{4,5},{5,4},{6,7},{7,6},{8,9},{9,8},{10,11... | collective-permute-start | bytes 3932168 | tf_op jit(solution)/shard_map/ppermute | solution.py:535
  118.2 3.4 %collective-permute-done.1.other = f32[64,40,128]{2,1,0:T(8,128)S(1)} collective-permute-done((f32[64,40,128]{2,1,0:T(8,128)S(1)}, f32[64,40,128]{2,1,0:T(8,128)S(1)}, u32[]{:S(2)}, u32[]{:S(2)}) %collective-permute-start.1) | collective-permute-done | bytes 1310752 | tf_op jit(solution)/shard_map/ppermute | solution.py:535
  122.7 5.3 %assemble.1 = (f32[24,128,128]{2,1,0:T(8,128)}, f32[128,128]{1,0:T(8,128)S(1)}, f32[2,4,4,64,128]{4,3,2,1,0:T(8,128)}, f32[2,4,4,64,128]{4,3,2,1,0:T(8,128)}) custom-call(s32[1]{0:T(128)} %bitcast.core, f32[256]{0:T(256)S(1)} %reshape.141.flags, f32[64,96,128]{2,1,0:T(8,128)} %all-to-all-done.1.mine, f32[64,40,128]{2,1,0:T(8,128)} %copy-done.1), custom_call_target="tpu_custom_call" | custom-call | bytes 3276800 | tf_op jit(solution)/shard_map/assemble/pallas_call | solution.py:35
  128.9 11.7 %cholesky.16 = f32[128,128]{1,0:T(8,128)S(1)} custom-call(f32[128,128]{1,0:T(8,128)S(1)} %fusion.2), custom_call_target="Cholesky" | custom-call | tf_op jit(solution)/shard_map/jit(cholesky)/cholesky | solution.py:571
  141.9 9.8 %custom-call.6 = f32[1,128,128]{1,2,0:T(8,128)S(1)} custom-call(f32[1,128,128]{2,1,0:T(8,128)S(1)} %get-tuple-element.43), custom_call_target="InvertDiagBlocksLowerTriangular" | custom-call | tf_op jit(solution)/shard_map/triangular_solve | solution.py:572
  151.7 2.8 %fusion.solved = f32[3072,128]{1,0:T(8,128)S(1)} fusion(f32[3072,128]{1,0:T(8,128)} %bitcast.32, f32[1,128,128]{1,2,0:T(8,128)S(1)} %custom-call.6), kind=kOutput, calls=%fused_computation.2 | convolution fusion | flops 603979776 | bytes 3211264 | tf_op jit(solution)/shard_map/triangular_solve | solution.py:572
  155.6 10.4 %base.1 = (f32[8,256,1024]{2,1,0:T(8,128)}, f32[8,128,1024]{2,1,0:T(8,128)}, f32[8,128]{1,0:T(8,128)S(1)}) custom-call(s32[3]{0:T(128)S(1)} %add_convert_fusion.edge, f32[16,128,1024]{2,1,0:T(8,128)} %bitcast.31, f32[3072,128]{1,0:T(8,128)S(1)} %fusion.solved, f32[128,128]{1,0:T(8,128)S(1)} %get-tuple-element.44.head, ...), custom_call_target="tpu_custom_call" | custom-call | bytes 16777216 | tf_op jit(solution)/shard_map/base/pallas_call | solution.py:35
  166.0 2.9 %late_sums.1 = f32[2,4,4,128,128]{4,3,2,1,0:T(8,128)S(1)} custom-call(f32[256]{0:T(256)S(1)} %reshape.142.flags, f32[64,128,128]{2,1,0:T(8,128)} %all-to-all-done.2.recv, f32[8,128]{1,0:T(8,128)S(1)} %get-tuple-element.42.wait), custom_call_target="tpu_custom_call" | custom-call | bytes 6291456 | tf_op jit(solution)/shard_map/late_sums/pallas_call | solution.py:35
  168.9 2.5 %collective-permute-start.4 = (f32[2,4,4,128,128]{4,3,2,1,0:T(8,128)S(1)}, f32[2,4,4,128,128]{4,3,2,1,0:T(8,128)S(1)}, u32[]{:S(2)}, u32[]{:S(2)}) collective-permute-start(f32[2,4,4,128,128]{4,3,2,1,0:T(8,128)S(1)} %late_sums.1), channel_id=1, source_target_pairs={{0,1},{1,0},{2,3},{3,2},{4,5},{5,4},{6,7},{7,6},{8,9},{9,8},{10,11... | collective-permute-start | bytes 6291464 | tf_op jit(solution)/shard_map/ppermute | solution.py:535
  171.5 4.3 %add_own.1.rest = f32[8,128,1024]{2,1,0:T(8,128)S(1)} custom-call(s32[1]{0:T(128)} %bitcast.core, f32[256]{0:T(256)S(1)} %reshape.142.flags, f32[8,128,1024]{2,1,0:T(8,128)} %get-tuple-element.40.rest, f32[64,128,128]{2,1,0:T(8,128)} %all-to-all-done.2.recv), custom_call_target="tpu_custom_call" | custom-call | bytes 12582912 | tf_op jit(solution)/shard_map/add_own/pallas_call | solution.py:35
  175.8 2.1 %add_late.1 = f32[8,256,1024]{2,1,0:T(8,128)} custom-call(s32[1]{0:T(128)} %bitcast.core, f32[8,256,1024]{2,1,0:T(8,128)} %get-tuple-element.39.before, f32[8,128,1024]{2,1,0:T(8,128)S(1)} %add_own.1.rest, f32[2,4,4,128,128]{4,3,2,1,0:T(8,128)S(1)} %collective-permute-done.4.sib), custom_call_target="tpu_custom_call", output_to_operand_aliasing={{}: (1, {})} | custom-call | bytes 12582912 | tf_op jit(solution)/shard_map/add_late/pallas_call | solution.py:35
  (48 shorter events, 8.3 us)
Async XLA Ops:
  2.4 4.9 %collective-permute-start = (f32[64,32,128]{2,1,0:T(8,128)S(1)}, f32[64,32,128]{2,1,0:T(8,128)S(1)}, u32[]{:S(2)}, u32[]{:S(2)}) collective-permute-start(f32[64,32,128]{2,1,0:T(8,128)S(1)} %get-tuple-element.28), channel_id=1, source_target_pairs={{0,1},{8,9},{16,17},{24,25},{32,33},{40,41},{48,49},{56,57},{64,65... | collective-permute-start | bytes 3145736 | tf_op jit(solution)/shard_map/ppermute | solution.py:557
  3.7 3.6 %copy-start = (s32[4,64]{1,0:T(4,128)S(1)}, s32[4,64]{1,0:T(4,128)}, u32[]{:S(2)}) copy-start(s32[4,64]{1,0:T(4,128)} %child_map.1) | copy-start | bytes 3076
  9.2 51.8 %all-to-all-start = ((f32[64,96,128]{2,1,0:T(8,128)}), f32[64,96,128]{2,1,0:T(8,128)S(1)}, u32[]{:S(2)}, u32[]{:S(2)}) async-start(f32[64,96,128]{2,1,0:T(8,128)} %get-tuple-element.29), calls=%async_computation | async-start | bytes 6291456 | tf_op jit(solution)/shard_map/all_to_all | solution.py:538
  62.3 45.6 %all-to-all-start.1 = ((f32[64,96,128]{2,1,0:T(8,128)}), f32[64,96,128]{2,1,0:T(8,128)}, u32[]{:S(2)}, u32[]{:S(2)}) async-start(f32[64,96,128]{2,1,0:T(8,128)} %get-tuple-element.31), calls=%async_computation.1 | async-start | bytes 6291456 | tf_op jit(solution)/shard_map/all_to_all | solution.py:538
  107.9 58.1 %all-to-all-start.2 = ((f32[64,128,128]{2,1,0:T(8,128)}), f32[64,128,128]{2,1,0:T(8,128)}, u32[]{:S(2)}, u32[]{:S(2)}) async-start(f32[64,128,128]{2,1,0:T(8,128)} %pack.5), calls=%async_computation.2 | async-start | bytes 8388608 | tf_op jit(solution)/shard_map/all_to_all | solution.py:538
  115.7 5.9 %collective-permute-start.1 = (f32[64,40,128]{2,1,0:T(8,128)S(1)}, f32[64,40,128]{2,1,0:T(8,128)S(1)}, u32[]{:S(2)}, u32[]{:S(2)}) collective-permute-start(f32[64,40,128]{2,1,0:T(8,128)S(1)} %slice.28), channel_id=1, source_target_pairs={{0,1},{1,0},{2,3},{3,2},{4,5},{5,4},{6,7},{7,6},{8,9},{9,8},{10,11... | collective-permute-start | bytes 3932168 | tf_op jit(solution)/shard_map/ppermute | solution.py:535
  118.0 36.6 %collective-permute-start.2 = (f32[2,4,4,72,128]{4,3,2,1,0:T(8,128)}, f32[2,4,4,72,128]{4,3,2,1,0:T(8,128)}, u32[]{:S(2)}, u32[]{:S(2)}) collective-permute-start(f32[2,4,4,72,128]{4,3,2,1,0:T(8,128)} %get-tuple-element.36), channel_id=1, source_target_pairs={{0,1},{1,0},{2,3},{3,2},{4,5},{5,4},{6,7},{7,6},{8,9},{9,8},{10,11... | collective-permute-start | bytes 3538952 | tf_op jit(solution)/shard_map/ppermute | solution.py:535
  121.6 1.1 copy-start.1
  128.1 26.5 %collective-permute-start.3 = (f32[2,4,4,64,128]{4,3,2,1,0:T(8,128)}, f32[2,4,4,64,128]{4,3,2,1,0:T(8,128)S(1)}, u32[]{:S(2)}, u32[]{:S(2)}) collective-permute-start(f32[2,4,4,64,128]{4,3,2,1,0:T(8,128)} %get-tuple-element.38), channel_id=1, source_target_pairs={{0,1},{1,0},{2,3},{3,2},{4,5},{5,4},{6,7},{7,6},{8,9},{9,8},{10,11... | collective-permute-start | bytes 3145736 | tf_op jit(solution)/shard_map/ppermute | solution.py:535
  154.6 1.0 copy-start.2
  168.9 6.8 %collective-permute-start.4 = (f32[2,4,4,128,128]{4,3,2,1,0:T(8,128)S(1)}, f32[2,4,4,128,128]{4,3,2,1,0:T(8,128)S(1)}, u32[]{:S(2)}, u32[]{:S(2)}) collective-permute-start(f32[2,4,4,128,128]{4,3,2,1,0:T(8,128)S(1)} %late_sums.1), channel_id=1, source_target_pairs={{0,1},{1,0},{2,3},{3,2},{4,5},{5,4},{6,7},{7,6},{8,9},{9,8},{10,11... | collective-permute-start | bytes 6291464 | tf_op jit(solution)/shard_map/ppermute | solution.py:535

commit v5 on v4

--- a/solution.py
+++ b/solution.py
@@ -85,51 +85,65 @@
     )(updates.reshape(blocks), front.reshape(blocks))
 
 
-def run_pack(blocks, wait, gi, at, rows, extra, ends=False):
+def run_pack(blocks, wait, gi, at, rows, extra, child_map=None):
     bs = blocks.shape[1]
-
-    def pack(blocks, wait, out, *rest):
-        held, read_sems, write_sems, end_sem = rest[-4:]
+    more = child_map is not None
+
+    def pack(blocks, wait, *rest):
+        out = rest[1] if more else rest[0]
+        held, parted, read_sems, write_sems = rest[-4:]
 
         def read(j):
             return pltpu.make_async_copy(blocks.at[8 * gi + j, pl.ds(at, rows)], held.at[j], read_sems.at[j])
 
-        def write(j, jc):
-            lanes = pl.ds(jc * bs, bs)
-            return pltpu.make_async_copy(
-                held.at[j, :, lanes], out.at[8 * j + jc, pl.ds(0, rows)], write_sems.at[8 * j + jc]
-            )
+        def write(j):
+            some = pl.ds(8 * j, 8)
+            return pltpu.make_async_copy(parted.at[some], out.at[some, pl.ds(0, rows)], write_sems.at[j])
 
         for j in range(8):
             read(j).start()
-        if ends:
-            last = pltpu.make_async_copy(blocks.at[pl.ds(0, 8), pl.ds(bs - 8, 8)], rest[0], end_sem)
+        if more:
+            whole_map, _, ends, adds, entries, sems = rest[:6]
+            last = pltpu.make_async_copy(blocks.at[pl.ds(0, 8), pl.ds(bs - 8, 8)], ends, sems.at[0])
+            fetch = pltpu.make_async_copy(whole_map, entries, sems.at[1])
             last.start()
+            fetch.start()
         for j in range(8):
             read(j).wait()
             for jc in range(8):
-                write(j, jc).start()
-        if ends:
+                parted[8 * j + jc] = held[j, :, jc * bs:(jc + 1) * bs]
+            write(j).start()
+        if more:
+            y, zh, x, zl, _ = (lax.axis_index(a) for a in ALL)
+            me, col_pair = 2 * y + zh, 2 * x + zl
             last.wait()
+            fetch.wait()
+            live = (col_pair == 0) & (entries[me // 4, 0] // 8 % 2 == 0)
+            place = lax.broadcasted_iota(jnp.int32, (16, bs), 0)
+            for g in range(2):
+                group = 2 * (me % 4) + g
+                to = jnp.where(live, 8 * (entries[me // 4, 8 * group + me] // 8 % 2) + group, -1)
+                adds[g] = jnp.where(place == to, 1.0, 0.0)
         for j in range(8):
-            for jc in range(8):
-                write(j, jc).wait()
+            write(j).wait()
 
     load = shape(64, rows + extra, bs)
-    return call(
-        pack, (load, shape(8, 8, 8 * bs)) if ends else load, [HBM, VMEM], (HBM, VMEM) if ends else HBM, "pack",
-        512 * rows * bs,
-        [
-            pltpu.VMEM((8, rows, 8 * bs), F32), pltpu.SemaphoreType.DMA((8,)), pltpu.SemaphoreType.DMA((64,)),
-            pltpu.SemaphoreType.DMA,
-        ],
-    )(blocks, wait)
-
-
-def run_put_rows(child_map, ends, load, low, other, rows):
+    scratch = [
+        pltpu.VMEM((8, rows, 8 * bs), F32), pltpu.VMEM((64, rows, bs), F32), pltpu.SemaphoreType.DMA((8,)),
+        pltpu.SemaphoreType.DMA((8,)),
+    ]
+    if not more:
+        return call(pack, load, [HBM, VMEM], HBM, "pack", 512 * rows * bs, scratch)(blocks, wait)
+    return call(
+        pack, (load, shape(8, 8, 8 * bs), shape(2, 16, bs)), [HBM, VMEM, HBM], (HBM, VMEM, VMEM), "pack", 512 * rows * bs,
+        [pltpu.SMEM(child_map.shape, jnp.int32), pltpu.SemaphoreType.DMA((2,))] + scratch,
+    )(blocks, wait, child_map)
+
+
+def run_put_rows(adds, ends, load, low, other, rows):
     bs = low.shape[-1]
 
-    def put_rows(child_map, ends, load, low, other, out, token, region, sems):
+    def put_rows(adds, ends, load, low, other, out, token, region, sems):
         y, zh, x, zl, t = (lax.axis_index(a) for a in ALL)
         me, col_pair = 2 * y + zh, 2 * x + zl
         token[...] = jnp.zeros_like(token)
@@ -138,19 +152,15 @@
             def _():
                 region[...] = part[...]
 
-        adds = (col_pair == 0) & (child_map[me // 4, 0] // 8 % 2 == 0)
+        @pl.when(col_pair == 0)
+        def _():
+            for at in range(64):
+                own = [region[at, pl.ds(8 * g + me, 1), :] for g in range(2)]
+                region[at, 16:32] += adds[0] * own[0] + adds[1] * own[1]
+
         slot = pl.ds(jnp.where(col_pair == 4, slot_of(0, 4), slot_of(me, 0)), 1)
         copies = []
         for j in range(8):
-            @pl.when(adds)
-            def _():
-                for gi in range(2):
-                    group = 2 * (me % 4) + gi
-                    up = child_map[me // 4, 8 * group + me] // 8 % 2
-                    to, of = pl.ds(16 + 8 * up + group, 1), pl.ds(8 * gi + me, 1)
-                    for at in range(8 * j, 8 * j + 8):
-                        region[at, to, :] += region[at, of, :]
-
             for jc in range(8):
                 region[8 * j + jc, slot, :] = ends[j, 7:8, jc * bs:(jc + 1) * bs]
             some = pl.ds(8 * j, 8)
@@ -160,9 +170,9 @@
             copy.wait()
 
     return call(
-        put_rows, (shape(*load.shape), TOKEN), [SMEM, VMEM, HBM, VMEM, VMEM], (HBM, VMEM), "put_rows", 8 * other.size,
+        put_rows, (shape(*load.shape), TOKEN), [VMEM, VMEM, HBM, VMEM, VMEM], (HBM, VMEM), "put_rows", 8 * other.size,
         [pltpu.VMEM(low.shape, F32), pltpu.SemaphoreType.DMA((8,))], aliases={2: 0},
-    )(child_map, ends, load, low, other)
+    )(adds, ends, load, low, other)
 
 
 def run_sum_rows(marks, recv, ends, load, first):
@@ -427,7 +437,10 @@
     chips, bs, _ = recv.shape
     step = 32
 
-    def late_sums(flags, recv, wait, sib, held, sems):
+    def late_sums(all_flags, recv, wait, sib, flags, held, flag_sem, sems):
+        fetch = pltpu.make_async_copy(all_flags, flags, flag_sem)
+        fetch.start()
+
         def read(sr, h):
             some = pl.ds((4 * h + sr) * 8, 8)
             return pltpu.make_async_copy(recv.at[some], held.at[some], sems.at[2 * sr + h])
@@ -435,6 +448,7 @@
         for sr in range(4):
             for h in range(2):
                 read(sr, h).start()
+        fetch.wait()
         for sr in range(4):
             for h in range(2):
                 read(sr, h).wait()
@@ -450,16 +464,23 @@
             lax.fori_loop(0, bs // step, one, 0)
 
     return call(
-        late_sums, shape(2, 4, 4, bs, bs), [SMEM, HBM, VMEM], VMEM, "late_sums", 96 * bs * bs * 4,
-        [pltpu.VMEM((chips, bs, bs), F32), pltpu.SemaphoreType.DMA((8,))],
+        late_sums, shape(2, 4, 4, bs, bs), [HBM, HBM, VMEM], VMEM, "late_sums", 96 * bs * bs * 4,
+        [
+            pltpu.SMEM(flags.shape, F32), pltpu.VMEM((chips, bs, bs), F32), pltpu.SemaphoreType.DMA,
+            pltpu.SemaphoreType.DMA((8,)),
+        ],
     )(flags, recv, wait)
 
 
-def run_add_own(core, flags, rest, recv):
+def run_add_own(flags, rest, recv):
     blocks, bs, cols = rest.shape
     step = 32
 
-    def add_own(core, flags, rest, recv, out, held, sems, more):
+    def add_own(all_flags, rest, recv, out, flags, held, flag_sem, sems, more):
+        fetch = pltpu.make_async_copy(all_flags, flags, flag_sem)
+        fetch.start()
+        left = lax.axis_index("core") == 0
+
         def read(sr, h):
             some = pl.ds((4 * h + sr) * 8, 8)
             return pltpu.make_async_copy(recv.at[some], held.at[some], sems.at[2 * sr + h])
@@ -471,6 +492,7 @@
             for n in range(2):
                 read(sr, n).start()
                 base(4 * n + sr).start()
+        fetch.wait()
         for sr in range(4):
             for n in range(2):
                 read(sr, n).wait()
@@ -481,7 +503,7 @@
                 for scp in range(4):
                     sums = add_blocks(flags, held, sr, scp, here, (0,))
                     for up in range(2):
-                        two = spread(core[0] == 0, sums[up, 0], 0.0)
+                        two = spread(left, sums[up, 0], 0.0)
                         for lanes, add in zip(pair(scp, bs), two):
                             out[4 * up + sr, here, lanes] += add
                 return carry
@@ -489,16 +511,21 @@
             lax.fori_loop(0, bs // step, one, 0)
 
     return call(
-        add_own, shape(blocks, bs, cols), [SMEM, SMEM, HBM, HBM], VMEM, "add_own", blocks * bs * cols * 12,
-        [pltpu.VMEM(recv.shape, F32), pltpu.SemaphoreType.DMA((8,)), pltpu.SemaphoreType.DMA((8,))],
-    )(core, flags, rest, recv)
-
-
-def run_add_late(core, out, rest, sib):
+        add_own, shape(blocks, bs, cols), [HBM, HBM, HBM], VMEM, "add_own", blocks * bs * cols * 12,
+        [
+            pltpu.SMEM(flags.shape, F32), pltpu.VMEM(recv.shape, F32), pltpu.SemaphoreType.DMA,
+            pltpu.SemaphoreType.DMA((8,)), pltpu.SemaphoreType.DMA((8,)),
+        ],
+    )(flags, rest, recv)
+
+
+def run_add_late(out, rest, sib):
     blocks, bs, cols = rest.shape
     step = 32
 
-    def add_late(core, before, rest, sib, out, done, sems):
+    def add_late(before, rest, sib, out, done, sems):
+        left = lax.axis_index("core") == 0
+
         def write(i):
             return pltpu.make_async_copy(done.at[i], out.at[i, pl.ds(bs, bs)], sems.at[i])
 
@@ -507,7 +534,7 @@
             for at in range(0, bs, step):
                 here = slice(at, at + step)
                 for scp in range(4):
-                    for lanes, add in zip(pair(scp, bs), spread(core[0] == 0, 0.0, sib[up, sr, scp, here])):
+                    for lanes, add in zip(pair(scp, bs), spread(left, 0.0, sib[up, sr, scp, here])):
                         done[i, here, lanes] = rest[i, here, lanes] + add
             write(i).start()
             return carry
@@ -516,9 +543,9 @@
         lax.fori_loop(0, blocks, lambda i, c: (write(i).wait(), c)[1], 0)
 
     return call(
-        add_late, shape(*out.shape), [SMEM, HBM, VMEM, VMEM], HBM, "add_late", out.size * 6,
-        [pltpu.VMEM((blocks, bs, cols), F32), pltpu.SemaphoreType.DMA((blocks,))], aliases={1: 0},
-    )(core, out, rest, sib)
+        add_late, shape(*out.shape), [HBM, VMEM, VMEM], HBM, "add_late", out.size * 6,
+        [pltpu.VMEM((blocks, bs, cols), F32), pltpu.SemaphoreType.DMA((blocks,))], aliases={0: 0},
+    )(out, rest, sib)
 
 
 def body(front, updates, child_map):
@@ -555,8 +582,8 @@
 
     low, high, lifted = run_lift(updates, front, bs)
     other = lax.ppermute(high, ALL, [((r * 8 + q) * 2, (r * 8 + q) * 2 + 1) for r in range(8) for q in (0, 4)])
-    load0, ends = run_pack(blocks, lifted, 0, 0, half, 32, True)
-    load0, sent0 = run_put_rows(child_map, ends, load0, low, other, half)
+    load0, ends, adds = run_pack(blocks, lifted, 0, 0, half, 32, child_map)
+    load0, sent0 = run_put_rows(adds, ends, load0, low, other, half)
     recv0 = send(load0)
 
     load1, sent1 = run_sum_rows(marks, recv0, ends, run_pack(blocks, sent0, 0, half, half, 32), half)
@@ -576,8 +603,8 @@
     out, rest, based = run_base(edge, front, solved, head, (own0, sib0, own1, sib1), bs)
 
     sib2 = swap(run_late_sums(flags[1], recv2, based))
-    rest = run_add_own(core, flags[1], rest, recv2)
-    return run_add_late(core, out, rest, sib2).reshape(rows_dev, cols_dev)
+    rest = run_add_own(flags[1], rest, recv2)
+    return run_add_late(out, rest, sib2).reshape(rows_dev, cols_dev)
 
 
 def solution(mesh):

time: 179 us -> 178 us (level)
  Pallas kernels: 42.8 us -> 39.7 us
  waiting for transfers between devices: 72.7 us -> 74.5 us
    pallas_call x12, Pallas kernels: 42.8 us -> 39.7 us  [placed(): run(*(pltpu.with_memory_space_constraint(arg, pltpu.HBM) if spec is HBM e...]
    all_to_all x3, waiting for transfers between devices: 68.7 us -> 70.6 us  [send(): return lax.all_to_all(load, CHIP, 0, 0, tiled=True)]
  transfers between devices with their start and end apart: 8 -> 8, of which waited for: 4 -> 4; matrix products, arithmetic and copies ran while one was open for 16% -> 17% of each run, Pallas kernels for 18% -> 17%
where the time goes in v5:
time: 178 us; the launch traced here: 177 us
  waiting for transfers between devices  74.5 us (42%)
  Pallas kernels  39.7 us (22%)
  starting transfers between devices  30.4 us (17%)
  other arithmetic  23.5 us (13%)
  local copies, waits for them, and re-layouts  5.6 us (3%)
  matrix products  2.78 us (2%)
    all_to_all x3, waiting for transfers between devices, send(): return lax.all_to_all(load, CHIP, 0, 0, tiled=True)  70.6 us
    pallas_call x12, Pallas kernels, placed(): run(*(pltpu.with_memory_space_constraint(arg, pltpu.HBM) if spec is HBM e...  39.7 us
    all_to_all x3, starting transfers between devices, send(): return lax.all_to_all(load, CHIP, 0, 0, tiled=True)  23.2 us
    another operation x3, other arithmetic, body(): head = jnp.linalg.cholesky(corner)  12.4 us
    another operation x2, other arithmetic, body(): lax.linalg.triangular_solve(head, slabs.reshape(24 * bs, bs), left_side=F...  10.4 us
    ppermute x4, starting transfers between devices, swap(): return lax.ppermute(a, 'core', CORE_SWAP)  5.91 us
  transfers between devices with their start and end apart: 8, of which 4 were waited for; matrix products, arithmetic and copies ran while one was open for 17% of the time, Pallas kernels for 17%

profile of v5, /device:TPU:1, one launch (start us, length us, event | category | flops | bytes accessed | tf_op | source)
XLA Modules:
  0.0 176.9 jit_solution(6813460314757672452)
XLA Ops:
  0.0 2.4 %lift.1 = (f32[64,32,128]{2,1,0:T(8,128)S(1)}, f32[64,32,128]{2,1,0:T(8,128)S(1)}, f32[8,128]{1,0:T(8,128)S(1)}) custom-call(f32[16,128,1024]{2,1,0:T(8,128)} %bitcast.26, f32[16,128,1024]{2,1,0:T(8,128)} %bitcast.30), custom_call_target="tpu_custom_call" | custom-call | bytes 4194304 | tf_op jit(solution)/shard_map/lift/pallas_call | solution.py:35
  2.4 1.3 collective-permute-start
  3.7 2.5 %pack.3 = (f32[64,96,128]{2,1,0:T(8,128)}, f32[8,8,1024]{2,1,0:T(8,128)S(1)}, f32[2,16,128]{2,1,0:T(8,128)S(1)}) custom-call(f32[16,128,1024]{2,1,0:T(8,128)} %bitcast.27, f32[8,128]{1,0:T(8,128)S(1)} %get-tuple-element.25.wait, s32[4,64]{1,0:T(4,128)} %rest_0_.1), custom_call_target="tpu_custom_call" | custom-call | bytes 4194304 | tf_op jit(solution)/shard_map/pack/pallas_call | solution.py:35
  7.3 1.4 put_rows.1
  8.7 11.2 %all-to-all-start = ((f32[64,96,128]{2,1,0:T(8,128)}), f32[64,96,128]{2,1,0:T(8,128)S(1)}, u32[]{:S(2)}, u32[]{:S(2)}) async-start(f32[64,96,128]{2,1,0:T(8,128)} %get-tuple-element.31), calls=%async_computation | async-start | bytes 6291456 | tf_op jit(solution)/shard_map/all_to_all | solution.py:565
  20.5 2.4 %pack.4.load = f32[64,96,128]{2,1,0:T(8,128)} custom-call(f32[16,128,1024]{2,1,0:T(8,128)} %bitcast.28, f32[8,128]{1,0:T(8,128)S(1)} %get-tuple-element.32.wait), custom_call_target="tpu_custom_call" | custom-call | bytes 4194304 | tf_op jit(solution)/shard_map/pack/pallas_call | solution.py:35
  23.0 37.8 %all-to-all-done.recv = f32[64,96,128]{2,1,0:T(8,128)S(1)} async-done(((f32[64,96,128]{2,1,0:T(8,128)}), f32[64,96,128]{2,1,0:T(8,128)S(1)}, u32[]{:S(2)}, u32[]{:S(2)}) %all-to-all-start) | async-done | bytes 3145760 | tf_op jit(solution)/shard_map/all_to_all | solution.py:565
  62.2 6.2 %all-to-all-start.1 = ((f32[64,96,128]{2,1,0:T(8,128)}), f32[64,96,128]{2,1,0:T(8,128)}, u32[]{:S(2)}, u32[]{:S(2)}) async-start(f32[64,96,128]{2,1,0:T(8,128)} %get-tuple-element.33), calls=%async_computation.1 | async-start | bytes 6291456 | tf_op jit(solution)/shard_map/all_to_all | solution.py:565
  69.7 2.2 %child_sums.1 = (f32[2,4,4,72,128]{4,3,2,1,0:T(8,128)}, f32[2,4,4,72,128]{4,3,2,1,0:T(8,128)}, f32[8,128]{1,0:T(8,128)S(1)}) custom-call(f32[256]{0:T(256)S(1)} %reshape.141.flags, f32[64,96,128]{2,1,0:T(8,128)S(1)} %all-to-all-done.recv, f32[8,128]{1,0:T(8,128)S(1)} %get-tuple-element.36.wait), custom_call_target="tpu_custom_call" | custom-call | bytes 4194304 | tf_op jit(solution)/shard_map/child_sums/pallas_call | solution.py:35
  71.9 3.6 %pack.5 = f32[64,128,128]{2,1,0:T(8,128)} custom-call(f32[16,128,1024]{2,1,0:T(8,128)} %bitcast.29, f32[8,128]{1,0:T(8,128)S(1)} %get-tuple-element.43.wait), custom_call_target="tpu_custom_call" | custom-call | bytes 8388608 | tf_op jit(solution)/shard_map/pack/pallas_call | solution.py:35
  75.5 32.7 %all-to-all-done.1.mine = f32[64,96,128]{2,1,0:T(8,128)} async-done(((f32[64,96,128]{2,1,0:T(8,128)}), f32[64,96,128]{2,1,0:T(8,128)}, u32[]{:S(2)}, u32[]{:S(2)}) %all-to-all-start.1) | async-done | bytes 3145760 | tf_op jit(solution)/shard_map/all_to_all | solution.py:565
  108.2 5.7 %all-to-all-start.2 = ((f32[64,128,128]{2,1,0:T(8,128)}), f32[64,128,128]{2,1,0:T(8,128)}, u32[]{:S(2)}, u32[]{:S(2)}) async-start(f32[64,128,128]{2,1,0:T(8,128)} %pack.5), calls=%async_computation.2 | async-start | bytes 8388608 | tf_op jit(solution)/shard_map/all_to_all | solution.py:565
  113.9 1.4 slice.28
  115.3 2.8 %collective-permute-start.1 = (f32[64,40,128]{2,1,0:T(8,128)S(1)}, f32[64,40,128]{2,1,0:T(8,128)S(1)}, u32[]{:S(2)}, u32[]{:S(2)}) collective-permute-start(f32[64,40,128]{2,1,0:T(8,128)S(1)} %slice.28), channel_id=1, source_target_pairs={{0,1},{1,0},{2,3},{3,2},{4,5},{5,4},{6,7},{7,6},{8,9},{9,8},{10,11... | collective-permute-start | bytes 3932168 | tf_op jit(solution)/shard_map/ppermute | solution.py:562
  118.9 2.8 %collective-permute-done.1.other = f32[64,40,128]{2,1,0:T(8,128)S(1)} collective-permute-done((f32[64,40,128]{2,1,0:T(8,128)S(1)}, f32[64,40,128]{2,1,0:T(8,128)S(1)}, u32[]{:S(2)}, u32[]{:S(2)}) %collective-permute-start.1) | collective-permute-done | bytes 1310752 | tf_op jit(solution)/shard_map/ppermute | solution.py:562
  122.8 5.3 %assemble.1 = (f32[24,128,128]{2,1,0:T(8,128)}, f32[128,128]{1,0:T(8,128)S(1)}, f32[2,4,4,64,128]{4,3,2,1,0:T(8,128)}, f32[2,4,4,64,128]{4,3,2,1,0:T(8,128)}) custom-call(s32[1]{0:T(128)} %bitcast.4.core, f32[256]{0:T(256)S(1)} %reshape.141.flags, f32[64,96,128]{2,1,0:T(8,128)} %all-to-all-done.1.mine, f32[64,40,128]{2,1,0:T(8,128)} %copy-done), custom_call_target="tpu_custom_call" | custom-call | bytes 3276800 | tf_op jit(solution)/shard_map/assemble/pallas_call | solution.py:35
  129.0 11.7 %cholesky.16 = f32[128,128]{1,0:T(8,128)S(1)} custom-call(f32[128,128]{1,0:T(8,128)S(1)} %fusion.2), custom_call_target="Cholesky" | custom-call | tf_op jit(solution)/shard_map/jit(cholesky)/cholesky | solution.py:598
  142.0 9.8 %custom-call.6 = f32[1,128,128]{1,2,0:T(8,128)S(1)} custom-call(f32[1,128,128]{2,1,0:T(8,128)S(1)} %get-tuple-element.45), custom_call_target="InvertDiagBlocksLowerTriangular" | custom-call | tf_op jit(solution)/shard_map/triangular_solve | solution.py:599
  151.8 2.8 %fusion.solved = f32[3072,128]{1,0:T(8,128)S(1)} fusion(f32[3072,128]{1,0:T(8,128)} %bitcast.32, f32[1,128,128]{1,2,0:T(8,128)S(1)} %custom-call.6), kind=kOutput, calls=%fused_computation.2 | convolution fusion | flops 603979776 | bytes 3211264 | tf_op jit(solution)/shard_map/triangular_solve | solution.py:599
  155.6 10.4 %base.1 = (f32[8,256,1024]{2,1,0:T(8,128)}, f32[8,128,1024]{2,1,0:T(8,128)}, f32[8,128]{1,0:T(8,128)S(1)}) custom-call(s32[3]{0:T(128)S(1)} %add_convert_fusion.edge, f32[16,128,1024]{2,1,0:T(8,128)} %bitcast.31, f32[3072,128]{1,0:T(8,128)S(1)} %fusion.solved, f32[128,128]{1,0:T(8,128)S(1)} %get-tuple-element.46.head, ...), custom_call_target="tpu_custom_call" | custom-call | bytes 16777216 | tf_op jit(solution)/shard_map/base/pallas_call | solution.py:35
  166.1 2.4 %late_sums.1 = f32[2,4,4,128,128]{4,3,2,1,0:T(8,128)S(1)} custom-call(f32[256]{0:T(256)} %reshape.142.all_flags, f32[64,128,128]{2,1,0:T(8,128)} %all-to-all-done.2.recv, f32[8,128]{1,0:T(8,128)S(1)} %get-tuple-element.44.wait), custom_call_target="tpu_custom_call" | custom-call | bytes 6291456 | tf_op jit(solution)/shard_map/late_sums/pallas_call | solution.py:35
  168.5 2.4 %collective-permute-start.4 = (f32[2,4,4,128,128]{4,3,2,1,0:T(8,128)S(1)}, f32[2,4,4,128,128]{4,3,2,1,0:T(8,128)S(1)}, u32[]{:S(2)}, u32[]{:S(2)}) collective-permute-start(f32[2,4,4,128,128]{4,3,2,1,0:T(8,128)S(1)} %late_sums.1), channel_id=1, source_target_pairs={{0,1},{1,0},{2,3},{3,2},{4,5},{5,4},{6,7},{7,6},{8,9},{9,8},{10,11... | collective-permute-start | bytes 6291464 | tf_op jit(solution)/shard_map/ppermute | solution.py:562
  170.8 3.7 %add_own.1.rest = f32[8,128,1024]{2,1,0:T(8,128)S(1)} custom-call(f32[256]{0:T(256)} %reshape.142.all_flags, f32[8,128,1024]{2,1,0:T(8,128)} %get-tuple-element.42.rest, f32[64,128,128]{2,1,0:T(8,128)} %all-to-all-done.2.recv), custom_call_target="tpu_custom_call" | custom-call | bytes 12582912 | tf_op jit(solution)/shard_map/add_own/pallas_call | solution.py:35
  174.6 2.1 %add_late.1 = f32[8,256,1024]{2,1,0:T(8,128)} custom-call(f32[8,256,1024]{2,1,0:T(8,128)} %get-tuple-element.41.before, f32[8,128,1024]{2,1,0:T(8,128)S(1)} %add_own.1.rest, f32[2,4,4,128,128]{4,3,2,1,0:T(8,128)S(1)} %collective-permute-done.4.sib), custom_call_target="tpu_custom_call", output_to_operand_aliasing={{}: (0, {})} | custom-call | bytes 12582912 | tf_op jit(solution)/shard_map/add_late/pallas_call | solution.py:35
  (48 shorter events, 9.3 us)
Async XLA Ops:
  2.4 4.9 %collective-permute-start = (f32[64,32,128]{2,1,0:T(8,128)S(1)}, f32[64,32,128]{2,1,0:T(8,128)S(1)}, u32[]{:S(2)}, u32[]{:S(2)}) collective-permute-start(f32[64,32,128]{2,1,0:T(8,128)S(1)} %get-tuple-element.30), channel_id=1, source_target_pairs={{0,1},{8,9},{16,17},{24,25},{32,33},{40,41},{48,49},{56,57},{64,65... | collective-permute-start | bytes 3145736 | tf_op jit(solution)/shard_map/ppermute | solution.py:584
  8.7 11.3 %copy-start.2 = (s32[4,64]{1,0:T(4,128)S(1)}, s32[4,64]{1,0:T(4,128)}, u32[]{:S(2)}) copy-start(s32[4,64]{1,0:T(4,128)} %rest_0_.1) | copy-start | bytes 3076
  8.7 52.2 %all-to-all-start = ((f32[64,96,128]{2,1,0:T(8,128)}), f32[64,96,128]{2,1,0:T(8,128)S(1)}, u32[]{:S(2)}, u32[]{:S(2)}) async-start(f32[64,96,128]{2,1,0:T(8,128)} %get-tuple-element.31), calls=%async_computation | async-start | bytes 6291456 | tf_op jit(solution)/shard_map/all_to_all | solution.py:565
  62.2 46.0 %all-to-all-start.1 = ((f32[64,96,128]{2,1,0:T(8,128)}), f32[64,96,128]{2,1,0:T(8,128)}, u32[]{:S(2)}, u32[]{:S(2)}) async-start(f32[64,96,128]{2,1,0:T(8,128)} %get-tuple-element.33), calls=%async_computation.1 | async-start | bytes 6291456 | tf_op jit(solution)/shard_map/all_to_all | solution.py:565
  108.2 57.9 %all-to-all-start.2 = ((f32[64,128,128]{2,1,0:T(8,128)}), f32[64,128,128]{2,1,0:T(8,128)}, u32[]{:S(2)}, u32[]{:S(2)}) async-start(f32[64,128,128]{2,1,0:T(8,128)} %pack.5), calls=%async_computation.2 | async-start | bytes 8388608 | tf_op jit(solution)/shard_map/all_to_all | solution.py:565
  115.3 6.4 %collective-permute-start.1 = (f32[64,40,128]{2,1,0:T(8,128)S(1)}, f32[64,40,128]{2,1,0:T(8,128)S(1)}, u32[]{:S(2)}, u32[]{:S(2)}) collective-permute-start(f32[64,40,128]{2,1,0:T(8,128)S(1)} %slice.28), channel_id=1, source_target_pairs={{0,1},{1,0},{2,3},{3,2},{4,5},{5,4},{6,7},{7,6},{8,9},{9,8},{10,11... | collective-permute-start | bytes 3932168 | tf_op jit(solution)/shard_map/ppermute | solution.py:562
  118.1 36.5 %collective-permute-start.2 = (f32[2,4,4,72,128]{4,3,2,1,0:T(8,128)}, f32[2,4,4,72,128]{4,3,2,1,0:T(8,128)}, u32[]{:S(2)}, u32[]{:S(2)}) collective-permute-start(f32[2,4,4,72,128]{4,3,2,1,0:T(8,128)} %get-tuple-element.38), channel_id=1, source_target_pairs={{0,1},{1,0},{2,3},{3,2},{4,5},{5,4},{6,7},{7,6},{8,9},{9,8},{10,11... | collective-permute-start | bytes 3538952 | tf_op jit(solution)/shard_map/ppermute | solution.py:562
  121.7 1.1 copy-start
  128.2 26.5 %collective-permute-start.3 = (f32[2,4,4,64,128]{4,3,2,1,0:T(8,128)}, f32[2,4,4,64,128]{4,3,2,1,0:T(8,128)S(1)}, u32[]{:S(2)}, u32[]{:S(2)}) collective-permute-start(f32[2,4,4,64,128]{4,3,2,1,0:T(8,128)} %get-tuple-element.40), channel_id=1, source_target_pairs={{0,1},{1,0},{2,3},{3,2},{4,5},{5,4},{6,7},{7,6},{8,9},{9,8},{10,11... | collective-permute-start | bytes 3145736 | tf_op jit(solution)/shard_map/ppermute | solution.py:562
  154.7 1.0 copy-start.1
  168.5 6.2 %collective-permute-start.4 = (f32[2,4,4,128,128]{4,3,2,1,0:T(8,128)S(1)}, f32[2,4,4,128,128]{4,3,2,1,0:T(8,128)S(1)}, u32[]{:S(2)}, u32[]{:S(2)}) collective-permute-start(f32[2,4,4,128,128]{4,3,2,1,0:T(8,128)S(1)} %late_sums.1), channel_id=1, source_target_pairs={{0,1},{1,0},{2,3},{3,2},{4,5},{5,4},{6,7},{7,6},{8,9},{9,8},{10,11... | collective-permute-start | bytes 6291464 | tf_op jit(solution)/shard_map/ppermute | solution.py:562

commit v6 on v5

--- a/solution.py
+++ b/solution.py
@@ -12,6 +12,7 @@
 VMEM = pl.BlockSpec(memory_space=pltpu.VMEM)
 SMEM = pl.BlockSpec(memory_space=pltpu.SMEM)
 HBM = pl.BlockSpec(memory_space=pltpu.HBM)
+ANY = pl.BlockSpec(memory_space=pl.ANY)
 F32 = jnp.float32
 
 
@@ -147,22 +148,16 @@
         y, zh, x, zl, t = (lax.axis_index(a) for a in ALL)
         me, col_pair = 2 * y + zh, 2 * x + zl
         token[...] = jnp.zeros_like(token)
-        for c, part in ((0, low), (1, other)):
-            @pl.when(t == c)
-            def _():
-                region[...] = part[...]
-
-        @pl.when(col_pair == 0)
-        def _():
-            for at in range(64):
-                own = [region[at, pl.ds(8 * g + me, 1), :] for g in range(2)]
-                region[at, 16:32] += adds[0] * own[0] + adds[1] * own[1]
-
         slot = pl.ds(jnp.where(col_pair == 4, slot_of(0, 4), slot_of(me, 0)), 1)
         copies = []
         for j in range(8):
+            some = slice(8 * j, 8 * j + 8)
+            region[some] = jnp.where(t == 0, low[some], other[some])
             for jc in range(8):
-                region[8 * j + jc, slot, :] = ends[j, 7:8, jc * bs:(jc + 1) * bs]
+                at = 8 * j + jc
+                own = [region[at, pl.ds(8 * g + me, 1), :] for g in range(2)]
+                region[at, 16:32] += adds[0] * own[0] + adds[1] * own[1]
+                region[at, slot, :] = ends[j, 7:8, jc * bs:(jc + 1) * bs]
             some = pl.ds(8 * j, 8)
             copies.append(pltpu.make_async_copy(region.at[some], out.at[some, pl.ds(rows, 32)], sems.at[j]))
             copies[-1].start()
@@ -316,7 +311,7 @@
 
     part = shape(2, 4, 4, first, bs)
     return call(
-        assemble, (shape(24, bs, bs), shape(bs, bs), part, part), [SMEM, SMEM, VMEM, HBM], (HBM, VMEM, HBM, HBM),
+        assemble, (shape(24, bs, bs), shape(bs, bs), part, part), [SMEM, SMEM, VMEM, ANY], (HBM, VMEM, HBM, HBM),
         "assemble", 200 * bs * bs,
         [pltpu.VMEM(((chips + 1) * wide, bs), F32)] * 2 + [pltpu.VMEM((24, bs, bs), F32), pltpu.SemaphoreType.DMA((3,))]
         + sums_scratch(first, bs),
@@ -345,15 +340,18 @@
 
     group = 4
 
-    def base(edge, front, solved, head, own0, sib0, own1, sib1, out, rest, token, held, right, o0, s0, o1, s1, sems, more, back):
+    def base(edge, front, solved, head, own0, sib0, own1, sib1, out, rest, token, held, right, o0, s0, o1, s1, sems, more, back, parts_back):
         top, col_zero, left = edge[0] == 1, edge[1] == 1, edge[2] == 0
         token[...] = jnp.zeros_like(token)
 
         def read(i):
             return pltpu.make_async_copy(front.at[i], held.at[i], sems.at[i])
 
-        def write(i, to):
-            return pltpu.make_async_copy(held.at[i], to.at[i // 2, pl.ds(0, bs)], back.at[i])
+        def write(n):
+            return pltpu.make_async_copy(held.at[2 * n], out.at[n, pl.ds(0, bs)], back.at[n])
+
+        def part(n, c):
+            return pltpu.make_async_copy(held.at[2 * n + 1, :, pl.ds(c * bs, bs)], rest.at[c, n], parts_back.at[c, n])
 
         sums = [
             pltpu.make_async_copy(src, dst, more.at[n])
@@ -410,25 +408,27 @@
                         two = spread(left, own[up, sr, scp, inner:inner + step], sib[up, sr, scp, inner:inner + step])
                         for lanes, add in zip(pair(scp, bs), two):
                             held[i, here, lanes] += add
-                write(i, out).start()
-                write(i + 1, rest).start()
+                write(i // 2).start()
+                for c in range(cols // bs):
+                    part(i // 2, c).start()
             return carry
 
         lax.fori_loop(0, blocks // group, some, 0)
 
         def finish(n, carry):
-            write(2 * n, out).wait()
-            write(2 * n + 1, rest).wait()
+            write(n).wait()
+            for c in range(cols // bs):
+                part(n, c).wait()
             return carry
 
         lax.fori_loop(0, blocks // 2, finish, 0)
 
     parts = [pltpu.VMEM(a.shape, F32) for a in early]
     return call(
-        base, (shape(blocks // 2, 2 * bs, cols), shape(blocks // 2, bs, cols), TOKEN), [SMEM, HBM, VMEM, VMEM] + [HBM] * 4,
+        base, (shape(blocks // 2, 2 * bs, cols), shape(cols // bs, blocks // 2, bs, bs), TOKEN), [SMEM, HBM, VMEM, VMEM] + [ANY] * 4,
         (HBM, HBM, VMEM), "base", rows * cols * 8,
         [pltpu.VMEM((blocks, bs, cols), F32), pltpu.VMEM((cols, 6 * bs), jnp.bfloat16)] + parts
-        + [pltpu.SemaphoreType.DMA((n,)) for n in (blocks, 4, blocks)],
+        + [pltpu.SemaphoreType.DMA(n) for n in ((blocks,), (4,), (blocks // 2,), (cols // bs, blocks // 2))],
         limit=28,
     )(edge, front.reshape(blocks, bs, cols), solved, head, *early)
 
@@ -437,7 +437,7 @@
     chips, bs, _ = recv.shape
     step = 32
 
-    def late_sums(all_flags, recv, wait, sib, flags, held, flag_sem, sems):
+    def late_sums(all_flags, recv, wait, sib, held, flags, flag_sem, sems):
         fetch = pltpu.make_async_copy(all_flags, flags, flag_sem)
         fetch.start()
 
@@ -464,88 +464,91 @@
             lax.fori_loop(0, bs // step, one, 0)
 
     return call(
-        late_sums, shape(2, 4, 4, bs, bs), [HBM, HBM, VMEM], VMEM, "late_sums", 96 * bs * bs * 4,
+        late_sums, (shape(2, 4, 4, bs, bs), shape(*recv.shape)), [HBM, HBM, VMEM], (VMEM, VMEM), "late_sums", 96 * bs * bs * 4,
         [
-            pltpu.SMEM(flags.shape, F32), pltpu.VMEM((chips, bs, bs), F32), pltpu.SemaphoreType.DMA,
+            pltpu.SMEM(flags.shape, F32), pltpu.SemaphoreType.DMA,
             pltpu.SemaphoreType.DMA((8,)),
         ],
     )(flags, recv, wait)
 
 
-def run_add_own(flags, rest, recv):
-    blocks, bs, cols = rest.shape
-    step = 32
-
-    def add_own(all_flags, rest, recv, out, flags, held, flag_sem, sems, more):
+def run_add_own(flags, out, rest, recv):
+    bs, step = recv.shape[1], 32
+    parts = rest.reshape(8, 2, 4, bs, bs)
+
+    def add_own(all_flags, before, rest, held, out, others, flags, mine, flag_sem, own_sems, other_sems, back):
         fetch = pltpu.make_async_copy(all_flags, flags, flag_sem)
         fetch.start()
-        left = lax.axis_index("core") == 0
-
-        def read(sr, h):
-            some = pl.ds((4 * h + sr) * 8, 8)
-            return pltpu.make_async_copy(recv.at[some], held.at[some], sems.at[2 * sr + h])
-
-        def base(i):
-            return pltpu.make_async_copy(rest.at[i], out.at[i], more.at[i])
-
+        t = lax.axis_index("core")
+
+        def own(scp):
+            return pltpu.make_async_copy(rest.at[2 * scp + t], mine.at[scp], own_sems.at[scp])
+
+        def other(scp):
+            return pltpu.make_async_copy(rest.at[2 * scp + 1 - t], others.at[scp], other_sems.at[scp])
+
+        def write(sr, scp):
+            lanes = pl.ds(pl.multiple_of((2 * scp + t) * bs, bs), bs)
+            return pltpu.make_async_copy(mine.at[scp, :, sr], out.at[:, sr, pl.ds(bs, bs), lanes], back.at[sr, scp])
+
+        for scp in range(4):
+            own(scp).start()
+        for scp in range(4):
+            other(scp).start()
+        fetch.wait()
+        for scp in range(4):
+            own(scp).wait()
         for sr in range(4):
-            for n in range(2):
-                read(sr, n).start()
-                base(4 * n + sr).start()
-        fetch.wait()
-        for sr in range(4):
-            for n in range(2):
-                read(sr, n).wait()
-                base(4 * n + sr).wait()
-
             def one(i, carry):
                 here = pl.ds(pl.multiple_of(i * step, step), step)
                 for scp in range(4):
                     sums = add_blocks(flags, held, sr, scp, here, (0,))
                     for up in range(2):
-                        two = spread(left, sums[up, 0], 0.0)
-                        for lanes, add in zip(pair(scp, bs), two):
-                            out[4 * up + sr, here, lanes] += add
+                        mine[scp, up, sr, here] += sums[up, 0]
                 return carry
 
             lax.fori_loop(0, bs // step, one, 0)
-
-    return call(
-        add_own, shape(blocks, bs, cols), [HBM, HBM, HBM], VMEM, "add_own", blocks * bs * cols * 12,
-        [
-            pltpu.SMEM(flags.shape, F32), pltpu.VMEM(recv.shape, F32), pltpu.SemaphoreType.DMA,
-            pltpu.SemaphoreType.DMA((8,)), pltpu.SemaphoreType.DMA((8,)),
-        ],
-    )(flags, rest, recv)
-
-
-def run_add_late(out, rest, sib):
-    blocks, bs, cols = rest.shape
-    step = 32
-
-    def add_late(before, rest, sib, out, done, sems):
-        left = lax.axis_index("core") == 0
-
-        def write(i):
-            return pltpu.make_async_copy(done.at[i], out.at[i, pl.ds(bs, bs)], sems.at[i])
-
-        def one(i, carry):
-            up, sr = i // 4, i % 4
-            for at in range(0, bs, step):
-                here = slice(at, at + step)
-                for scp in range(4):
-                    for lanes, add in zip(pair(scp, bs), spread(left, 0.0, sib[up, sr, scp, here])):
-                        done[i, here, lanes] = rest[i, here, lanes] + add
-            write(i).start()
-            return carry
-
-        lax.fori_loop(0, blocks, one, 0)
-        lax.fori_loop(0, blocks, lambda i, c: (write(i).wait(), c)[1], 0)
-
-    return call(
-        add_late, shape(*out.shape), [HBM, VMEM, VMEM], HBM, "add_late", out.size * 6,
-        [pltpu.VMEM((blocks, bs, cols), F32), pltpu.SemaphoreType.DMA((blocks,))], aliases={0: 0},
-    )(out, rest, sib)
+            for scp in range(4):
+                write(sr, scp).start()
+        for scp in range(4):
+            other(scp).wait()
+            for sr in range(4):
+                write(sr, scp).wait()
+
+    half = (4, 2, 4, bs, bs)
+    return call(
+        add_own, (shape(*out.shape), shape(*half)), [HBM] * 3 + [VMEM], (HBM, VMEM), "add_own", rest.size * 12,
+        [pltpu.SMEM(flags.shape, F32), pltpu.VMEM(half, F32), pltpu.SemaphoreType.DMA]
+        + [pltpu.SemaphoreType.DMA(n) for n in ((4,), (4,), (4, 4))],
+        aliases={1: 0},
+    )(flags, out, parts, recv)
+
+
+def run_add_late(out, others, sib):
+    bs, step = sib.shape[-1], 32
+
+    def add_late(before, others, sib, out, done, sems):
+        t = lax.axis_index("core")
+
+        def write(scp, up):
+            lanes = pl.ds(pl.multiple_of((2 * scp + 1 - t) * bs, bs), bs)
+            return pltpu.make_async_copy(done.at[scp, up], out.at[up, :, pl.ds(bs, bs), lanes], sems.at[scp, up])
+
+        for scp in range(4):
+            for up in range(2):
+                for sr in range(4):
+                    for at in range(0, bs, step):
+                        here = slice(at, at + step)
+                        done[scp, up, sr, here] = others[scp, up, sr, here] + sib[up, sr, scp, here]
+                write(scp, up).start()
+        for scp in range(4):
+            for up in range(2):
+                write(scp, up).wait()
+
+    return call(
+        add_late, shape(*out.shape), [HBM, VMEM, VMEM], HBM, "add_late", others.size * 12,
+        [pltpu.VMEM(others.shape, F32), pltpu.SemaphoreType.DMA((4, 2))], aliases={0: 0},
+    )(out, others, sib)
 
 
 def body(front, updates, child_map):
@@ -602,9 +605,10 @@
     edge = jnp.stack([ji == 0, col == 0, t == 1]).astype(jnp.int32)
     out, rest, based = run_base(edge, front, solved, head, (own0, sib0, own1, sib1), bs)
 
-    sib2 = swap(run_late_sums(flags[1], recv2, based))
-    rest = run_add_own(flags[1], rest, recv2)
-    return run_add_late(out, rest, sib2).reshape(rows_dev, cols_dev)
+    sib2, held2 = run_late_sums(flags[1], recv2, based)
+    sib2 = swap(sib2)
+    out, others = run_add_own(flags[1], out.reshape(2, 4, 2 * bs, cols_dev), rest, held2)
+    return run_add_late(out, others, sib2).reshape(rows_dev, cols_dev)
 
 
 def solution(mesh):

time: 178 us -> 177 us (level)
  Pallas kernels: 39.7 us -> 36.4 us
    pallas_call x12, Pallas kernels: 39.7 us -> 36.4 us  [placed(): run(*(pltpu.with_memory_space_constraint(arg, pltpu.HBM) if spec is HBM e...]
  transfers between devices with their start and end apart: 8 -> 8, of which waited for: 4 -> 4; matrix products, arithmetic and copies ran while one was open for 17% -> 18% of each run, Pallas kernels for 17% -> 16%
where the time goes in v6:
time: 177 us; the launch traced here: 176 us
  waiting for transfers between devices  75.3 us (43%)
  Pallas kernels  36.4 us (21%)
  starting transfers between devices  30.8 us (17%)
  other arithmetic  24.4 us (14%)
  local copies, waits for them, and re-layouts  5.98 us (3%)
  matrix products  2.79 us (2%)
    all_to_all x3, waiting for transfers between devices, send(): return lax.all_to_all(load, CHIP, 0, 0, tiled=True)  70.3 us
    pallas_call x12, Pallas kernels, placed(): run(*(pltpu.with_memory_space_constraint(arg, pltpu.HBM) if spec is HBM e...  36.4 us
    all_to_all x3, starting transfers between devices, send(): return lax.all_to_all(load, CHIP, 0, 0, tiled=True)  23.9 us
    another operation x3, other arithmetic, body(): head = jnp.linalg.cholesky(corner)  12.5 us
    another operation x2, other arithmetic, body(): lax.linalg.triangular_solve(head, slabs.reshape(24 * bs, bs), left_side=F...  10.4 us
    ppermute x4, starting transfers between devices, swap(): return lax.ppermute(a, 'core', CORE_SWAP)  5.68 us
    ppermute x4, waiting for transfers between devices, swap(): return lax.ppermute(a, 'core', CORE_SWAP)  3.9 us
  transfers between devices with their start and end apart: 8, of which 4 were waited for; matrix products, arithmetic and copies ran while one was open for 18% of the time, Pallas kernels for 16%

profile of v6, /device:TPU:1, one launch (start us, length us, event | category | flops | bytes accessed | tf_op | source)
XLA Modules:
  0.0 176.2 jit_solution(12300145118738898859)
XLA Ops:
  0.0 2.4 %lift.1 = (f32[64,32,128]{2,1,0:T(8,128)S(1)}, f32[64,32,128]{2,1,0:T(8,128)S(1)}, f32[8,128]{1,0:T(8,128)S(1)}) custom-call(f32[16,128,1024]{2,1,0:T(8,128)} %bitcast.28, f32[16,128,1024]{2,1,0:T(8,128)} %bitcast.32), custom_call_target="tpu_custom_call" | custom-call | bytes 4194304 | tf_op jit(solution)/shard_map/lift/pallas_call | solution.py:36
  2.4 1.3 collective-permute-start
  3.7 2.5 %pack.3 = (f32[64,96,128]{2,1,0:T(8,128)}, f32[8,8,1024]{2,1,0:T(8,128)S(1)}, f32[2,16,128]{2,1,0:T(8,128)S(1)}) custom-call(f32[16,128,1024]{2,1,0:T(8,128)} %bitcast.29, f32[8,128]{1,0:T(8,128)S(1)} %get-tuple-element.29.wait, s32[4,64]{1,0:T(4,128)} %rest_0_.1), custom_call_target="tpu_custom_call" | custom-call | bytes 4194304 | tf_op jit(solution)/shard_map/pack/pallas_call | solution.py:36
  8.4 11.5 %all-to-all-start = ((f32[64,96,128]{2,1,0:T(8,128)}), f32[64,96,128]{2,1,0:T(8,128)S(1)}, u32[]{:S(2)}, u32[]{:S(2)}) async-start(f32[64,96,128]{2,1,0:T(8,128)} %get-tuple-element.35), calls=%async_computation | async-start | bytes 6291456 | tf_op jit(solution)/shard_map/all_to_all | solution.py:568
  20.6 2.5 %pack.4.load = f32[64,96,128]{2,1,0:T(8,128)} custom-call(f32[16,128,1024]{2,1,0:T(8,128)} %bitcast.30, f32[8,128]{1,0:T(8,128)S(1)} %get-tuple-element.36.wait), custom_call_target="tpu_custom_call" | custom-call | bytes 4194304 | tf_op jit(solution)/shard_map/pack/pallas_call | solution.py:36
  23.0 37.9 %all-to-all-done.recv = f32[64,96,128]{2,1,0:T(8,128)S(1)} async-done(((f32[64,96,128]{2,1,0:T(8,128)}), f32[64,96,128]{2,1,0:T(8,128)S(1)}, u32[]{:S(2)}, u32[]{:S(2)}) %all-to-all-start) | async-done | bytes 3145760 | tf_op jit(solution)/shard_map/all_to_all | solution.py:568
  61.0 1.3 sum_rows.1
  62.3 6.1 %all-to-all-start.1 = ((f32[64,96,128]{2,1,0:T(8,128)}), f32[64,96,128]{2,1,0:T(8,128)}, u32[]{:S(2)}, u32[]{:S(2)}) async-start(f32[64,96,128]{2,1,0:T(8,128)} %get-tuple-element.37), calls=%async_computation.1 | async-start | bytes 6291456 | tf_op jit(solution)/shard_map/all_to_all | solution.py:568
  69.7 2.3 %child_sums.1 = (f32[2,4,4,72,128]{4,3,2,1,0:T(8,128)}, f32[2,4,4,72,128]{4,3,2,1,0:T(8,128)}, f32[8,128]{1,0:T(8,128)S(1)}) custom-call(f32[256]{0:T(256)S(1)} %reshape.150.flags, f32[64,96,128]{2,1,0:T(8,128)S(1)} %all-to-all-done.recv, f32[8,128]{1,0:T(8,128)S(1)} %get-tuple-element.40.wait), custom_call_target="tpu_custom_call" | custom-call | bytes 4194304 | tf_op jit(solution)/shard_map/child_sums/pallas_call | solution.py:36
  72.0 3.5 %pack.5 = f32[64,128,128]{2,1,0:T(8,128)} custom-call(f32[16,128,1024]{2,1,0:T(8,128)} %bitcast.31, f32[8,128]{1,0:T(8,128)S(1)} %get-tuple-element.47.wait), custom_call_target="tpu_custom_call" | custom-call | bytes 8388608 | tf_op jit(solution)/shard_map/pack/pallas_call | solution.py:36
  75.5 32.5 %all-to-all-done.1.mine = f32[64,96,128]{2,1,0:T(8,128)} async-done(((f32[64,96,128]{2,1,0:T(8,128)}), f32[64,96,128]{2,1,0:T(8,128)}, u32[]{:S(2)}, u32[]{:S(2)}) %all-to-all-start.1) | async-done | bytes 3145760 | tf_op jit(solution)/shard_map/all_to_all | solution.py:568
  108.0 6.2 %all-to-all-start.2 = ((f32[64,128,128]{2,1,0:T(8,128)}), f32[64,128,128]{2,1,0:T(8,128)}, u32[]{:S(2)}, u32[]{:S(2)}) async-start(f32[64,128,128]{2,1,0:T(8,128)} %pack.5), calls=%async_computation.2 | async-start | bytes 8388608 | tf_op jit(solution)/shard_map/all_to_all | solution.py:568
  114.2 2.5 %slice.29 = f32[64,40,128]{2,1,0:T(8,128)} slice(f32[64,96,128]{2,1,0:T(8,128)} %all-to-all-done.1.mine), slice={[0:64], [56:96], [0:128]} | slice | bytes 2621440 | tf_op jit(solution)/shard_map/slice | solution.py:599
  116.7 2.3 %collective-permute-start.1 = (f32[64,40,128]{2,1,0:T(8,128)}, f32[64,40,128]{2,1,0:T(8,128)S(1)}, u32[]{:S(2)}, u32[]{:S(2)}) collective-permute-start(f32[64,40,128]{2,1,0:T(8,128)} %slice.29), channel_id=1, source_target_pairs={{0,1},{1,0},{2,3},{3,2},{4,5},{5,4},{6,7},{7,6},{8,9},{9,8},{10,11... | collective-permute-start | bytes 3932168 | tf_op jit(solution)/shard_map/ppermute | solution.py:565
  119.6 3.9 %collective-permute-done.1.other = f32[64,40,128]{2,1,0:T(8,128)S(1)} collective-permute-done((f32[64,40,128]{2,1,0:T(8,128)}, f32[64,40,128]{2,1,0:T(8,128)S(1)}, u32[]{:S(2)}, u32[]{:S(2)}) %collective-permute-start.1) | collective-permute-done | bytes 1310752 | tf_op jit(solution)/shard_map/ppermute | solution.py:565
  123.5 4.4 %assemble.1 = (f32[24,128,128]{2,1,0:T(8,128)}, f32[128,128]{1,0:T(8,128)S(1)}, f32[2,4,4,64,128]{4,3,2,1,0:T(8,128)}, f32[2,4,4,64,128]{4,3,2,1,0:T(8,128)}) custom-call(s32[1]{0:T(128)} %bitcast.7.core, f32[256]{0:T(256)S(1)} %reshape.150.flags, f32[64,96,128]{2,1,0:T(8,128)} %all-to-all-done.1.mine, f32[64,40,128]{2,1,0:T(8,128)S(1)} %collective-permute-done.1.other), custom_call_target="tpu_custom_call" | custom-call | bytes 3276800 | tf_op jit(solution)/shard_map/assemble/pallas_call | solution.py:36
  130.7 11.7 %cholesky.16 = f32[128,128]{1,0:T(8,128)S(1)} custom-call(f32[128,128]{1,0:T(8,128)S(1)} %fusion.2), custom_call_target="Cholesky" | custom-call | tf_op jit(solution)/shard_map/jit(cholesky)/cholesky | solution.py:601
  143.8 9.8 %custom-call.6 = f32[1,128,128]{1,2,0:T(8,128)S(1)} custom-call(f32[1,128,128]{2,1,0:T(8,128)S(1)} %get-tuple-element.53), custom_call_target="InvertDiagBlocksLowerTriangular" | custom-call | tf_op jit(solution)/shard_map/triangular_solve | solution.py:602
  153.7 2.8 %fusion.solved = f32[3072,128]{1,0:T(8,128)S(1)} fusion(f32[3072,128]{1,0:T(8,128)} %bitcast.36, f32[1,128,128]{1,2,0:T(8,128)S(1)} %custom-call.6), kind=kOutput, calls=%fused_computation.2 | convolution fusion | flops 603979776 | bytes 3211264 | tf_op jit(solution)/shard_map/triangular_solve | solution.py:602
  156.5 9.0 %base.1 = (f32[8,256,1024]{2,1,0:T(8,128)}, f32[8,8,128,128]{3,2,1,0:T(8,128)}, f32[8,128]{1,0:T(8,128)S(1)}) custom-call(s32[3]{0:T(128)S(1)} %add_convert_fusion.edge, f32[16,128,1024]{2,1,0:T(8,128)} %bitcast.33, f32[3072,128]{1,0:T(8,128)S(1)} %fusion.solved, f32[128,128]{1,0:T(8,128)S(1)} %get-tuple-element.54.head, f32[2,4,4,72,128]{4,3,2,1,0:T(8,128)S(1)} %copy-done, ...), custom_call_target="tpu_custom_call" | custom-call | bytes 16777216 | tf_op jit(solution)/shard_map/base/pallas_call | solution.py:36
  165.5 2.4 %late_sums.1 = (f32[2,4,4,128,128]{4,3,2,1,0:T(8,128)S(1)}, f32[64,128,128]{2,1,0:T(8,128)S(1)}) custom-call(f32[256]{0:T(256)} %reshape.149.all_flags, f32[64,128,128]{2,1,0:T(8,128)} %all-to-all-done.2.recv, f32[8,128]{1,0:T(8,128)S(1)} %get-tuple-element.48.wait), custom_call_target="tpu_custom_call" | custom-call | bytes 6291456 | tf_op jit(solution)/shard_map/late_sums/pallas_call | solution.py:36
  167.9 3.0 %collective-permute-start.4 = (f32[2,4,4,128,128]{4,3,2,1,0:T(8,128)S(1)}, f32[2,4,4,128,128]{4,3,2,1,0:T(8,128)S(1)}, u32[]{:S(2)}, u32[]{:S(2)}) collective-permute-start(f32[2,4,4,128,128]{4,3,2,1,0:T(8,128)S(1)} %get-tuple-element.52), channel_id=1, source_target_pairs={{0,1},{1,0},{2,3},{3,2},{4,5},{5,4},{6,7},{7,6},{8,9},{9,8},{10,11... | collective-permute-start | bytes 6291464 | tf_op jit(solution)/shard_map/ppermute | solution.py:565
  170.9 3.7 %add_own.1 = (f32[2,4,256,1024]{3,2,1,0:T(8,128)}, f32[4,2,4,128,128]{4,3,2,1,0:T(8,128)S(1)}) custom-call(f32[256]{0:T(256)} %reshape.149.all_flags, f32[2,4,256,1024]{3,2,1,0:T(8,128)} %bitcast.34, f32[8,2,4,128,128]{4,3,2,1,0:T(8,128)} %bitcast.35, f32[64,128,128]{2,1,0:T(8,128)S(1)} %get-tuple-element.49.held), custom_call_target="tpu_custom_call", output_to_operand_aliasing={{0}: (1, {})} | custom-call | bytes 12582912 | tf_op jit(solution)/shard_map/add_own/pallas_call | solution.py:36
  174.7 1.4 add_late.1
  (50 shorter events, 9.0 us)
Async XLA Ops:
  2.4 4.9 %collective-permute-start = (f32[64,32,128]{2,1,0:T(8,128)S(1)}, f32[64,32,128]{2,1,0:T(8,128)S(1)}, u32[]{:S(2)}, u32[]{:S(2)}) collective-permute-start(f32[64,32,128]{2,1,0:T(8,128)S(1)} %get-tuple-element.34), channel_id=1, source_target_pairs={{0,1},{8,9},{16,17},{24,25},{32,33},{40,41},{48,49},{56,57},{64,65... | collective-permute-start | bytes 3145736 | tf_op jit(solution)/shard_map/ppermute | solution.py:587
  8.4 11.5 %copy-start.3 = (s32[4,64]{1,0:T(4,128)S(1)}, s32[4,64]{1,0:T(4,128)}, u32[]{:S(2)}) copy-start(s32[4,64]{1,0:T(4,128)} %rest_0_.1) | copy-start | bytes 3076
  8.4 52.4 %all-to-all-start = ((f32[64,96,128]{2,1,0:T(8,128)}), f32[64,96,128]{2,1,0:T(8,128)S(1)}, u32[]{:S(2)}, u32[]{:S(2)}) async-start(f32[64,96,128]{2,1,0:T(8,128)} %get-tuple-element.35), calls=%async_computation | async-start | bytes 6291456 | tf_op jit(solution)/shard_map/all_to_all | solution.py:568
  62.3 45.7 %all-to-all-start.1 = ((f32[64,96,128]{2,1,0:T(8,128)}), f32[64,96,128]{2,1,0:T(8,128)}, u32[]{:S(2)}, u32[]{:S(2)}) async-start(f32[64,96,128]{2,1,0:T(8,128)} %get-tuple-element.37), calls=%async_computation.1 | async-start | bytes 6291456 | tf_op jit(solution)/shard_map/all_to_all | solution.py:568
  108.0 57.5 %all-to-all-start.2 = ((f32[64,128,128]{2,1,0:T(8,128)}), f32[64,128,128]{2,1,0:T(8,128)}, u32[]{:S(2)}, u32[]{:S(2)}) async-start(f32[64,128,128]{2,1,0:T(8,128)} %pack.5), calls=%async_computation.2 | async-start | bytes 8388608 | tf_op jit(solution)/shard_map/all_to_all | solution.py:568
  116.7 6.8 %collective-permute-start.1 = (f32[64,40,128]{2,1,0:T(8,128)}, f32[64,40,128]{2,1,0:T(8,128)S(1)}, u32[]{:S(2)}, u32[]{:S(2)}) collective-permute-start(f32[64,40,128]{2,1,0:T(8,128)} %slice.29), channel_id=1, source_target_pairs={{0,1},{1,0},{2,3},{3,2},{4,5},{5,4},{6,7},{7,6},{8,9},{9,8},{10,11... | collective-permute-start | bytes 3932168 | tf_op jit(solution)/shard_map/ppermute | solution.py:565
  118.9 37.5 %collective-permute-start.2 = (f32[2,4,4,72,128]{4,3,2,1,0:T(8,128)}, f32[2,4,4,72,128]{4,3,2,1,0:T(8,128)}, u32[]{:S(2)}, u32[]{:S(2)}) collective-permute-start(f32[2,4,4,72,128]{4,3,2,1,0:T(8,128)} %get-tuple-element.42), channel_id=1, source_target_pairs={{0,1},{1,0},{2,3},{3,2},{4,5},{5,4},{6,7},{7,6},{8,9},{9,8},{10,11... | collective-permute-start | bytes 3538952 | tf_op jit(solution)/shard_map/ppermute | solution.py:565
  123.5 33.0 %copy-start = (f32[2,4,4,72,128]{4,3,2,1,0:T(8,128)S(1)}, f32[2,4,4,72,128]{4,3,2,1,0:T(8,128)}, u32[]{:S(2)}) copy-start(f32[2,4,4,72,128]{4,3,2,1,0:T(8,128)} %get-tuple-element.41.own0) | copy-start | bytes 3538948
  127.9 0.6 copy-start.2
  128.5 28.0 %copy-start.1 = (f32[2,4,4,64,128]{4,3,2,1,0:T(8,128)S(1)}, f32[2,4,4,64,128]{4,3,2,1,0:T(8,128)}, u32[]{:S(2)}) copy-start(f32[2,4,4,64,128]{4,3,2,1,0:T(8,128)} %get-tuple-element.43.own1) | copy-start | bytes 3145732
  128.5 28.0 %collective-permute-start.3 = (f32[2,4,4,64,128]{4,3,2,1,0:T(8,128)}, f32[2,4,4,64,128]{4,3,2,1,0:T(8,128)S(1)}, u32[]{:S(2)}, u32[]{:S(2)}) collective-permute-start(f32[2,4,4,64,128]{4,3,2,1,0:T(8,128)} %get-tuple-element.44), channel_id=1, source_target_pairs={{0,1},{1,0},{2,3},{3,2},{4,5},{5,4},{6,7},{7,6},{8,9},{9,8},{10,11... | collective-permute-start | bytes 3145736 | tf_op jit(solution)/shard_map/ppermute | solution.py:565
  167.9 6.8 %collective-permute-start.4 = (f32[2,4,4,128,128]{4,3,2,1,0:T(8,128)S(1)}, f32[2,4,4,128,128]{4,3,2,1,0:T(8,128)S(1)}, u32[]{:S(2)}, u32[]{:S(2)}) collective-permute-start(f32[2,4,4,128,128]{4,3,2,1,0:T(8,128)S(1)} %get-tuple-element.52), channel_id=1, source_target_pairs={{0,1},{1,0},{2,3},{3,2},{4,5},{5,4},{6,7},{7,6},{8,9},{9,8},{10,11... | collective-permute-start | bytes 6291464 | tf_op jit(solution)/shard_map/ppermute | solution.py:565

commit v7 on v6

--- a/solution.py
+++ b/solution.py
@@ -435,39 +435,41 @@
 
 def run_late_sums(flags, recv, wait):
     chips, bs, _ = recv.shape
-    step = 32
+    step, cuts = 32, 2
+    part = bs // cuts
 
     def late_sums(all_flags, recv, wait, sib, held, flags, flag_sem, sems):
         fetch = pltpu.make_async_copy(all_flags, flags, flag_sem)
         fetch.start()
 
-        def read(sr, h):
-            some = pl.ds((4 * h + sr) * 8, 8)
-            return pltpu.make_async_copy(recv.at[some], held.at[some], sems.at[2 * sr + h])
-
-        for sr in range(4):
+        def read(sr, cut, h):
+            some, here = pl.ds((4 * h + sr) * 8, 8), pl.ds(cut * part, part)
+            return pltpu.make_async_copy(recv.at[some, here], held.at[some, here], sems.at[sr, cut, h])
+
+        pieces = [(sr, cut) for sr in range(4) for cut in range(cuts)]
+        for sr, cut in pieces:
             for h in range(2):
-                read(sr, h).start()
+                read(sr, cut, h).start()
         fetch.wait()
-        for sr in range(4):
+        for sr, cut in pieces:
             for h in range(2):
-                read(sr, h).wait()
+                read(sr, cut, h).wait()
 
             def one(i, carry):
-                here = pl.ds(pl.multiple_of(i * step, step), step)
+                here = pl.ds(pl.multiple_of(cut * part + i * step, step), step)
                 for scp in range(4):
                     sums = add_blocks(flags, held, sr, scp, here, (1,))
                     for up in range(2):
                         sib[up, sr, scp, here] = sums[up, 1]
                 return carry
 
-            lax.fori_loop(0, bs // step, one, 0)
+            lax.fori_loop(0, part // step, one, 0)
 
     return call(
         late_sums, (shape(2, 4, 4, bs, bs), shape(*recv.shape)), [HBM, HBM, VMEM], (VMEM, VMEM), "late_sums", 96 * bs * bs * 4,
         [
             pltpu.SMEM(flags.shape, F32), pltpu.SemaphoreType.DMA,
-            pltpu.SemaphoreType.DMA((8,)),
+            pltpu.SemaphoreType.DMA((4, cuts, 2)),
         ],
     )(flags, recv, wait)
 

time: 177 us -> 177 us (level)
  no operation moved by 1% of the time
where the time goes in v7:
time: 177 us; the launch traced here: 176 us
  waiting for transfers between devices  75.3 us (43%)
  Pallas kernels  36.4 us (21%)
  starting transfers between devices  30.8 us (17%)
  other arithmetic  24.4 us (14%)
  local copies, waits for them, and re-layouts  5.98 us (3%)
  matrix products  2.79 us (2%)
    all_to_all x3, waiting for transfers between devices, send(): return lax.all_to_all(load, CHIP, 0, 0, tiled=True)  70.3 us
    pallas_call x12, Pallas kernels, placed(): run(*(pltpu.with_memory_space_constraint(arg, pltpu.HBM) if spec is HBM e...  36.4 us
    all_to_all x3, starting transfers between devices, send(): return lax.all_to_all(load, CHIP, 0, 0, tiled=True)  23.9 us
    another operation x3, other arithmetic, body(): head = jnp.linalg.cholesky(corner)  12.5 us
    another operation x2, other arithmetic, body(): lax.linalg.triangular_solve(head, slabs.reshape(24 * bs, bs), left_side=F...  10.4 us
    ppermute x4, starting transfers between devices, swap(): return lax.ppermute(a, 'core', CORE_SWAP)  5.67 us
    ppermute x4, waiting for transfers between devices, swap(): return lax.ppermute(a, 'core', CORE_SWAP)  3.9 us
  transfers between devices with their start and end apart: 8, of which 4 were waited for; matrix products, arithmetic and copies ran while one was open for 18% of the time, Pallas kernels for 16%

profile of v7, /device:TPU:1, one launch (start us, length us, event | category | flops | bytes accessed | tf_op | source)
XLA Modules:
  0.0 176.2 jit_solution(3467908631535856214)
XLA Ops:
  0.0 2.4 %lift.1 = (f32[64,32,128]{2,1,0:T(8,128)S(1)}, f32[64,32,128]{2,1,0:T(8,128)S(1)}, f32[8,128]{1,0:T(8,128)S(1)}) custom-call(f32[16,128,1024]{2,1,0:T(8,128)} %bitcast.28, f32[16,128,1024]{2,1,0:T(8,128)} %bitcast.32), custom_call_target="tpu_custom_call" | custom-call | bytes 4194304 | tf_op jit(solution)/shard_map/lift/pallas_call | solution.py:36
  2.4 1.3 collective-permute-start
  3.7 2.5 %pack.3 = (f32[64,96,128]{2,1,0:T(8,128)}, f32[8,8,1024]{2,1,0:T(8,128)S(1)}, f32[2,16,128]{2,1,0:T(8,128)S(1)}) custom-call(f32[16,128,1024]{2,1,0:T(8,128)} %bitcast.29, f32[8,128]{1,0:T(8,128)S(1)} %get-tuple-element.29.wait, s32[4,64]{1,0:T(4,128)} %rest_0_.1), custom_call_target="tpu_custom_call" | custom-call | bytes 4194304 | tf_op jit(solution)/shard_map/pack/pallas_call | solution.py:36
  8.4 11.5 %all-to-all-start = ((f32[64,96,128]{2,1,0:T(8,128)}), f32[64,96,128]{2,1,0:T(8,128)S(1)}, u32[]{:S(2)}, u32[]{:S(2)}) async-start(f32[64,96,128]{2,1,0:T(8,128)} %get-tuple-element.35), calls=%async_computation | async-start | bytes 6291456 | tf_op jit(solution)/shard_map/all_to_all | solution.py:570
  20.6 2.5 %pack.4.load = f32[64,96,128]{2,1,0:T(8,128)} custom-call(f32[16,128,1024]{2,1,0:T(8,128)} %bitcast.30, f32[8,128]{1,0:T(8,128)S(1)} %get-tuple-element.36.wait), custom_call_target="tpu_custom_call" | custom-call | bytes 4194304 | tf_op jit(solution)/shard_map/pack/pallas_call | solution.py:36
  23.0 37.9 %all-to-all-done.recv = f32[64,96,128]{2,1,0:T(8,128)S(1)} async-done(((f32[64,96,128]{2,1,0:T(8,128)}), f32[64,96,128]{2,1,0:T(8,128)S(1)}, u32[]{:S(2)}, u32[]{:S(2)}) %all-to-all-start) | async-done | bytes 3145760 | tf_op jit(solution)/shard_map/all_to_all | solution.py:570
  61.0 1.3 sum_rows.1
  62.3 6.1 %all-to-all-start.1 = ((f32[64,96,128]{2,1,0:T(8,128)}), f32[64,96,128]{2,1,0:T(8,128)}, u32[]{:S(2)}, u32[]{:S(2)}) async-start(f32[64,96,128]{2,1,0:T(8,128)} %get-tuple-element.37), calls=%async_computation.1 | async-start | bytes 6291456 | tf_op jit(solution)/shard_map/all_to_all | solution.py:570
  69.7 2.3 %child_sums.1 = (f32[2,4,4,72,128]{4,3,2,1,0:T(8,128)}, f32[2,4,4,72,128]{4,3,2,1,0:T(8,128)}, f32[8,128]{1,0:T(8,128)S(1)}) custom-call(f32[256]{0:T(256)S(1)} %reshape.150.flags, f32[64,96,128]{2,1,0:T(8,128)S(1)} %all-to-all-done.recv, f32[8,128]{1,0:T(8,128)S(1)} %get-tuple-element.40.wait), custom_call_target="tpu_custom_call" | custom-call | bytes 4194304 | tf_op jit(solution)/shard_map/child_sums/pallas_call | solution.py:36
  72.0 3.5 %pack.5 = f32[64,128,128]{2,1,0:T(8,128)} custom-call(f32[16,128,1024]{2,1,0:T(8,128)} %bitcast.31, f32[8,128]{1,0:T(8,128)S(1)} %get-tuple-element.47.wait), custom_call_target="tpu_custom_call" | custom-call | bytes 8388608 | tf_op jit(solution)/shard_map/pack/pallas_call | solution.py:36
  75.5 32.5 %all-to-all-done.1.mine = f32[64,96,128]{2,1,0:T(8,128)} async-done(((f32[64,96,128]{2,1,0:T(8,128)}), f32[64,96,128]{2,1,0:T(8,128)}, u32[]{:S(2)}, u32[]{:S(2)}) %all-to-all-start.1) | async-done | bytes 3145760 | tf_op jit(solution)/shard_map/all_to_all | solution.py:570
  108.0 6.2 %all-to-all-start.2 = ((f32[64,128,128]{2,1,0:T(8,128)}), f32[64,128,128]{2,1,0:T(8,128)}, u32[]{:S(2)}, u32[]{:S(2)}) async-start(f32[64,128,128]{2,1,0:T(8,128)} %pack.5), calls=%async_computation.2 | async-start | bytes 8388608 | tf_op jit(solution)/shard_map/all_to_all | solution.py:570
  114.2 2.5 %slice.29 = f32[64,40,128]{2,1,0:T(8,128)} slice(f32[64,96,128]{2,1,0:T(8,128)} %all-to-all-done.1.mine), slice={[0:64], [56:96], [0:128]} | slice | bytes 2621440 | tf_op jit(solution)/shard_map/slice | solution.py:601
  116.7 2.3 %collective-permute-start.1 = (f32[64,40,128]{2,1,0:T(8,128)}, f32[64,40,128]{2,1,0:T(8,128)S(1)}, u32[]{:S(2)}, u32[]{:S(2)}) collective-permute-start(f32[64,40,128]{2,1,0:T(8,128)} %slice.29), channel_id=1, source_target_pairs={{0,1},{1,0},{2,3},{3,2},{4,5},{5,4},{6,7},{7,6},{8,9},{9,8},{10,11... | collective-permute-start | bytes 3932168 | tf_op jit(solution)/shard_map/ppermute | solution.py:567
  119.6 3.9 %collective-permute-done.1.other = f32[64,40,128]{2,1,0:T(8,128)S(1)} collective-permute-done((f32[64,40,128]{2,1,0:T(8,128)}, f32[64,40,128]{2,1,0:T(8,128)S(1)}, u32[]{:S(2)}, u32[]{:S(2)}) %collective-permute-start.1) | collective-permute-done | bytes 1310752 | tf_op jit(solution)/shard_map/ppermute | solution.py:567
  123.5 4.4 %assemble.1 = (f32[24,128,128]{2,1,0:T(8,128)}, f32[128,128]{1,0:T(8,128)S(1)}, f32[2,4,4,64,128]{4,3,2,1,0:T(8,128)}, f32[2,4,4,64,128]{4,3,2,1,0:T(8,128)}) custom-call(s32[1]{0:T(128)} %bitcast.7.core, f32[256]{0:T(256)S(1)} %reshape.150.flags, f32[64,96,128]{2,1,0:T(8,128)} %all-to-all-done.1.mine, f32[64,40,128]{2,1,0:T(8,128)S(1)} %collective-permute-done.1.other), custom_call_target="tpu_custom_call" | custom-call | bytes 3276800 | tf_op jit(solution)/shard_map/assemble/pallas_call | solution.py:36
  130.7 11.7 %cholesky.16 = f32[128,128]{1,0:T(8,128)S(1)} custom-call(f32[128,128]{1,0:T(8,128)S(1)} %fusion.2), custom_call_target="Cholesky" | custom-call | tf_op jit(solution)/shard_map/jit(cholesky)/cholesky | solution.py:603
  143.8 9.8 %custom-call.6 = f32[1,128,128]{1,2,0:T(8,128)S(1)} custom-call(f32[1,128,128]{2,1,0:T(8,128)S(1)} %get-tuple-element.53), custom_call_target="InvertDiagBlocksLowerTriangular" | custom-call | tf_op jit(solution)/shard_map/triangular_solve | solution.py:604
  153.7 2.8 %fusion.solved = f32[3072,128]{1,0:T(8,128)S(1)} fusion(f32[3072,128]{1,0:T(8,128)} %bitcast.36, f32[1,128,128]{1,2,0:T(8,128)S(1)} %custom-call.6), kind=kOutput, calls=%fused_computation.2 | convolution fusion | flops 603979776 | bytes 3211264 | tf_op jit(solution)/shard_map/triangular_solve | solution.py:604
  156.5 9.0 %base.1 = (f32[8,256,1024]{2,1,0:T(8,128)}, f32[8,8,128,128]{3,2,1,0:T(8,128)}, f32[8,128]{1,0:T(8,128)S(1)}) custom-call(s32[3]{0:T(128)S(1)} %add_convert_fusion.edge, f32[16,128,1024]{2,1,0:T(8,128)} %bitcast.33, f32[3072,128]{1,0:T(8,128)S(1)} %fusion.solved, f32[128,128]{1,0:T(8,128)S(1)} %get-tuple-element.54.head, f32[2,4,4,72,128]{4,3,2,1,0:T(8,128)S(1)} %copy-done, ...), custom_call_target="tpu_custom_call" | custom-call | bytes 16777216 | tf_op jit(solution)/shard_map/base/pallas_call | solution.py:36
  165.5 2.4 %late_sums.1 = (f32[2,4,4,128,128]{4,3,2,1,0:T(8,128)S(1)}, f32[64,128,128]{2,1,0:T(8,128)S(1)}) custom-call(f32[256]{0:T(256)} %reshape.149.all_flags, f32[64,128,128]{2,1,0:T(8,128)} %all-to-all-done.2.recv, f32[8,128]{1,0:T(8,128)S(1)} %get-tuple-element.48.wait), custom_call_target="tpu_custom_call" | custom-call | bytes 6291456 | tf_op jit(solution)/shard_map/late_sums/pallas_call | solution.py:36
  167.8 3.0 %collective-permute-start.4 = (f32[2,4,4,128,128]{4,3,2,1,0:T(8,128)S(1)}, f32[2,4,4,128,128]{4,3,2,1,0:T(8,128)S(1)}, u32[]{:S(2)}, u32[]{:S(2)}) collective-permute-start(f32[2,4,4,128,128]{4,3,2,1,0:T(8,128)S(1)} %get-tuple-element.52), channel_id=1, source_target_pairs={{0,1},{1,0},{2,3},{3,2},{4,5},{5,4},{6,7},{7,6},{8,9},{9,8},{10,11... | collective-permute-start | bytes 6291464 | tf_op jit(solution)/shard_map/ppermute | solution.py:567
  170.9 3.7 %add_own.1 = (f32[2,4,256,1024]{3,2,1,0:T(8,128)}, f32[4,2,4,128,128]{4,3,2,1,0:T(8,128)S(1)}) custom-call(f32[256]{0:T(256)} %reshape.149.all_flags, f32[2,4,256,1024]{3,2,1,0:T(8,128)} %bitcast.34, f32[8,2,4,128,128]{4,3,2,1,0:T(8,128)} %bitcast.35, f32[64,128,128]{2,1,0:T(8,128)S(1)} %get-tuple-element.49.held), custom_call_target="tpu_custom_call", output_to_operand_aliasing={{0}: (1, {})} | custom-call | bytes 12582912 | tf_op jit(solution)/shard_map/add_own/pallas_call | solution.py:36
  174.7 1.4 add_late.1
  (50 shorter events, 9.0 us)
Async XLA Ops:
  2.4 4.9 %collective-permute-start = (f32[64,32,128]{2,1,0:T(8,128)S(1)}, f32[64,32,128]{2,1,0:T(8,128)S(1)}, u32[]{:S(2)}, u32[]{:S(2)}) collective-permute-start(f32[64,32,128]{2,1,0:T(8,128)S(1)} %get-tuple-element.34), channel_id=1, source_target_pairs={{0,1},{8,9},{16,17},{24,25},{32,33},{40,41},{48,49},{56,57},{64,65... | collective-permute-start | bytes 3145736 | tf_op jit(solution)/shard_map/ppermute | solution.py:589
  8.4 11.5 %copy-start.3 = (s32[4,64]{1,0:T(4,128)S(1)}, s32[4,64]{1,0:T(4,128)}, u32[]{:S(2)}) copy-start(s32[4,64]{1,0:T(4,128)} %rest_0_.1) | copy-start | bytes 3076
  8.4 52.4 %all-to-all-start = ((f32[64,96,128]{2,1,0:T(8,128)}), f32[64,96,128]{2,1,0:T(8,128)S(1)}, u32[]{:S(2)}, u32[]{:S(2)}) async-start(f32[64,96,128]{2,1,0:T(8,128)} %get-tuple-element.35), calls=%async_computation | async-start | bytes 6291456 | tf_op jit(solution)/shard_map/all_to_all | solution.py:570
  62.3 45.7 %all-to-all-start.1 = ((f32[64,96,128]{2,1,0:T(8,128)}), f32[64,96,128]{2,1,0:T(8,128)}, u32[]{:S(2)}, u32[]{:S(2)}) async-start(f32[64,96,128]{2,1,0:T(8,128)} %get-tuple-element.37), calls=%async_computation.1 | async-start | bytes 6291456 | tf_op jit(solution)/shard_map/all_to_all | solution.py:570
  108.0 57.5 %all-to-all-start.2 = ((f32[64,128,128]{2,1,0:T(8,128)}), f32[64,128,128]{2,1,0:T(8,128)}, u32[]{:S(2)}, u32[]{:S(2)}) async-start(f32[64,128,128]{2,1,0:T(8,128)} %pack.5), calls=%async_computation.2 | async-start | bytes 8388608 | tf_op jit(solution)/shard_map/all_to_all | solution.py:570
  116.7 6.8 %collective-permute-start.1 = (f32[64,40,128]{2,1,0:T(8,128)}, f32[64,40,128]{2,1,0:T(8,128)S(1)}, u32[]{:S(2)}, u32[]{:S(2)}) collective-permute-start(f32[64,40,128]{2,1,0:T(8,128)} %slice.29), channel_id=1, source_target_pairs={{0,1},{1,0},{2,3},{3,2},{4,5},{5,4},{6,7},{7,6},{8,9},{9,8},{10,11... | collective-permute-start | bytes 3932168 | tf_op jit(solution)/shard_map/ppermute | solution.py:567
  118.9 37.5 %collective-permute-start.2 = (f32[2,4,4,72,128]{4,3,2,1,0:T(8,128)}, f32[2,4,4,72,128]{4,3,2,1,0:T(8,128)}, u32[]{:S(2)}, u32[]{:S(2)}) collective-permute-start(f32[2,4,4,72,128]{4,3,2,1,0:T(8,128)} %get-tuple-element.42), channel_id=1, source_target_pairs={{0,1},{1,0},{2,3},{3,2},{4,5},{5,4},{6,7},{7,6},{8,9},{9,8},{10,11... | collective-permute-start | bytes 3538952 | tf_op jit(solution)/shard_map/ppermute | solution.py:567
  123.5 33.0 %copy-start = (f32[2,4,4,72,128]{4,3,2,1,0:T(8,128)S(1)}, f32[2,4,4,72,128]{4,3,2,1,0:T(8,128)}, u32[]{:S(2)}) copy-start(f32[2,4,4,72,128]{4,3,2,1,0:T(8,128)} %get-tuple-element.41.own0) | copy-start | bytes 3538948
  127.9 0.6 copy-start.2
  128.5 28.0 %copy-start.1 = (f32[2,4,4,64,128]{4,3,2,1,0:T(8,128)S(1)}, f32[2,4,4,64,128]{4,3,2,1,0:T(8,128)}, u32[]{:S(2)}) copy-start(f32[2,4,4,64,128]{4,3,2,1,0:T(8,128)} %get-tuple-element.43.own1) | copy-start | bytes 3145732
  128.5 28.0 %collective-permute-start.3 = (f32[2,4,4,64,128]{4,3,2,1,0:T(8,128)}, f32[2,4,4,64,128]{4,3,2,1,0:T(8,128)S(1)}, u32[]{:S(2)}, u32[]{:S(2)}) collective-permute-start(f32[2,4,4,64,128]{4,3,2,1,0:T(8,128)} %get-tuple-element.44), channel_id=1, source_target_pairs={{0,1},{1,0},{2,3},{3,2},{4,5},{5,4},{6,7},{7,6},{8,9},{9,8},{10,11... | collective-permute-start | bytes 3145736 | tf_op jit(solution)/shard_map/ppermute | solution.py:567
  167.8 6.8 %collective-permute-start.4 = (f32[2,4,4,128,128]{4,3,2,1,0:T(8,128)S(1)}, f32[2,4,4,128,128]{4,3,2,1,0:T(8,128)S(1)}, u32[]{:S(2)}, u32[]{:S(2)}) collective-permute-start(f32[2,4,4,128,128]{4,3,2,1,0:T(8,128)S(1)} %get-tuple-element.52), channel_id=1, source_target_pairs={{0,1},{1,0},{2,3},{3,2},{4,5},{5,4},{6,7},{7,6},{8,9},{9,8},{10,11... | collective-permute-start | bytes 6291464 | tf_op jit(solution)/shard_map/ppermute | solution.py:567
